TPU v7x, 32 devices: a whole 2x2x4 slice. The times are simulated.
32 devices in a mesh: series: 1, tm: 16 (over z, y, x), tile: 2 (over core).
Axes of the slice: x: 2, y: 2, z: 4, core: 2. Of those that a mesh axis runs over, the one named last changes fastest.
Arguments:
- frames: bfloat16 [128, 2304, 128], P('tm', ('series', 'tile')), may hold values from 0.001 to 6000, as said below
- block_cycle: int32 [2304], P('series'), may hold values from 0 to 31, as said below
- block_valid: int32 [2304], P('series'), may hold values from 1 to 128, as said below
- cycle_owner: int32 [32], replicated, may hold values from 0 to 31, each once
Outputs:
- two_time: float32 [4096, 128], P(('series', 'tm', 'tile'))
Inputs may be any that keep to these rules, and one draw needn't show every extreme that they name: `block_cycle`: each cycle is named by at least one block; in each aligned run of 1152 blocks no cycle is named by more than 71 blocks, and one cycle is named by exactly 71. The first block_valid[b] pixels of block b are valid. `frames`: positive intensities.
All inputs are finite; a program needn't handle non-finite values.
Results may differ from a plain program's by a relative error of at most 0.0003.
Values may be sent and summed in bfloat16 or wider, within the bound.
No kernel may reach another device: no remote copies, remote signals or barrier semaphores. Data moves between devices by JAX's collectives and lax.ppermute only.
A program may use at most 64 MiB of HBM per device.

v0:
```python
import functools

import jax
import jax.numpy as jnp
from jax import lax
from jax.experimental import pallas as pl
from jax.experimental.pallas import tpu as pltpu
from jax.sharding import PartitionSpec as P

LANE = 128
UNROLL = 32
GROUPS = 2
STEP = 128
VMEM_LIMIT = 24 * 1024 * 1024
LADDER = (24, 32, 36, 40, 42, 44, 46, 50, 64, 96, 144)
NT = (((1,), (1,)), ((), ()))


def apart_of(turn, count):
    side = count // 2
    return (side if turn % 2 == 0 else 0) + side - 1 - turn // 2


def plan_kernel(
    owner_in, cycle_in, valid_in, word_ref, scalar_ref, owner_ref, cycle_ref, valid_ref, arrived
):
    tm_index, tile_index = lax.axis_index("tm"), lax.axis_index("tile")
    fetches = [
        pltpu.make_async_copy(source, target, arrived.at[i])
        for i, (source, target) in enumerate(
            ((owner_in, owner_ref), (cycle_in, cycle_ref), (valid_in, valid_ref))
        )
    ]
    for fetch in fetches:
        fetch.start()
    for fetch in fetches:
        fetch.wait()
    chunks = cycle_ref.shape[0] // LANE
    slots = owner_ref.shape[0]
    half = cycle_ref.shape[0] // 2
    list_rows = word_ref.shape[0]
    slot = lax.broadcasted_iota(jnp.int32, (slots, LANE), 0)
    mine = (slot % 2 == tile_index).astype(jnp.float32)
    owner = jnp.zeros((slots, LANE), jnp.int32)
    for s in range(slots):
        owner = jnp.where(slot == s, owner_ref[s], owner)

    member, weighted = [], []
    for k in range(chunks):
        cut = slice(k * LANE, (k + 1) * LANE)
        hit = (cycle_ref[cut].reshape(1, LANE) == owner).astype(jnp.float32)
        member.append(hit)
        weighted.append(hit * valid_ref[cut].reshape(1, LANE).astype(jnp.float32))
    stacked = jnp.concatenate(member + weighted, axis=0).astype(jnp.bfloat16)
    before = lax.broadcasted_iota(jnp.int32, (LANE, 2 * LANE), 0)
    column = lax.broadcasted_iota(jnp.int32, (LANE, 2 * LANE), 1)
    prefix = ((before < column) | (column >= LANE)).astype(jnp.float32).astype(jnp.bfloat16)
    sums = jnp.dot(stacked, prefix, preferred_element_type=jnp.float32)

    count = jnp.zeros((slots, LANE), jnp.float32)
    pixels = jnp.zeros((slots, LANE), jnp.float32)
    rank, start = [], []
    for k in range(chunks):
        low = slice(k * slots, (k + 1) * slots)
        high = slice((chunks + k) * slots, (chunks + k + 1) * slots)
        rank.append(count + sums[low, :LANE])
        start.append(pixels + sums[high, :LANE])
        count = count + sums[low, LANE:]
        pixels = pixels + sums[high, LANE:]

    rows = (jnp.max(pixels).astype(jnp.int32) + LANE - 1) // LANE
    rung = jnp.int32(0)
    size = jnp.int32(LADDER[0])
    for smaller, larger in zip(LADDER[:-1], LADDER[1:]):
        rung = rung + (rows > smaller).astype(jnp.int32)
        size = jnp.where(rows > smaller, larger, size)

    def turn_of(index):
        apart = (index // 2) ^ tm_index
        side = slots // 4
        return 2 * (side - 1 - apart % side) + (apart < side).astype(jnp.int32)

    row = turn_of(lax.broadcasted_iota(jnp.int32, (slots, slots), 0))
    index = lax.broadcasted_iota(jnp.int32, (slots, slots), 1)
    earlier = ((turn_of(index) < row) & (index % 2 == tile_index)).astype(jnp.float32)
    turn = turn_of(slot)
    base = jnp.dot(
        earlier, count, precision=lax.Precision.HIGHEST, preferred_element_type=jnp.float32
    )
    begin = (turn * size * LANE).astype(jnp.float32)

    list_row = lax.broadcasted_iota(jnp.int32, (list_rows, LANE), 0)
    list_col = lax.broadcasted_iota(jnp.int32, (LANE, LANE), 0)
    lane = lax.broadcasted_iota(jnp.int32, (1, LANE), 1)
    lists = jnp.zeros((4 * list_rows, LANE), jnp.float32)
    for k in range(chunks):
        own = member[k] * mine
        place = jnp.sum(own * (rank[k] + base), axis=0, keepdims=True).astype(jnp.int32)
        at = jnp.sum(own * (start[k] + begin), axis=0, keepdims=True).astype(jnp.int32)
        used = jnp.sum(own, axis=0, keepdims=True) > 0
        block = k * LANE + lane
        far = (block >= half) != (tile_index == 1)
        block = jnp.where(block >= half, block - half, block) + jnp.where(far, half, 0)
        pixel_count = jnp.sum(own * weighted[k], axis=0, keepdims=True).astype(jnp.int32)
        wraps = at % LANE + pixel_count >= LANE
        word = at * 4096 + block + jnp.where(wraps, jnp.int32(-(2**31)), 0)
        at_row = list_row == jnp.where(used, place // LANE, -1)
        at_col = (list_col == place % LANE).astype(jnp.float32).astype(jnp.bfloat16)
        spread = jnp.concatenate(
            [
                jnp.where(at_row, ((word >> (8 * part)) & 255).astype(jnp.float32), 0.0)
                for part in range(4)
            ],
            axis=0,
        ).astype(jnp.bfloat16)
        lists = lists + lax.dot_general(spread, at_col, NT, preferred_element_type=jnp.float32)
    lists = lists.astype(jnp.int32)
    words = jnp.zeros((list_rows, LANE), jnp.int32)
    for part in range(4):
        words = words + (lists[part * list_rows : (part + 1) * list_rows] << (8 * part))
    index = LANE * lax.broadcasted_iota(jnp.int32, (list_rows, LANE), 0)
    index = index + lax.broadcasted_iota(jnp.int32, (list_rows, LANE), 1)
    total = jnp.sum(count[:, :1] * mine[:, :1]).astype(jnp.int32)
    word_ref[...] = jnp.where(index < total, words, (slots // 2 * size) << 19)

    own_slot = 2 * tm_index + tile_index
    scalar_ref[0] = rung
    scalar_ref[1] = tm_index
    scalar_ref[2] = jnp.sum(jnp.where(slot == own_slot, pixels, 0.0)[:, :1]).astype(jnp.int32)
    for group in range(GROUPS + 1):
        ahead = jnp.where(turn * GROUPS < group * (slots // 2), count * mine, 0.0)
        scalar_ref[3 + group] = jnp.sum(ahead[:, :1]).astype(jnp.int32)


def widen_kernel(part, in_ref, *rest):
    out_ref = rest[-1]
    half = in_ref.shape[1]

    def widen(i, _):
        begin = pl.multiple_of(i * STEP, STEP)
        rows = in_ref[:, pl.ds(begin, STEP), :].astype(jnp.float32)
        out_ref[pl.ds(part * half + begin, STEP)] = jnp.transpose(rows, (1, 0, 2))
        return 0

    lax.fori_loop(0, half // STEP, widen, 0)


def pack_kernel(group, word_ref, scalar_ref, pool_ref, *rest):
    out_refs, stage = rest[:-1], rest[-1]
    depth = out_refs[0].shape[0]
    frames = pool_ref.shape[1]
    lane = lax.broadcasted_iota(jnp.int32, (frames, LANE), 1)
    begin, end = scalar_ref[3 + group], scalar_ref[4 + group]

    def place(i, held):
        at = begin + i * UNROLL
        turned = []
        for j in range(UNROLL):
            word = word_ref[at + j]
            turned.append(pltpu.roll(pool_ref[word & 4095], (word >> 12) & (LANE - 1), 1))
        for j in range(UNROLL):
            word = word_ref[at + j]
            shift = (word >> 12) & (LANE - 1)
            row = pl.multiple_of((word >> 16) & 0x7FF8, frames)
            stage[pl.ds(row, frames), :] = jnp.where(lane >= shift, turned[j], held)
            stage[pl.ds(row + frames, frames), :] = turned[j]
            held = jnp.where(lane >= jnp.where(word < 0, 0, shift), turned[j], held)
        return held

    held = jnp.zeros((frames, LANE), jnp.float32)
    lax.fori_loop(0, (end - begin + UNROLL - 1) // UNROLL, place, held)

    step = depth if depth <= 512 else LANE
    for d, out_ref in enumerate(out_refs):
        base = (group * len(out_refs) + d) * depth

        def narrow(i, _, out_ref=out_ref, base=base):
            row = pl.multiple_of(i * step, step)
            out_ref[pl.ds(row, step), :] = stage[pl.ds(base + row, step), :].astype(jnp.bfloat16)
            return 0

        if step == depth:
            narrow(0, 0)
        else:
            lax.fori_loop(0, depth // step, narrow, 0)


def gram_kernel(scalar_ref, *refs):
    x_refs, (out_ref, turn) = refs[:-2], refs[-2:]
    sources = len(x_refs)
    frames = out_ref.shape[0]
    local = frames // sources
    pixels = scalar_ref[2]
    tm_index = scalar_ref[1]
    lane = lax.broadcasted_iota(jnp.int32, (1, LANE), 1)

    last = x_refs[0].shape[0] // (2 * local) - 1

    def pair(j, carry):
        gram, total = carry
        rows = pl.ds(pl.multiple_of(jnp.minimum(j, last) * 2 * local, 2 * local), 2 * local)
        both = [ref[rows, :].astype(jnp.float32) for ref in x_refs]
        exact, high, low = [], [], []
        for i in range(2):
            used = lane + (2 * j + i) * LANE < pixels
            x = jnp.concatenate([part[i * local : (i + 1) * local] for part in both], axis=0)
            x = jnp.where(used, x, 0.0)
            mean = jnp.where(used, jnp.sum(x, axis=0, keepdims=True) / frames, 1.0)
            scale = 1.0 / mean
            total = total + x * scale
            y = x * (scale * scale)
            top = y.astype(jnp.bfloat16)
            exact.append(x.astype(jnp.bfloat16))
            high.append(top)
            low.append((y - top.astype(jnp.float32)).astype(jnp.bfloat16))
        left = jnp.concatenate(exact, axis=1)
        right = jnp.concatenate(
            [jnp.concatenate(high, axis=1), jnp.concatenate(low, axis=1)], axis=0
        )
        gram = gram + lax.dot_general(left, right, NT, preferred_element_type=jnp.float32)
        return gram, total

    def two_pairs(j, carry):
        return pair(2 * j + 1, pair(2 * j, carry))

    def in_order(value):
        for j in range(sources):
            at = pl.multiple_of((tm_index ^ apart_of(j, sources)) * local, local)
            turn[pl.ds(at, local), :] = value[j * local : (j + 1) * local]
        return turn[...]

    carry = (jnp.zeros((frames, 2 * frames), jnp.float32), jnp.zeros((frames, LANE), jnp.float32))
    pairs = (pixels + 2 * LANE - 1) // (2 * LANE)
    gram, total = lax.fori_loop(0, (pairs + 1) // 2, two_pairs, carry)
    gram = in_order(gram[:, :frames] + gram[:, frames:])
    gram = in_order(gram.T)
    total = in_order(total)
    first = jnp.sum(total, axis=1, keepdims=True)
    second = jnp.sum(total.T, axis=0, keepdims=True)
    out_ref[...] = pixels.astype(jnp.float32) * gram / (first * second)


def on_device_routed(frames, block_cycle, block_valid, cycle_owner):
    tm_count = lax.axis_size("tm")
    local_frames, half, _ = frames.shape
    frame_count = tm_count * local_frames
    list_rows = -(-(block_cycle.shape[0] + UNROLL) // (8 * LANE)) * 8
    vmem = pl.BlockSpec(memory_space=pltpu.VMEM)
    smem = pl.BlockSpec(memory_space=pltpu.SMEM)
    params = pltpu.CompilerParams(vmem_limit_bytes=VMEM_LIMIT)

    def widen(*given):
        return pl.pallas_call(
            functools.partial(widen_kernel, len(given) - 1),
            out_shape=jax.ShapeDtypeStruct((2 * half, local_frames, LANE), jnp.float32),
            in_specs=[vmem] * len(given),
            out_specs=vmem,
            input_output_aliases={1: 0} if len(given) > 1 else {},
            compiler_params=params,
            name="widen",
        )(*given)

    far = lax.ppermute(frames, "tile", [(0, 1), (1, 0)])
    words, scalars = pl.pallas_call(
        plan_kernel,
        out_shape=(
            jax.ShapeDtypeStruct((list_rows, LANE), jnp.int32),
            jax.ShapeDtypeStruct((4 + GROUPS,), jnp.int32),
        ),
        in_specs=[pl.BlockSpec(memory_space=pltpu.HBM)] * 3,
        out_specs=(vmem, smem),
        scratch_shapes=[
            pltpu.SMEM(cycle_owner.shape, jnp.int32),
            pltpu.VMEM(block_cycle.shape, jnp.int32),
            pltpu.VMEM(block_valid.shape, jnp.int32),
            pltpu.SemaphoreType.DMA((3,)),
        ],
        compiler_params=params,
        name="plan",
    )(cycle_owner, block_cycle, block_valid)
    pool = widen(far, widen(frames))
    members = tm_count // GROUPS

    def branch(size):
        depth = size * local_frames

        def run(words, scalars, pool):
            got = []
            for group in range(GROUPS):
                send = pl.pallas_call(
                    functools.partial(pack_kernel, group),
                    out_shape=(jax.ShapeDtypeStruct((depth, LANE), jnp.bfloat16),) * members,
                    in_specs=[smem, smem, vmem],
                    out_specs=(vmem,) * members,
                    scratch_shapes=[
                        pltpu.VMEM(((tm_count * size + 2) * local_frames, LANE), jnp.float32)
                    ],
                    compiler_params=params,
                    cost_estimate=pl.CostEstimate(
                        flops=2_000_000, bytes_accessed=16_000_000, transcendentals=0
                    ),
                    name="pack",
                )(words, scalars, pool)
                for j in range(members):
                    apart = apart_of(group * members + j, tm_count)
                    pairs = [(i, i ^ apart) for i in range(tm_count)]
                    got.append(lax.ppermute(send[j], "tm", pairs) if apart else send[j])
            return pl.pallas_call(
                gram_kernel,
                out_shape=jax.ShapeDtypeStruct((frame_count, frame_count), jnp.float32),
                in_specs=[smem] + [vmem] * tm_count,
                out_specs=vmem,
                scratch_shapes=[pltpu.VMEM((frame_count, LANE), jnp.float32)],
                compiler_params=params,
                name="gram",
            )(scalars, *got)

        return run

    return lax.switch(
        scalars[0],
        [branch(size) for size in LADDER],
        words.reshape(-1),
        scalars,
        pool,
    )


def normalize(pixel_intensity, valid_count, lanes):
    lane_index = jnp.arange(lanes, dtype=jnp.int32)
    valid_mask = lane_index[None, :] < valid_count[:, None]
    pixel_mean = jnp.sum(pixel_intensity, axis=0) / pixel_intensity.shape[0]
    guarded_average = jnp.where(valid_mask, pixel_mean, jnp.float32(1.0))
    return jnp.where(valid_mask[None], pixel_intensity / guarded_average[None], jnp.float32(0.0))


def on_device_summed(frames, block_cycle, block_valid, cycle_owner):
    tm_count = lax.axis_size("tm")
    tile_count = lax.axis_size("tile")
    tm_index = lax.axis_index("tm")
    tile_index = lax.axis_index("tile")
    local_frames = frames.shape[0]
    half = frames.shape[1]
    lanes = frames.shape[2]
    cycle_count = cycle_owner.shape[0]
    frame_count = local_frames * tm_count
    cycle_range = jnp.arange(cycle_count, dtype=jnp.int32)
    member_all = (block_cycle[None, :] == cycle_owner[:, None]).astype(jnp.float32)
    pixel_total = jnp.dot(
        member_all, block_valid.astype(jnp.float32), precision=lax.Precision.HIGHEST
    )
    row_count = cycle_count * frame_count // (tm_count * tile_count)
    block_local = half // tm_count
    reshaped = frames.reshape(local_frames, tm_count, block_local, lanes)
    arrived = lax.all_to_all(reshaped, "tm", split_axis=1, concat_axis=0, tiled=True)
    pixel_intensity = arrived.reshape(frame_count, block_local, lanes).astype(jnp.float32)
    offset = (tile_index * tm_count + tm_index) * block_local
    cycle_ids = lax.dynamic_slice_in_dim(block_cycle, offset, block_local, 0)
    valid_count = lax.dynamic_slice_in_dim(block_valid, offset, block_local, 0)
    members = (cycle_ids[None, :] == cycle_owner[:, None]).astype(jnp.float32)
    normalized_frames = normalize(pixel_intensity, valid_count, lanes)
    gram_matrices = jnp.einsum(
        "rnk,jnk->nrj", normalized_frames, normalized_frames, precision=lax.Precision.HIGHEST
    )
    partial_value = jnp.dot(
        members,
        gram_matrices.reshape(block_local, frame_count * frame_count),
        precision=lax.Precision.HIGHEST,
    )
    partial_value = partial_value.reshape(cycle_count * frame_count, frame_count)
    frame_sums = jnp.dot(
        members, jnp.sum(normalized_frames, axis=2).T, precision=lax.Precision.HIGHEST
    )
    owned = lax.psum_scatter(partial_value, ("tm", "tile"), scatter_dimension=0, tiled=True)
    frame_total = lax.psum(frame_sums, ("tm", "tile"))
    row_start = (tm_index * tile_count + tile_index) * row_count
    row_global = row_start + jnp.arange(row_count, dtype=jnp.int32)
    slot_index = row_global // frame_count
    frame_time_index = row_global % frame_count
    select = (slot_index[:, None] == cycle_range[None, :]).astype(jnp.float32)
    row_sums = jnp.dot(select, frame_total, precision=lax.Precision.HIGHEST)
    row_pixels = jnp.dot(select, pixel_total, precision=lax.Precision.HIGHEST)
    time_pick = (
        jnp.arange(frame_count, dtype=jnp.int32)[None, :] == frame_time_index[:, None]
    ).astype(jnp.float32)
    first_sums = jnp.sum(row_sums * time_pick, axis=1)
    return row_pixels[:, None] * owned / (first_sums[:, None] * row_sums)


def solution(mesh):
    in_specs = (P("tm", ("series", "tile"), None), P("series"), P("series"), P())
    out_specs = P(("series", "tm", "tile"), None)

    def on_device(frames, block_cycle, block_valid, cycle_owner):
        routed = (
            mesh.shape["tile"] == 2
            and mesh.shape["tm"] * 2 == cycle_owner.shape[0]
            and frames.shape[0] == 8
            and mesh.shape["tm"] * 8 == LANE
            and block_cycle.shape[0] <= 4096
        )
        body = on_device_routed if routed else on_device_summed
        return body(frames, block_cycle, block_valid, cycle_owner)

    return jax.shard_map(
        on_device, mesh=mesh, in_specs=in_specs, out_specs=out_specs, check_vma=False
    )
```

profile of v0, /device:TPU:0, one launch (start us, length us, event | category | flops | bytes accessed | tf_op | source)
XLA Modules:
  0.0 54.9 jit_solution(10500339407936505240)
XLA Ops:
  0.0 0.5 collective-permute-start.165
  0.5 1.7 %copy-done = bf16[8,1152,128]{2,1,0:T(8,128)(2,1)S(1)} copy-done((bf16[8,1152,128]{2,1,0:T(8,128)(2,1)S(1)}, bf16[8,1152,128]{2,1,0:T(8,128)(2,1)}, u32[]{:S(2)}) %copy-start) | copy-done | bytes 2359320
  2.1 1.0 %widen.2.rest_0_ = f32[2304,8,128]{2,1,0:T(8,128)S(1)} custom-call(bf16[8,1152,128]{2,1,0:T(8,128)(2,1)S(1)} %copy-done), custom_call_target="tpu_custom_call" | custom-call | tf_op jit(solution)/shard_map/widen/pallas_call | solution.py:253
  3.1 1.8 %plan.1 = (s32[24,128]{1,0:T(8,128)S(1)}, s32[6]{0:T(128)S(1)}) custom-call(s32[32]{0:T(128)S(1)} %copy-done.3, s32[2304]{0:T(1024)S(1)} %copy-done.1, s32[2304]{0:T(1024)S(1)} %copy-done.2), custom_call_target="tpu_custom_call" | custom-call | tf_op jit(solution)/shard_map/plan/pallas_call | solution.py:264
  5.0 1.0 %widen.3 = f32[2304,8,128]{2,1,0:T(8,128)S(1)} custom-call(bf16[8,1152,128]{2,1,0:T(8,128)(2,1)S(1)} %collective-permute-done.165.in_ref, f32[2304,8,128]{2,1,0:T(8,128)S(1)} %widen.2.rest_0_), custom_call_target="tpu_custom_call", output_to_operand_aliasing={{}: (1, {})} | custom-call | tf_op jit(solution)/shard_map/widen/pallas_call | solution.py:253
  6.0 48.2 %conditional.1 = (f32[128,128]{1,0:T(8,128)S(1)}) conditional(s32[]{:T(128)} %bitcast.11, (s32[24,128]{1,0:T(8,128)S(1)}, s32[6]{0:T(128)S(1)}, f32[2304,8,128]{2,1,0:T(8,128)S(1)}) %tuple.38, (s32[24,128]{1,0:T(8,128)S(1)}, s32[6]{0:T(128)S(1)}, f32[2304,8,128]{2,1,0:T(8,128)S(1)}) %tuple.38, ...), branch_computations={%region_0.0_spmd, %region_1.0_spmd, %region_2.0_spmd, %region_3.0_... | conditional | flops 4000000 | bytes 49695328 | solution.py:320
  6.1 3.7 %pack.30 = (bf16[336,128]{1,0:T(8,128)(2,1)S(1)}, bf16[336,128]{1,0:T(8,128)(2,1)S(1)}, bf16[336,128]{1,0:T(8,128)(2,1)S(1)}, bf16[336,128]{1,0:T(8,128)(2,1)S(1...) custom-call(s32[3072]{0:T(1024)S(1)} %bitcast.21, ...), custom_call_target="tpu_custom_call" | custom-call | flops 2000000 | bytes 16000000 | tf_op jit(solution)/shard_map/cond/branch_4_fun/pack/pallas_call | solution.py:290
  9.8 6.7 %collective-permute-start.60 = (bf16[336,128]{1,0:T(8,128)(2,1)S(1)}, bf16[336,128]{1,0:T(8,128)(2,1)S(1)}, u32[]{:S(2)}, u32[]{:S(2)}) collective-permute-start(bf16[336,128]{1,0:T(8,128)(2,1)S(1)} %get-tuple-element.162), channel_id=1, source_target_pairs={{0,30},{2,28},{4,26},{6,24},{8,22},{10,20},{12,18},{14,16},{16,14}... | collective-permute-start | bytes 258056 | tf_op jit(solution)/shard_map/cond/branch_4_fun/ppermute | solution.py:307
  16.5 0.0 collective-permute-start.61
  16.5 1.8 %collective-permute-start.62 = (bf16[336,128]{1,0:T(8,128)(2,1)S(1)}, bf16[336,128]{1,0:T(8,128)(2,1)S(1)}, u32[]{:S(2)}, u32[]{:S(2)}) collective-permute-start(bf16[336,128]{1,0:T(8,128)(2,1)S(1)} %get-tuple-element.164), channel_id=1, source_target_pairs={{0,28},{2,30},{4,24},{6,26},{8,20},{10,22},{12,16},{14,18},{16,12}... | collective-permute-start | bytes 258056 | tf_op jit(solution)/shard_map/cond/branch_4_fun/ppermute | solution.py:307
  18.3 1.1 %collective-permute-start.63 = (bf16[336,128]{1,0:T(8,128)(2,1)S(1)}, bf16[336,128]{1,0:T(8,128)(2,1)S(1)}, u32[]{:S(2)}, u32[]{:S(2)}) collective-permute-start(bf16[336,128]{1,0:T(8,128)(2,1)S(1)} %get-tuple-element.165), channel_id=1, source_target_pairs={{0,12},{2,14},{4,8},{6,10},{8,4},{10,6},{12,0},{14,2},{16,28},{18,... | collective-permute-start | bytes 258056 | tf_op jit(solution)/shard_map/cond/branch_4_fun/ppermute | solution.py:307
  19.4 3.8 %collective-permute-start.64 = (bf16[336,128]{1,0:T(8,128)(2,1)S(1)}, bf16[336,128]{1,0:T(8,128)(2,1)S(1)}, u32[]{:S(2)}, u32[]{:S(2)}) collective-permute-start(bf16[336,128]{1,0:T(8,128)(2,1)S(1)} %get-tuple-element.166), channel_id=1, source_target_pairs={{0,26},{2,24},{4,30},{6,28},{8,18},{10,16},{12,22},{14,20},{16,10}... | collective-permute-start | bytes 258056 | tf_op jit(solution)/shard_map/cond/branch_4_fun/ppermute | solution.py:307
  23.2 3.7 %pack.31 = (bf16[336,128]{1,0:T(8,128)(2,1)S(1)}, bf16[336,128]{1,0:T(8,128)(2,1)S(1)}, bf16[336,128]{1,0:T(8,128)(2,1)S(1)}, bf16[336,128]{1,0:T(8,128)(2,1)S(1...) custom-call(s32[3072]{0:T(1024)S(1)} %bitcast.22, ...), custom_call_target="tpu_custom_call" | custom-call | flops 2000000 | bytes 16000000 | tf_op jit(solution)/shard_map/cond/branch_4_fun/pack/pallas_call | solution.py:290
  26.9 0.0 collective-permute-done.60.refs_0_
  27.0 0.1 collective-permute-start.65
  27.1 0.0 collective-permute-done.61.refs_1_
  27.1 1.0 %collective-permute-start.66 = (bf16[336,128]{1,0:T(8,128)(2,1)S(1)}, bf16[336,128]{1,0:T(8,128)(2,1)S(1)}, u32[]{:S(2)}, u32[]{:S(2)}) collective-permute-start(bf16[336,128]{1,0:T(8,128)(2,1)S(1)} %get-tuple-element.168), channel_id=1, source_target_pairs={{0,24},{2,26},{4,28},{6,30},{8,16},{10,18},{12,20},{14,22},{16,8},... | collective-permute-start | bytes 258056 | tf_op jit(solution)/shard_map/cond/branch_4_fun/ppermute | solution.py:307
  28.1 1.0 %collective-permute-start.67 = (bf16[336,128]{1,0:T(8,128)(2,1)S(1)}, bf16[336,128]{1,0:T(8,128)(2,1)S(1)}, u32[]{:S(2)}, u32[]{:S(2)}) collective-permute-start(bf16[336,128]{1,0:T(8,128)(2,1)S(1)} %get-tuple-element.169), channel_id=1, source_target_pairs={{0,8},{2,10},{4,12},{6,14},{8,0},{10,2},{12,4},{14,6},{16,24},{18,... | collective-permute-start | bytes 258056 | tf_op jit(solution)/shard_map/cond/branch_4_fun/ppermute | solution.py:307
  29.1 0.0 collective-permute-done.63.refs_3_
  29.1 3.7 %collective-permute-start.68 = (bf16[336,128]{1,0:T(8,128)(2,1)S(1)}, bf16[336,128]{1,0:T(8,128)(2,1)S(1)}, u32[]{:S(2)}, u32[]{:S(2)}) collective-permute-start(bf16[336,128]{1,0:T(8,128)(2,1)S(1)} %get-tuple-element.170), channel_id=1, source_target_pairs={{0,22},{2,20},{4,18},{6,16},{8,30},{10,28},{12,26},{14,24},{16,6},... | collective-permute-start | bytes 258056 | tf_op jit(solution)/shard_map/cond/branch_4_fun/ppermute | solution.py:307
  32.8 0.0 collective-permute-done.64.refs_4_
  32.8 1.0 %collective-permute-start.69 = (bf16[336,128]{1,0:T(8,128)(2,1)S(1)}, bf16[336,128]{1,0:T(8,128)(2,1)S(1)}, u32[]{:S(2)}, u32[]{:S(2)}) collective-permute-start(bf16[336,128]{1,0:T(8,128)(2,1)S(1)} %get-tuple-element.171), channel_id=1, source_target_pairs={{0,6},{2,4},{4,2},{6,0},{8,14},{10,12},{12,10},{14,8},{16,22},{18,... | collective-permute-start | bytes 258056 | tf_op jit(solution)/shard_map/cond/branch_4_fun/ppermute | solution.py:307
  33.9 1.5 %collective-permute-start.70 = (bf16[336,128]{1,0:T(8,128)(2,1)S(1)}, bf16[336,128]{1,0:T(8,128)(2,1)S(1)}, u32[]{:S(2)}, u32[]{:S(2)}) collective-permute-start(bf16[336,128]{1,0:T(8,128)(2,1)S(1)} %get-tuple-element.172), channel_id=1, source_target_pairs={{0,20},{2,22},{4,16},{6,18},{8,28},{10,30},{12,24},{14,26},{16,4},... | collective-permute-start | bytes 258056 | tf_op jit(solution)/shard_map/cond/branch_4_fun/ppermute | solution.py:307
  35.4 0.8 %collective-permute-start.71 = (bf16[336,128]{1,0:T(8,128)(2,1)S(1)}, bf16[336,128]{1,0:T(8,128)(2,1)S(1)}, u32[]{:S(2)}, u32[]{:S(2)}) collective-permute-start(bf16[336,128]{1,0:T(8,128)(2,1)S(1)} %get-tuple-element.173), channel_id=1, source_target_pairs={{0,4},{2,6},{4,0},{6,2},{8,12},{10,14},{12,8},{14,10},{16,20},{18,... | collective-permute-start | bytes 258056 | tf_op jit(solution)/shard_map/cond/branch_4_fun/ppermute | solution.py:307
  36.2 4.2 %collective-permute-start.72 = (bf16[336,128]{1,0:T(8,128)(2,1)S(1)}, bf16[336,128]{1,0:T(8,128)(2,1)S(1)}, u32[]{:S(2)}, u32[]{:S(2)}) collective-permute-start(bf16[336,128]{1,0:T(8,128)(2,1)S(1)} %get-tuple-element.174), channel_id=1, source_target_pairs={{0,18},{2,16},{4,22},{6,20},{8,26},{10,24},{12,30},{14,28},{16,2},... | collective-permute-start | bytes 258056 | tf_op jit(solution)/shard_map/cond/branch_4_fun/ppermute | solution.py:307
  40.4 4.6 %collective-permute-done.68.refs_8_ = bf16[336,128]{1,0:T(8,128)(2,1)S(1)} collective-permute-done((bf16[336,128]{1,0:T(8,128)(2,1)S(1)}, bf16[336,128]{1,0:T(8,128)(2,1)S(1)}, u32[]{:S(2)}, u32[]{:S(2)}) %collective-permute-start.68) | collective-permute-done | bytes 86048 | tf_op jit(solution)/shard_map/cond/branch_4_fun/ppermute | solution.py:307
  45.0 3.4 %collective-permute-done.72.refs_12_ = bf16[336,128]{1,0:T(8,128)(2,1)S(1)} collective-permute-done((bf16[336,128]{1,0:T(8,128)(2,1)S(1)}, bf16[336,128]{1,0:T(8,128)(2,1)S(1)}, u32[]{:S(2)}, u32[]{:S(2)}) %collective-permute-start.72) | collective-permute-done | bytes 86048 | tf_op jit(solution)/shard_map/cond/branch_4_fun/ppermute | solution.py:307
  48.5 1.0 %collective-permute-done.73.refs_13_ = bf16[336,128]{1,0:T(8,128)(2,1)S(1)} collective-permute-done((bf16[336,128]{1,0:T(8,128)(2,1)S(1)}, bf16[336,128]{1,0:T(8,128)(2,1)S(1)}, u32[]{:S(2)}, u32[]{:S(2)}) %collective-permute-start.73) | collective-permute-done | bytes 86048 | tf_op jit(solution)/shard_map/cond/branch_4_fun/ppermute | solution.py:307
  49.5 0.9 %collective-permute-done.74.refs_14_ = bf16[336,128]{1,0:T(8,128)(2,1)S(1)} collective-permute-done((bf16[336,128]{1,0:T(8,128)(2,1)S(1)}, bf16[336,128]{1,0:T(8,128)(2,1)S(1)}, u32[]{:S(2)}, u32[]{:S(2)}) %collective-permute-start.74) | collective-permute-done | bytes 86048 | tf_op jit(solution)/shard_map/cond/branch_4_fun/ppermute | solution.py:307
  50.4 3.6 %gram.15 = f32[128,128]{1,0:T(8,128)S(1)} custom-call(s32[6]{0:T(128)S(1)} %get-tuple-element.159.scalar_ref, bf16[336,128]{1,0:T(8,128)(2,1)S(1)} %collective-permute-done.60.refs_0_, bf16[336,128]{1,0:T(8,128)(2,1)S(1)} %collective-permute-done.61.refs_1_, bf16[336,128]{1,0:T(8,128)(2,1)S(1)} %collective-permute-done.62.refs_2_, ...), custom_call_target="tpu_custom_call" | custom-call | tf_op jit(solution)/shard_map/cond/branch_4_fun/gram/pallas_call | solution.py:308
  54.2 0.0 copy-start.4
  54.2 0.6 %copy-done.4 = f32[128,128]{1,0:T(8,128)} copy-done((f32[128,128]{1,0:T(8,128)}, f32[128,128]{1,0:T(8,128)S(1)}, u32[]{:S(2)}) %copy-start.4) | copy-done | bytes 65560
  (17 shorter events, 0.0 us)
Async XLA Ops:
  0.0 5.0 %collective-permute-start.165 = (bf16[8,1152,128]{2,1,0:T(8,128)(2,1)}, bf16[8,1152,128]{2,1,0:T(8,128)(2,1)S(1)}, u32[]{:S(2)}, u32[]{:S(2)}) collective-permute-start(bf16[8,1152,128]{2,1,0:T(8,128)(2,1)} %in_ref.1), channel_id=1, source_target_pairs={{0,1},{1,0},{2,3},{3,2},{4,5},{5,4},{6,7},{7,6},{8,9},{9,8},{10,11... | collective-permute-start | bytes 7077896 | tf_op jit(solution)/shard_map/ppermute | solution.py:263
  0.5 1.7 %copy-start = (bf16[8,1152,128]{2,1,0:T(8,128)(2,1)S(1)}, bf16[8,1152,128]{2,1,0:T(8,128)(2,1)}, u32[]{:S(2)}) copy-start(bf16[8,1152,128]{2,1,0:T(8,128)(2,1)} %in_ref.1) | copy-start | bytes 7077892
  2.1 1.0 %copy-start.1 = (s32[2304]{0:T(1024)S(1)}, s32[2304]{0:T(1024)}, u32[]{:S(2)}) copy-start(s32[2304]{0:T(1024)} %cycle_in.1) | copy-start | bytes 27652
  2.1 1.0 %copy-start.2 = (s32[2304]{0:T(1024)S(1)}, s32[2304]{0:T(1024)}, u32[]{:S(2)}) copy-start(s32[2304]{0:T(1024)} %valid_in.1) | copy-start | bytes 27652
  2.1 1.0 %copy-start.3 = (s32[32]{0:T(128)S(1)}, s32[32]{0:T(128)}, u32[]{:S(2)}) copy-start(s32[32]{0:T(128)} %owner_in.1) | copy-start | bytes 388
  9.8 17.1 %collective-permute-start.60 = (bf16[336,128]{1,0:T(8,128)(2,1)S(1)}, bf16[336,128]{1,0:T(8,128)(2,1)S(1)}, u32[]{:S(2)}, u32[]{:S(2)}) collective-permute-start(bf16[336,128]{1,0:T(8,128)(2,1)S(1)} %get-tuple-element.162), channel_id=1, source_target_pairs={{0,30},{2,28},{4,26},{6,24},{8,22},{10,20},{12,18},{14,16},{16,14}... | collective-permute-start | bytes 258056 | tf_op jit(solution)/shard_map/cond/branch_4_fun/ppermute | solution.py:307
  16.5 10.6 %collective-permute-start.61 = (bf16[336,128]{1,0:T(8,128)(2,1)S(1)}, bf16[336,128]{1,0:T(8,128)(2,1)S(1)}, u32[]{:S(2)}, u32[]{:S(2)}) collective-permute-start(bf16[336,128]{1,0:T(8,128)(2,1)S(1)} %get-tuple-element.163), channel_id=1, source_target_pairs={{0,14},{2,12},{4,10},{6,8},{8,6},{10,4},{12,2},{14,0},{16,30},{18,... | collective-permute-start | bytes 258056 | tf_op jit(solution)/shard_map/cond/branch_4_fun/ppermute | solution.py:307
  16.5 11.6 %collective-permute-start.62 = (bf16[336,128]{1,0:T(8,128)(2,1)S(1)}, bf16[336,128]{1,0:T(8,128)(2,1)S(1)}, u32[]{:S(2)}, u32[]{:S(2)}) collective-permute-start(bf16[336,128]{1,0:T(8,128)(2,1)S(1)} %get-tuple-element.164), channel_id=1, source_target_pairs={{0,28},{2,30},{4,24},{6,26},{8,20},{10,22},{12,16},{14,18},{16,12}... | collective-permute-start | bytes 258056 | tf_op jit(solution)/shard_map/cond/branch_4_fun/ppermute | solution.py:307
  18.3 10.8 %collective-permute-start.63 = (bf16[336,128]{1,0:T(8,128)(2,1)S(1)}, bf16[336,128]{1,0:T(8,128)(2,1)S(1)}, u32[]{:S(2)}, u32[]{:S(2)}) collective-permute-start(bf16[336,128]{1,0:T(8,128)(2,1)S(1)} %get-tuple-element.165), channel_id=1, source_target_pairs={{0,12},{2,14},{4,8},{6,10},{8,4},{10,6},{12,0},{14,2},{16,28},{18,... | collective-permute-start | bytes 258056 | tf_op jit(solution)/shard_map/cond/branch_4_fun/ppermute | solution.py:307
  19.4 13.4 %collective-permute-start.64 = (bf16[336,128]{1,0:T(8,128)(2,1)S(1)}, bf16[336,128]{1,0:T(8,128)(2,1)S(1)}, u32[]{:S(2)}, u32[]{:S(2)}) collective-permute-start(bf16[336,128]{1,0:T(8,128)(2,1)S(1)} %get-tuple-element.166), channel_id=1, source_target_pairs={{0,26},{2,24},{4,30},{6,28},{8,18},{10,16},{12,22},{14,20},{16,10}... | collective-permute-start | bytes 258056 | tf_op jit(solution)/shard_map/cond/branch_4_fun/ppermute | solution.py:307
  27.0 6.9 %collective-permute-start.65 = (bf16[336,128]{1,0:T(8,128)(2,1)S(1)}, bf16[336,128]{1,0:T(8,128)(2,1)S(1)}, u32[]{:S(2)}, u32[]{:S(2)}) collective-permute-start(bf16[336,128]{1,0:T(8,128)(2,1)S(1)} %get-tuple-element.167), channel_id=1, source_target_pairs={{0,10},{2,8},{4,14},{6,12},{8,2},{10,0},{12,6},{14,4},{16,26},{18,... | collective-permute-start | bytes 258056 | tf_op jit(solution)/shard_map/cond/branch_4_fun/ppermute | solution.py:307
  27.1 8.3 %collective-permute-start.66 = (bf16[336,128]{1,0:T(8,128)(2,1)S(1)}, bf16[336,128]{1,0:T(8,128)(2,1)S(1)}, u32[]{:S(2)}, u32[]{:S(2)}) collective-permute-start(bf16[336,128]{1,0:T(8,128)(2,1)S(1)} %get-tuple-element.168), channel_id=1, source_target_pairs={{0,24},{2,26},{4,28},{6,30},{8,16},{10,18},{12,20},{14,22},{16,8},... | collective-permute-start | bytes 258056 | tf_op jit(solution)/shard_map/cond/branch_4_fun/ppermute | solution.py:307
  28.1 8.1 %collective-permute-start.67 = (bf16[336,128]{1,0:T(8,128)(2,1)S(1)}, bf16[336,128]{1,0:T(8,128)(2,1)S(1)}, u32[]{:S(2)}, u32[]{:S(2)}) collective-permute-start(bf16[336,128]{1,0:T(8,128)(2,1)S(1)} %get-tuple-element.169), channel_id=1, source_target_pairs={{0,8},{2,10},{4,12},{6,14},{8,0},{10,2},{12,4},{14,6},{16,24},{18,... | collective-permute-start | bytes 258056 | tf_op jit(solution)/shard_map/cond/branch_4_fun/ppermute | solution.py:307
  29.1 15.9 %collective-permute-start.68 = (bf16[336,128]{1,0:T(8,128)(2,1)S(1)}, bf16[336,128]{1,0:T(8,128)(2,1)S(1)}, u32[]{:S(2)}, u32[]{:S(2)}) collective-permute-start(bf16[336,128]{1,0:T(8,128)(2,1)S(1)} %get-tuple-element.170), channel_id=1, source_target_pairs={{0,22},{2,20},{4,18},{6,16},{8,30},{10,28},{12,26},{14,24},{16,6},... | collective-permute-start | bytes 258056 | tf_op jit(solution)/shard_map/cond/branch_4_fun/ppermute | solution.py:307
  32.8 12.2 %collective-permute-start.69 = (bf16[336,128]{1,0:T(8,128)(2,1)S(1)}, bf16[336,128]{1,0:T(8,128)(2,1)S(1)}, u32[]{:S(2)}, u32[]{:S(2)}) collective-permute-start(bf16[336,128]{1,0:T(8,128)(2,1)S(1)} %get-tuple-element.171), channel_id=1, source_target_pairs={{0,6},{2,4},{4,2},{6,0},{8,14},{10,12},{12,10},{14,8},{16,22},{18,... | collective-permute-start | bytes 258056 | tf_op jit(solution)/shard_map/cond/branch_4_fun/ppermute | solution.py:307
  33.9 11.2 %collective-permute-start.70 = (bf16[336,128]{1,0:T(8,128)(2,1)S(1)}, bf16[336,128]{1,0:T(8,128)(2,1)S(1)}, u32[]{:S(2)}, u32[]{:S(2)}) collective-permute-start(bf16[336,128]{1,0:T(8,128)(2,1)S(1)} %get-tuple-element.172), channel_id=1, source_target_pairs={{0,20},{2,22},{4,16},{6,18},{8,28},{10,30},{12,24},{14,26},{16,4},... | collective-permute-start | bytes 258056 | tf_op jit(solution)/shard_map/cond/branch_4_fun/ppermute | solution.py:307
  35.4 9.7 %collective-permute-start.71 = (bf16[336,128]{1,0:T(8,128)(2,1)S(1)}, bf16[336,128]{1,0:T(8,128)(2,1)S(1)}, u32[]{:S(2)}, u32[]{:S(2)}) collective-permute-start(bf16[336,128]{1,0:T(8,128)(2,1)S(1)} %get-tuple-element.173), channel_id=1, source_target_pairs={{0,4},{2,6},{4,0},{6,2},{8,12},{10,14},{12,8},{14,10},{16,20},{18,... | collective-permute-start | bytes 258056 | tf_op jit(solution)/shard_map/cond/branch_4_fun/ppermute | solution.py:307
  36.2 12.3 %collective-permute-start.72 = (bf16[336,128]{1,0:T(8,128)(2,1)S(1)}, bf16[336,128]{1,0:T(8,128)(2,1)S(1)}, u32[]{:S(2)}, u32[]{:S(2)}) collective-permute-start(bf16[336,128]{1,0:T(8,128)(2,1)S(1)} %get-tuple-element.174), channel_id=1, source_target_pairs={{0,18},{2,16},{4,22},{6,20},{8,26},{10,24},{12,30},{14,28},{16,2},... | collective-permute-start | bytes 258056 | tf_op jit(solution)/shard_map/cond/branch_4_fun/ppermute | solution.py:307
  45.0 4.5 %collective-permute-start.73 = (bf16[336,128]{1,0:T(8,128)(2,1)S(1)}, bf16[336,128]{1,0:T(8,128)(2,1)S(1)}, u32[]{:S(2)}, u32[]{:S(2)}) collective-permute-start(bf16[336,128]{1,0:T(8,128)(2,1)S(1)} %get-tuple-element.175), channel_id=1, source_target_pairs={{0,2},{2,0},{4,6},{6,4},{8,10},{10,8},{12,14},{14,12},{16,18},{18,... | collective-permute-start | bytes 258056 | tf_op jit(solution)/shard_map/cond/branch_4_fun/ppermute | solution.py:307
  45.0 5.4 %collective-permute-start.74 = (bf16[336,128]{1,0:T(8,128)(2,1)S(1)}, bf16[336,128]{1,0:T(8,128)(2,1)S(1)}, u32[]{:S(2)}, u32[]{:S(2)}) collective-permute-start(bf16[336,128]{1,0:T(8,128)(2,1)S(1)} %get-tuple-element.176), channel_id=1, source_target_pairs={{0,16},{2,18},{4,20},{6,22},{8,24},{10,26},{12,28},{14,30},{16,0},... | collective-permute-start | bytes 258056 | tf_op jit(solution)/shard_map/cond/branch_4_fun/ppermute | solution.py:307
  54.2 0.6 %copy-start.4 = (f32[128,128]{1,0:T(8,128)}, f32[128,128]{1,0:T(8,128)S(1)}, u32[]{:S(2)}) copy-start(f32[128,128]{1,0:T(8,128)S(1)} %get-tuple-element.651) | copy-start | bytes 196612
where the time goes:
time: 54.5 us; the launch traced here: 54.9 us
  starting transfers between devices  27.3 us (50%)
  Pallas kernels  14.8 us (27%)
  waiting for transfers between devices  10 us (18%)
  local copies, waits for them, and re-layouts  2.3 us (4%)
    ppermute x15, starting transfers between devices, run(): got.append(lax.ppermute(send[j], 'tm', pairs) if apart else send[j])  26.8 us
    ppermute x15, waiting for transfers between devices, run(): got.append(lax.ppermute(send[j], 'tm', pairs) if apart else send[j])  10 us
    pallas_call x2, Pallas kernels, run(): pl.pallas_call(functools.partial(pack_kernel, group), out_shape=(jax.Shap...  7.46 us
    pallas_call x1, Pallas kernels, run(): pl.pallas_call(gram_kernel, out_shape=jax.ShapeDtypeStruct((frame_count,...  3.55 us
    unnamed x10, local copies, waits for them, and re-layouts  2.3 us
    pallas_call x2, Pallas kernels, widen(): pl.pallas_call(functools.partial(widen_kernel, len(given) - 1), out_shape...  1.95 us
    pallas_call x1, Pallas kernels, on_device_routed(): pl.pallas_call(plan_kernel, out_shape=(jax.ShapeDtypeStruct((list_rows, L...  1.84 us
  transfers between devices with their start and end apart: 16, of which 4 were waited for; matrix products, arithmetic and copies ran while one was open for 0% of the time, Pallas kernels for 12%

commit v1 on v0

--- a/solution.py
+++ b/solution.py
@@ -9,16 +9,25 @@
 
 LANE = 128
 UNROLL = 32
-GROUPS = 2
+FIRST = 5
 STEP = 128
 VMEM_LIMIT = 24 * 1024 * 1024
 LADDER = (24, 32, 36, 40, 42, 44, 46, 50, 64, 96, 144)
 NT = (((1,), (1,)), ((), ()))
 
 
-def apart_of(turn, count):
+def exchange_order(count):
     side = count // 2
-    return (side if turn % 2 == 0 else 0) + side - 1 - turn // 2
+    across = [count - 1 - i for i in range(side)]
+    beside = [side - 1 - i for i in range(side)]
+    order = across[:3] + beside[:1] + across[3:4]
+    for far, near in zip(across[4:], beside[1:]):
+        order += [near, far]
+    return order + [apart for apart in beside if apart not in order]
+
+
+def group_ends(count):
+    return (0, FIRST, count)
 
 
 def plan_kernel(
@@ -77,8 +86,10 @@
 
     def turn_of(index):
         apart = (index // 2) ^ tm_index
-        side = slots // 4
-        return 2 * (side - 1 - apart % side) + (apart < side).astype(jnp.int32)
+        turn = jnp.zeros_like(apart)
+        for place, each in enumerate(exchange_order(slots // 2)):
+            turn = jnp.where(apart == each, place, turn)
+        return turn
 
     row = turn_of(lax.broadcasted_iota(jnp.int32, (slots, slots), 0))
     index = lax.broadcasted_iota(jnp.int32, (slots, slots), 1)
@@ -127,8 +138,8 @@
     scalar_ref[0] = rung
     scalar_ref[1] = tm_index
     scalar_ref[2] = jnp.sum(jnp.where(slot == own_slot, pixels, 0.0)[:, :1]).astype(jnp.int32)
-    for group in range(GROUPS + 1):
-        ahead = jnp.where(turn * GROUPS < group * (slots // 2), count * mine, 0.0)
+    for group, end in enumerate(group_ends(slots // 2)):
+        ahead = jnp.where(turn < end, count * mine, 0.0)
         scalar_ref[3 + group] = jnp.sum(ahead[:, :1]).astype(jnp.int32)
 
 
@@ -145,7 +156,7 @@
     lax.fori_loop(0, half // STEP, widen, 0)
 
 
-def pack_kernel(group, word_ref, scalar_ref, pool_ref, *rest):
+def pack_kernel(group, first, word_ref, scalar_ref, pool_ref, after_ref, *rest):
     out_refs, stage = rest[:-1], rest[-1]
     depth = out_refs[0].shape[0]
     frames = pool_ref.shape[1]
@@ -172,7 +183,7 @@
 
     step = depth if depth <= 512 else LANE
     for d, out_ref in enumerate(out_refs):
-        base = (group * len(out_refs) + d) * depth
+        base = (first + d) * depth
 
         def narrow(i, _, out_ref=out_ref, base=base):
             row = pl.multiple_of(i * step, step)
@@ -223,9 +234,11 @@
     def two_pairs(j, carry):
         return pair(2 * j + 1, pair(2 * j, carry))
 
+    order = exchange_order(sources)
+
     def in_order(value):
         for j in range(sources):
-            at = pl.multiple_of((tm_index ^ apart_of(j, sources)) * local, local)
+            at = pl.multiple_of((tm_index ^ order[j]) * local, local)
             turn[pl.ds(at, local), :] = value[j * local : (j + 1) * local]
         return turn[...]
 
@@ -244,6 +257,8 @@
     tm_count = lax.axis_size("tm")
     local_frames, half, _ = frames.shape
     frame_count = tm_count * local_frames
+    ends = group_ends(tm_count)
+    order = exchange_order(tm_count)
     list_rows = -(-(block_cycle.shape[0] + UNROLL) // (8 * LANE)) * 8
     vmem = pl.BlockSpec(memory_space=pltpu.VMEM)
     smem = pl.BlockSpec(memory_space=pltpu.SMEM)
@@ -265,7 +280,7 @@
         plan_kernel,
         out_shape=(
             jax.ShapeDtypeStruct((list_rows, LANE), jnp.int32),
-            jax.ShapeDtypeStruct((4 + GROUPS,), jnp.int32),
+            jax.ShapeDtypeStruct((3 + len(ends),), jnp.int32),
         ),
         in_specs=[pl.BlockSpec(memory_space=pltpu.HBM)] * 3,
         out_specs=(vmem, smem),
@@ -279,18 +294,19 @@
         name="plan",
     )(cycle_owner, block_cycle, block_valid)
     pool = widen(far, widen(frames))
-    members = tm_count // GROUPS
 
     def branch(size):
         depth = size * local_frames
 
         def run(words, scalars, pool):
             got = []
-            for group in range(GROUPS):
+            after = scalars
+            for group, (first, end) in enumerate(zip(ends[:-1], ends[1:])):
+                members = end - first
                 send = pl.pallas_call(
-                    functools.partial(pack_kernel, group),
+                    functools.partial(pack_kernel, group, first),
                     out_shape=(jax.ShapeDtypeStruct((depth, LANE), jnp.bfloat16),) * members,
-                    in_specs=[smem, smem, vmem],
+                    in_specs=[smem, smem, vmem, pl.BlockSpec(memory_space=pl.ANY)],
                     out_specs=(vmem,) * members,
                     scratch_shapes=[
                         pltpu.VMEM(((tm_count * size + 2) * local_frames, LANE), jnp.float32)
@@ -300,11 +316,11 @@
                         flops=2_000_000, bytes_accessed=16_000_000, transcendentals=0
                     ),
                     name="pack",
-                )(words, scalars, pool)
-                for j in range(members):
-                    apart = apart_of(group * members + j, tm_count)
+                )(words, scalars, pool, after)
+                for part, apart in zip(send, order[first:end]):
                     pairs = [(i, i ^ apart) for i in range(tm_count)]
-                    got.append(lax.ppermute(send[j], "tm", pairs) if apart else send[j])
+                    got.append(lax.ppermute(part, "tm", pairs) if apart else part)
+                after = got[first]
             return pl.pallas_call(
                 gram_kernel,
                 out_shape=jax.ShapeDtypeStruct((frame_count, frame_count), jnp.float32),

time: 54.5 us -> 54.5 us (level); the launches traced: 54.9 us -> 54 us
  waiting for transfers between devices: 10 us -> 7.35 us
  starting transfers between devices: 27.3 us -> 29 us
    ppermute x15, waiting for transfers between devices: 10 us -> 7.34 us  [run(): got.append(lax.ppermute(part, 'tm', pairs) if apart else part)]
    ppermute x15, starting transfers between devices: 26.8 us -> 28.5 us  [run(): got.append(lax.ppermute(part, 'tm', pairs) if apart else part)]
  transfers between devices with their start and end apart: 16 -> 16, of which waited for: 4 -> 4; matrix products, arithmetic and copies ran while one was open for 0% -> 0% of each run, Pallas kernels for 12% -> 14%
where the time goes in v1:
time: 54.5 us; the launch traced here: 54 us
  starting transfers between devices  29 us (53%)
  Pallas kernels  15 us (28%)
  waiting for transfers between devices  7.35 us (13%)
  local copies, waits for them, and re-layouts  2.3 us (4%)
    ppermute x15, starting transfers between devices, run(): got.append(lax.ppermute(part, 'tm', pairs) if apart else part)  28.5 us
    pallas_call x2, Pallas kernels, run(): pl.pallas_call(functools.partial(pack_kernel, group, first), out_shape=(j...  7.62 us
    ppermute x15, waiting for transfers between devices, run(): got.append(lax.ppermute(part, 'tm', pairs) if apart else part)  7.34 us
    pallas_call x1, Pallas kernels, run(): pl.pallas_call(gram_kernel, out_shape=jax.ShapeDtypeStruct((frame_count,...  3.55 us
    unnamed x10, local copies, waits for them, and re-layouts  2.3 us
    pallas_call x2, Pallas kernels, widen(): pl.pallas_call(functools.partial(widen_kernel, len(given) - 1), out_shape...  1.95 us
    pallas_call x1, Pallas kernels, on_device_routed(): pl.pallas_call(plan_kernel, out_shape=(jax.ShapeDtypeStruct((list_rows, L...  1.84 us
  transfers between devices with their start and end apart: 16, of which 4 were waited for; matrix products, arithmetic and copies ran while one was open for 0% of the time, Pallas kernels for 14%

profile of v1, /device:TPU:0, one launch (start us, length us, event | category | flops | bytes accessed | tf_op | source)
XLA Modules:
  0.0 54.0 jit_solution(16127002046567037837)
XLA Ops:
  0.0 0.5 collective-permute-start.165
  0.5 1.7 %copy-done = bf16[8,1152,128]{2,1,0:T(8,128)(2,1)S(1)} copy-done((bf16[8,1152,128]{2,1,0:T(8,128)(2,1)S(1)}, bf16[8,1152,128]{2,1,0:T(8,128)(2,1)}, u32[]{:S(2)}) %copy-start) | copy-done | bytes 2359320
  2.1 1.0 %widen.2.rest_0_ = f32[2304,8,128]{2,1,0:T(8,128)S(1)} custom-call(bf16[8,1152,128]{2,1,0:T(8,128)(2,1)S(1)} %copy-done), custom_call_target="tpu_custom_call" | custom-call | tf_op jit(solution)/shard_map/widen/pallas_call | solution.py:268
  3.1 1.8 %plan.1 = (s32[24,128]{1,0:T(8,128)S(1)}, s32[6]{0:T(128)S(1)}) custom-call(s32[32]{0:T(128)S(1)} %copy-done.3, s32[2304]{0:T(1024)S(1)} %copy-done.1, s32[2304]{0:T(1024)S(1)} %copy-done.2), custom_call_target="tpu_custom_call" | custom-call | tf_op jit(solution)/shard_map/plan/pallas_call | solution.py:279
  5.0 1.0 %widen.3 = f32[2304,8,128]{2,1,0:T(8,128)S(1)} custom-call(bf16[8,1152,128]{2,1,0:T(8,128)(2,1)S(1)} %collective-permute-done.165.in_ref, f32[2304,8,128]{2,1,0:T(8,128)S(1)} %widen.2.rest_0_), custom_call_target="tpu_custom_call", output_to_operand_aliasing={{}: (1, {})} | custom-call | tf_op jit(solution)/shard_map/widen/pallas_call | solution.py:268
  6.0 47.4 %conditional.1 = (f32[128,128]{1,0:T(8,128)S(1)}) conditional(s32[]{:T(128)} %bitcast.11, (s32[24,128]{1,0:T(8,128)S(1)}, s32[6]{0:T(128)S(1)}, f32[2304,8,128]{2,1,0:T(8,128)S(1)}) %tuple.38, (s32[24,128]{1,0:T(8,128)S(1)}, s32[6]{0:T(128)S(1)}, f32[2304,8,128]{2,1,0:T(8,128)S(1)}) %tuple.38, ...), branch_computations={%region_0.0_spmd, %region_1.0_spmd, %region_2.0_spmd, %region_3.0_... | conditional | flops 4000000 | bytes 49695328 | solution.py:336
  6.1 2.7 %pack.30 = (bf16[336,128]{1,0:T(8,128)(2,1)S(1)}, bf16[336,128]{1,0:T(8,128)(2,1)S(1)}, bf16[336,128]{1,0:T(8,128)(2,1)S(1)}, bf16[336,128]{1,0:T(8,128)(2,1)S(1)}, bf16[336,128]{1,0:T(8,128)(2,1)S(1)}) custom-call(s32[3072]{0:T(1024)S(1)} %bitcast.21, s32[6]{0:T(128)S(1)} %get-tuple-element.159.scalar_ref.after_ref, ...), custom_call_target="tpu_custom_call" | custom-call | flops 2000000 | bytes 16000000 | tf_op jit(solution)/shard_map/cond/branch_4_fun/pack/pallas_call | solution.py:306
  8.8 6.7 %collective-permute-start.60 = (bf16[336,128]{1,0:T(8,128)(2,1)S(1)}, bf16[336,128]{1,0:T(8,128)(2,1)S(1)}, u32[]{:S(2)}, u32[]{:S(2)}) collective-permute-start(bf16[336,128]{1,0:T(8,128)(2,1)S(1)} %get-tuple-element.162), channel_id=1, source_target_pairs={{0,30},{2,28},{4,26},{6,24},{8,22},{10,20},{12,18},{14,16},{16,14}... | collective-permute-start | bytes 258056 | tf_op jit(solution)/shard_map/cond/branch_4_fun/ppermute | solution.py:322
  15.5 0.2 collective-permute-start.61
  15.7 3.6 %collective-permute-start.62 = (bf16[336,128]{1,0:T(8,128)(2,1)S(1)}, bf16[336,128]{1,0:T(8,128)(2,1)S(1)}, u32[]{:S(2)}, u32[]{:S(2)}) collective-permute-start(bf16[336,128]{1,0:T(8,128)(2,1)S(1)} %get-tuple-element.164), channel_id=1, source_target_pairs={{0,26},{2,24},{4,30},{6,28},{8,18},{10,16},{12,22},{14,20},{16,10}... | collective-permute-start | bytes 258056 | tf_op jit(solution)/shard_map/cond/branch_4_fun/ppermute | solution.py:322
  19.3 0.0 collective-permute-start.63
  19.3 1.0 %collective-permute-start.64 = (bf16[336,128]{1,0:T(8,128)(2,1)S(1)}, bf16[336,128]{1,0:T(8,128)(2,1)S(1)}, u32[]{:S(2)}, u32[]{:S(2)}) collective-permute-start(bf16[336,128]{1,0:T(8,128)(2,1)S(1)} %get-tuple-element.166), channel_id=1, source_target_pairs={{0,24},{2,26},{4,28},{6,30},{8,16},{10,18},{12,20},{14,22},{16,8},... | collective-permute-start | bytes 258056 | tf_op jit(solution)/shard_map/cond/branch_4_fun/ppermute | solution.py:322
  20.2 0.0 collective-permute-done.60.after_ref.refs_0_
  20.2 4.9 %pack.31 = (bf16[336,128]{1,0:T(8,128)(2,1)S(1)}, bf16[336,128]{1,0:T(8,128)(2,1)S(1)}, bf16[336,128]{1,0:T(8,128)(2,1)S(1)}, bf16[336,128]{1,0:T(8,128)(2,1)S(1...) custom-call(s32[3072]{0:T(1024)S(1)} %bitcast.22, ...), custom_call_target="tpu_custom_call" | custom-call | flops 2000000 | bytes 16000000 | tf_op jit(solution)/shard_map/cond/branch_4_fun/pack/pallas_call | solution.py:306
  25.1 4.4 %collective-permute-start.65 = (bf16[336,128]{1,0:T(8,128)(2,1)S(1)}, bf16[336,128]{1,0:T(8,128)(2,1)S(1)}, u32[]{:S(2)}, u32[]{:S(2)}) collective-permute-start(bf16[336,128]{1,0:T(8,128)(2,1)S(1)} %get-tuple-element.167), channel_id=1, source_target_pairs={{0,12},{2,14},{4,8},{6,10},{8,4},{10,6},{12,0},{14,2},{16,28},{18,... | collective-permute-start | bytes 258056 | tf_op jit(solution)/shard_map/cond/branch_4_fun/ppermute | solution.py:322
  29.5 0.0 collective-permute-done.61.refs_1_
  29.5 2.6 %collective-permute-start.66 = (bf16[336,128]{1,0:T(8,128)(2,1)S(1)}, bf16[336,128]{1,0:T(8,128)(2,1)S(1)}, u32[]{:S(2)}, u32[]{:S(2)}) collective-permute-start(bf16[336,128]{1,0:T(8,128)(2,1)S(1)} %get-tuple-element.168), channel_id=1, source_target_pairs={{0,22},{2,20},{4,18},{6,16},{8,30},{10,28},{12,26},{14,24},{16,6},... | collective-permute-start | bytes 258056 | tf_op jit(solution)/shard_map/cond/branch_4_fun/ppermute | solution.py:322
  32.2 0.0 collective-permute-done.62.refs_2_
  32.2 1.3 %collective-permute-start.67 = (bf16[336,128]{1,0:T(8,128)(2,1)S(1)}, bf16[336,128]{1,0:T(8,128)(2,1)S(1)}, u32[]{:S(2)}, u32[]{:S(2)}) collective-permute-start(bf16[336,128]{1,0:T(8,128)(2,1)S(1)} %get-tuple-element.169), channel_id=1, source_target_pairs={{0,10},{2,8},{4,14},{6,12},{8,2},{10,0},{12,6},{14,4},{16,26},{18,... | collective-permute-start | bytes 258056 | tf_op jit(solution)/shard_map/cond/branch_4_fun/ppermute | solution.py:322
  33.4 0.9 %collective-permute-start.68 = (bf16[336,128]{1,0:T(8,128)(2,1)S(1)}, bf16[336,128]{1,0:T(8,128)(2,1)S(1)}, u32[]{:S(2)}, u32[]{:S(2)}) collective-permute-start(bf16[336,128]{1,0:T(8,128)(2,1)S(1)} %get-tuple-element.170), channel_id=1, source_target_pairs={{0,20},{2,22},{4,16},{6,18},{8,28},{10,30},{12,24},{14,26},{16,4},... | collective-permute-start | bytes 258056 | tf_op jit(solution)/shard_map/cond/branch_4_fun/ppermute | solution.py:322
  34.4 2.0 %collective-permute-start.69 = (bf16[336,128]{1,0:T(8,128)(2,1)S(1)}, bf16[336,128]{1,0:T(8,128)(2,1)S(1)}, u32[]{:S(2)}, u32[]{:S(2)}) collective-permute-start(bf16[336,128]{1,0:T(8,128)(2,1)S(1)} %get-tuple-element.171), channel_id=1, source_target_pairs={{0,8},{2,10},{4,12},{6,14},{8,0},{10,2},{12,4},{14,6},{16,24},{18,... | collective-permute-start | bytes 258056 | tf_op jit(solution)/shard_map/cond/branch_4_fun/ppermute | solution.py:322
  36.3 2.6 %collective-permute-start.70 = (bf16[336,128]{1,0:T(8,128)(2,1)S(1)}, bf16[336,128]{1,0:T(8,128)(2,1)S(1)}, u32[]{:S(2)}, u32[]{:S(2)}) collective-permute-start(bf16[336,128]{1,0:T(8,128)(2,1)S(1)} %get-tuple-element.172), channel_id=1, source_target_pairs={{0,18},{2,16},{4,22},{6,20},{8,26},{10,24},{12,30},{14,28},{16,2},... | collective-permute-start | bytes 258056 | tf_op jit(solution)/shard_map/cond/branch_4_fun/ppermute | solution.py:322
  38.9 1.2 %collective-permute-done.66.refs_6_ = bf16[336,128]{1,0:T(8,128)(2,1)S(1)} collective-permute-done((bf16[336,128]{1,0:T(8,128)(2,1)S(1)}, bf16[336,128]{1,0:T(8,128)(2,1)S(1)}, u32[]{:S(2)}, u32[]{:S(2)}) %collective-permute-start.66) | collective-permute-done | bytes 86048 | tf_op jit(solution)/shard_map/cond/branch_4_fun/ppermute | solution.py:322
  40.1 0.9 %collective-permute-start.72 = (bf16[336,128]{1,0:T(8,128)(2,1)S(1)}, bf16[336,128]{1,0:T(8,128)(2,1)S(1)}, u32[]{:S(2)}, u32[]{:S(2)}) collective-permute-start(bf16[336,128]{1,0:T(8,128)(2,1)S(1)} %get-tuple-element.174), channel_id=1, source_target_pairs={{0,16},{2,18},{4,20},{6,22},{8,24},{10,26},{12,28},{14,30},{16,0},... | collective-permute-start | bytes 258056 | tf_op jit(solution)/shard_map/cond/branch_4_fun/ppermute | solution.py:322
  41.0 3.6 %collective-permute-done.68.refs_8_ = bf16[336,128]{1,0:T(8,128)(2,1)S(1)} collective-permute-done((bf16[336,128]{1,0:T(8,128)(2,1)S(1)}, bf16[336,128]{1,0:T(8,128)(2,1)S(1)}, u32[]{:S(2)}, u32[]{:S(2)}) %collective-permute-start.68) | collective-permute-done | bytes 86048 | tf_op jit(solution)/shard_map/cond/branch_4_fun/ppermute | solution.py:322
  44.6 0.5 collective-permute-start.73
  45.1 2.0 %collective-permute-start.74 = (bf16[336,128]{1,0:T(8,128)(2,1)S(1)}, bf16[336,128]{1,0:T(8,128)(2,1)S(1)}, u32[]{:S(2)}, u32[]{:S(2)}) collective-permute-start(bf16[336,128]{1,0:T(8,128)(2,1)S(1)} %get-tuple-element.176), channel_id=1, source_target_pairs={{0,2},{2,0},{4,6},{6,4},{8,10},{10,8},{12,14},{14,12},{16,18},{18,... | collective-permute-start | bytes 258056 | tf_op jit(solution)/shard_map/cond/branch_4_fun/ppermute | solution.py:322
  47.1 2.0 %collective-permute-done.73.refs_13_ = bf16[336,128]{1,0:T(8,128)(2,1)S(1)} collective-permute-done((bf16[336,128]{1,0:T(8,128)(2,1)S(1)}, bf16[336,128]{1,0:T(8,128)(2,1)S(1)}, u32[]{:S(2)}, u32[]{:S(2)}) %collective-permute-start.73) | collective-permute-done | bytes 86048 | tf_op jit(solution)/shard_map/cond/branch_4_fun/ppermute | solution.py:322
  49.1 0.5 collective-permute-done.74.refs_14_
  49.6 3.6 %gram.15 = f32[128,128]{1,0:T(8,128)S(1)} custom-call(s32[6]{0:T(128)S(1)} %get-tuple-element.159.scalar_ref.after_ref, bf16[336,128]{1,0:T(8,128)(2,1)S(1)} %collective-permute-done.60.after_ref.refs_0_, bf16[336,128]{1,0:T(8,128)(2,1)S(1)} %collective-permute-done.61.refs_1_, bf16[336,128]{1,0:T(8,128)(2,1)S(1)} %collective-permute-done.62.refs_2_, ...), custom_call_target="tpu_custom_call" | custom-call | tf_op jit(solution)/shard_map/cond/branch_4_fun/gram/pallas_call | solution.py:324
  53.4 0.0 copy-start.4
  53.4 0.6 %copy-done.4 = f32[128,128]{1,0:T(8,128)} copy-done((f32[128,128]{1,0:T(8,128)}, f32[128,128]{1,0:T(8,128)S(1)}, u32[]{:S(2)}) %copy-start.4) | copy-done | bytes 65560
  (17 shorter events, 0.0 us)
Async XLA Ops:
  0.0 5.0 %collective-permute-start.165 = (bf16[8,1152,128]{2,1,0:T(8,128)(2,1)}, bf16[8,1152,128]{2,1,0:T(8,128)(2,1)S(1)}, u32[]{:S(2)}, u32[]{:S(2)}) collective-permute-start(bf16[8,1152,128]{2,1,0:T(8,128)(2,1)} %in_ref.1), channel_id=1, source_target_pairs={{0,1},{1,0},{2,3},{3,2},{4,5},{5,4},{6,7},{7,6},{8,9},{9,8},{10,11... | collective-permute-start | bytes 7077896 | tf_op jit(solution)/shard_map/ppermute | solution.py:278
  0.5 1.7 %copy-start = (bf16[8,1152,128]{2,1,0:T(8,128)(2,1)S(1)}, bf16[8,1152,128]{2,1,0:T(8,128)(2,1)}, u32[]{:S(2)}) copy-start(bf16[8,1152,128]{2,1,0:T(8,128)(2,1)} %in_ref.1) | copy-start | bytes 7077892
  2.1 1.0 %copy-start.1 = (s32[2304]{0:T(1024)S(1)}, s32[2304]{0:T(1024)}, u32[]{:S(2)}) copy-start(s32[2304]{0:T(1024)} %cycle_in.1) | copy-start | bytes 27652
  2.1 1.0 %copy-start.2 = (s32[2304]{0:T(1024)S(1)}, s32[2304]{0:T(1024)}, u32[]{:S(2)}) copy-start(s32[2304]{0:T(1024)} %valid_in.1) | copy-start | bytes 27652
  2.1 1.0 %copy-start.3 = (s32[32]{0:T(128)S(1)}, s32[32]{0:T(128)}, u32[]{:S(2)}) copy-start(s32[32]{0:T(128)} %owner_in.1) | copy-start | bytes 388
  8.8 11.4 %collective-permute-start.60 = (bf16[336,128]{1,0:T(8,128)(2,1)S(1)}, bf16[336,128]{1,0:T(8,128)(2,1)S(1)}, u32[]{:S(2)}, u32[]{:S(2)}) collective-permute-start(bf16[336,128]{1,0:T(8,128)(2,1)S(1)} %get-tuple-element.162), channel_id=1, source_target_pairs={{0,30},{2,28},{4,26},{6,24},{8,22},{10,20},{12,18},{14,16},{16,14}... | collective-permute-start | bytes 258056 | tf_op jit(solution)/shard_map/cond/branch_4_fun/ppermute | solution.py:322
  15.5 14.0 %collective-permute-start.61 = (bf16[336,128]{1,0:T(8,128)(2,1)S(1)}, bf16[336,128]{1,0:T(8,128)(2,1)S(1)}, u32[]{:S(2)}, u32[]{:S(2)}) collective-permute-start(bf16[336,128]{1,0:T(8,128)(2,1)S(1)} %get-tuple-element.163), channel_id=1, source_target_pairs={{0,28},{2,30},{4,24},{6,26},{8,20},{10,22},{12,16},{14,18},{16,12}... | collective-permute-start | bytes 258056 | tf_op jit(solution)/shard_map/cond/branch_4_fun/ppermute | solution.py:322
  15.7 16.5 %collective-permute-start.62 = (bf16[336,128]{1,0:T(8,128)(2,1)S(1)}, bf16[336,128]{1,0:T(8,128)(2,1)S(1)}, u32[]{:S(2)}, u32[]{:S(2)}) collective-permute-start(bf16[336,128]{1,0:T(8,128)(2,1)S(1)} %get-tuple-element.164), channel_id=1, source_target_pairs={{0,26},{2,24},{4,30},{6,28},{8,18},{10,16},{12,22},{14,20},{16,10}... | collective-permute-start | bytes 258056 | tf_op jit(solution)/shard_map/cond/branch_4_fun/ppermute | solution.py:322
  19.3 14.2 %collective-permute-start.63 = (bf16[336,128]{1,0:T(8,128)(2,1)S(1)}, bf16[336,128]{1,0:T(8,128)(2,1)S(1)}, u32[]{:S(2)}, u32[]{:S(2)}) collective-permute-start(bf16[336,128]{1,0:T(8,128)(2,1)S(1)} %get-tuple-element.165), channel_id=1, source_target_pairs={{0,14},{2,12},{4,10},{6,8},{8,6},{10,4},{12,2},{14,0},{16,30},{18,... | collective-permute-start | bytes 258056 | tf_op jit(solution)/shard_map/cond/branch_4_fun/ppermute | solution.py:322
  19.3 15.1 %collective-permute-start.64 = (bf16[336,128]{1,0:T(8,128)(2,1)S(1)}, bf16[336,128]{1,0:T(8,128)(2,1)S(1)}, u32[]{:S(2)}, u32[]{:S(2)}) collective-permute-start(bf16[336,128]{1,0:T(8,128)(2,1)S(1)} %get-tuple-element.166), channel_id=1, source_target_pairs={{0,24},{2,26},{4,28},{6,30},{8,16},{10,18},{12,20},{14,22},{16,8},... | collective-permute-start | bytes 258056 | tf_op jit(solution)/shard_map/cond/branch_4_fun/ppermute | solution.py:322
  25.1 11.2 %collective-permute-start.65 = (bf16[336,128]{1,0:T(8,128)(2,1)S(1)}, bf16[336,128]{1,0:T(8,128)(2,1)S(1)}, u32[]{:S(2)}, u32[]{:S(2)}) collective-permute-start(bf16[336,128]{1,0:T(8,128)(2,1)S(1)} %get-tuple-element.167), channel_id=1, source_target_pairs={{0,12},{2,14},{4,8},{6,10},{8,4},{10,6},{12,0},{14,2},{16,28},{18,... | collective-permute-start | bytes 258056 | tf_op jit(solution)/shard_map/cond/branch_4_fun/ppermute | solution.py:322
  29.5 10.5 %collective-permute-start.66 = (bf16[336,128]{1,0:T(8,128)(2,1)S(1)}, bf16[336,128]{1,0:T(8,128)(2,1)S(1)}, u32[]{:S(2)}, u32[]{:S(2)}) collective-permute-start(bf16[336,128]{1,0:T(8,128)(2,1)S(1)} %get-tuple-element.168), channel_id=1, source_target_pairs={{0,22},{2,20},{4,18},{6,16},{8,30},{10,28},{12,26},{14,24},{16,6},... | collective-permute-start | bytes 258056 | tf_op jit(solution)/shard_map/cond/branch_4_fun/ppermute | solution.py:322
  32.2 7.9 %collective-permute-start.67 = (bf16[336,128]{1,0:T(8,128)(2,1)S(1)}, bf16[336,128]{1,0:T(8,128)(2,1)S(1)}, u32[]{:S(2)}, u32[]{:S(2)}) collective-permute-start(bf16[336,128]{1,0:T(8,128)(2,1)S(1)} %get-tuple-element.169), channel_id=1, source_target_pairs={{0,10},{2,8},{4,14},{6,12},{8,2},{10,0},{12,6},{14,4},{16,26},{18,... | collective-permute-start | bytes 258056 | tf_op jit(solution)/shard_map/cond/branch_4_fun/ppermute | solution.py:322
  33.4 11.2 %collective-permute-start.68 = (bf16[336,128]{1,0:T(8,128)(2,1)S(1)}, bf16[336,128]{1,0:T(8,128)(2,1)S(1)}, u32[]{:S(2)}, u32[]{:S(2)}) collective-permute-start(bf16[336,128]{1,0:T(8,128)(2,1)S(1)} %get-tuple-element.170), channel_id=1, source_target_pairs={{0,20},{2,22},{4,16},{6,18},{8,28},{10,30},{12,24},{14,26},{16,4},... | collective-permute-start | bytes 258056 | tf_op jit(solution)/shard_map/cond/branch_4_fun/ppermute | solution.py:322
  34.4 10.7 %collective-permute-start.69 = (bf16[336,128]{1,0:T(8,128)(2,1)S(1)}, bf16[336,128]{1,0:T(8,128)(2,1)S(1)}, u32[]{:S(2)}, u32[]{:S(2)}) collective-permute-start(bf16[336,128]{1,0:T(8,128)(2,1)S(1)} %get-tuple-element.171), channel_id=1, source_target_pairs={{0,8},{2,10},{4,12},{6,14},{8,0},{10,2},{12,4},{14,6},{16,24},{18,... | collective-permute-start | bytes 258056 | tf_op jit(solution)/shard_map/cond/branch_4_fun/ppermute | solution.py:322
  36.3 10.7 %collective-permute-start.70 = (bf16[336,128]{1,0:T(8,128)(2,1)S(1)}, bf16[336,128]{1,0:T(8,128)(2,1)S(1)}, u32[]{:S(2)}, u32[]{:S(2)}) collective-permute-start(bf16[336,128]{1,0:T(8,128)(2,1)S(1)} %get-tuple-element.172), channel_id=1, source_target_pairs={{0,18},{2,16},{4,22},{6,20},{8,26},{10,24},{12,30},{14,28},{16,2},... | collective-permute-start | bytes 258056 | tf_op jit(solution)/shard_map/cond/branch_4_fun/ppermute | solution.py:322
  40.1 7.0 %collective-permute-start.71 = (bf16[336,128]{1,0:T(8,128)(2,1)S(1)}, bf16[336,128]{1,0:T(8,128)(2,1)S(1)}, u32[]{:S(2)}, u32[]{:S(2)}) collective-permute-start(bf16[336,128]{1,0:T(8,128)(2,1)S(1)} %get-tuple-element.173), channel_id=1, source_target_pairs={{0,6},{2,4},{4,2},{6,0},{8,14},{10,12},{12,10},{14,8},{16,22},{18,... | collective-permute-start | bytes 258056 | tf_op jit(solution)/shard_map/cond/branch_4_fun/ppermute | solution.py:322
  40.1 7.0 %collective-permute-start.72 = (bf16[336,128]{1,0:T(8,128)(2,1)S(1)}, bf16[336,128]{1,0:T(8,128)(2,1)S(1)}, u32[]{:S(2)}, u32[]{:S(2)}) collective-permute-start(bf16[336,128]{1,0:T(8,128)(2,1)S(1)} %get-tuple-element.174), channel_id=1, source_target_pairs={{0,16},{2,18},{4,20},{6,22},{8,24},{10,26},{12,28},{14,30},{16,0},... | collective-permute-start | bytes 258056 | tf_op jit(solution)/shard_map/cond/branch_4_fun/ppermute | solution.py:322
  44.6 4.5 %collective-permute-start.73 = (bf16[336,128]{1,0:T(8,128)(2,1)S(1)}, bf16[336,128]{1,0:T(8,128)(2,1)S(1)}, u32[]{:S(2)}, u32[]{:S(2)}) collective-permute-start(bf16[336,128]{1,0:T(8,128)(2,1)S(1)} %get-tuple-element.175), channel_id=1, source_target_pairs={{0,4},{2,6},{4,0},{6,2},{8,12},{10,14},{12,8},{14,10},{16,20},{18,... | collective-permute-start | bytes 258056 | tf_op jit(solution)/shard_map/cond/branch_4_fun/ppermute | solution.py:322
  45.1 4.5 %collective-permute-start.74 = (bf16[336,128]{1,0:T(8,128)(2,1)S(1)}, bf16[336,128]{1,0:T(8,128)(2,1)S(1)}, u32[]{:S(2)}, u32[]{:S(2)}) collective-permute-start(bf16[336,128]{1,0:T(8,128)(2,1)S(1)} %get-tuple-element.176), channel_id=1, source_target_pairs={{0,2},{2,0},{4,6},{6,4},{8,10},{10,8},{12,14},{14,12},{16,18},{18,... | collective-permute-start | bytes 258056 | tf_op jit(solution)/shard_map/cond/branch_4_fun/ppermute | solution.py:322
  53.4 0.6 %copy-start.4 = (f32[128,128]{1,0:T(8,128)}, f32[128,128]{1,0:T(8,128)S(1)}, u32[]{:S(2)}) copy-start(f32[128,128]{1,0:T(8,128)S(1)} %get-tuple-element.651) | copy-start | bytes 196612

commit v2 on v1

--- a/solution.py
+++ b/solution.py
@@ -9,10 +9,10 @@
 
 LANE = 128
 UNROLL = 32
-FIRST = 5
+FIRST = 3
 STEP = 128
 VMEM_LIMIT = 24 * 1024 * 1024
-LADDER = (24, 32, 36, 40, 42, 44, 46, 50, 64, 96, 144)
+LADDER = (32, 40, 42, 44, 46, 56, 144)
 NT = (((1,), (1,)), ((), ()))
 
 
@@ -20,9 +20,9 @@
     side = count // 2
     across = [count - 1 - i for i in range(side)]
     beside = [side - 1 - i for i in range(side)]
-    order = across[:3] + beside[:1] + across[3:4]
-    for far, near in zip(across[4:], beside[1:]):
-        order += [near, far]
+    order = across[:FIRST]
+    for far, near in zip(across[FIRST:], beside):
+        order += [far, near]
     return order + [apart for apart in beside if apart not in order]
 
 
@@ -197,42 +197,53 @@
 
 
 def gram_kernel(scalar_ref, *refs):
-    x_refs, (out_ref, turn) = refs[:-2], refs[-2:]
+    x_refs, (out_ref, turn, scales, totals) = refs[:-4], refs[-4:]
     sources = len(x_refs)
     frames = out_ref.shape[0]
     local = frames // sources
-    pixels = scalar_ref[2]
-    tm_index = scalar_ref[1]
+    size = x_refs[0].shape[0] // local
+    tm_index, pixels = scalar_ref[1], scalar_ref[2]
+    pairs = (pixels + 2 * LANE - 1) // (2 * LANE)
     lane = lax.broadcasted_iota(jnp.int32, (1, LANE), 1)
-
-    last = x_refs[0].shape[0] // (2 * local) - 1
-
-    def pair(j, carry):
-        gram, total = carry
-        rows = pl.ds(pl.multiple_of(jnp.minimum(j, last) * 2 * local, 2 * local), 2 * local)
+    row = lax.broadcasted_iota(jnp.int32, (8, LANE), 0)
+
+    def scale(i, _):
+        begin = jnp.minimum(8 * i, size - 8)
+        part = pl.ds(pl.multiple_of(begin * local, 2 * local), 8 * local)
+        each = x_refs[0][part, :].astype(jnp.float32)
+        for ref in x_refs[1:]:
+            each = each + ref[part, :].astype(jnp.float32)
+        mean = jnp.sum(each.reshape(8, local, LANE), axis=1) / frames
+        used = lane + (begin + row) * LANE < pixels
+        scales[pl.ds(begin, 8), :] = jnp.where(used, 1.0 / jnp.where(used, mean, 1.0), 0.0)
+        return 0
+
+    lax.fori_loop(0, (pairs + 3) // 4, scale, 0)
+    totals[...] = jnp.zeros(totals.shape, jnp.float32)
+
+    def pair(j, gram):
+        rows = pl.ds(pl.multiple_of(j * 2 * local, 2 * local), 2 * local)
         both = [ref[rows, :].astype(jnp.float32) for ref in x_refs]
         exact, high, low = [], [], []
+        total = totals[...]
         for i in range(2):
             used = lane + (2 * j + i) * LANE < pixels
             x = jnp.concatenate([part[i * local : (i + 1) * local] for part in both], axis=0)
             x = jnp.where(used, x, 0.0)
-            mean = jnp.where(used, jnp.sum(x, axis=0, keepdims=True) / frames, 1.0)
-            scale = 1.0 / mean
-            total = total + x * scale
-            y = x * (scale * scale)
+            factor = scales[pl.ds(2 * j + i, 1), :]
+            normed = x * factor
+            total = total + normed
+            y = normed * factor
             top = y.astype(jnp.bfloat16)
             exact.append(x.astype(jnp.bfloat16))
             high.append(top)
             low.append((y - top.astype(jnp.float32)).astype(jnp.bfloat16))
+        totals[...] = total
         left = jnp.concatenate(exact, axis=1)
         right = jnp.concatenate(
             [jnp.concatenate(high, axis=1), jnp.concatenate(low, axis=1)], axis=0
         )
-        gram = gram + lax.dot_general(left, right, NT, preferred_element_type=jnp.float32)
-        return gram, total
-
-    def two_pairs(j, carry):
-        return pair(2 * j + 1, pair(2 * j, carry))
+        return gram + lax.dot_general(left, right, NT, preferred_element_type=jnp.float32)
 
     order = exchange_order(sources)
 
@@ -242,12 +253,10 @@
             turn[pl.ds(at, local), :] = value[j * local : (j + 1) * local]
         return turn[...]
 
-    carry = (jnp.zeros((frames, 2 * frames), jnp.float32), jnp.zeros((frames, LANE), jnp.float32))
-    pairs = (pixels + 2 * LANE - 1) // (2 * LANE)
-    gram, total = lax.fori_loop(0, (pairs + 1) // 2, two_pairs, carry)
+    gram = lax.fori_loop(0, pairs, pair, jnp.zeros((frames, 2 * frames), jnp.float32))
     gram = in_order(gram[:, :frames] + gram[:, frames:])
     gram = in_order(gram.T)
-    total = in_order(total)
+    total = in_order(totals[...])
     first = jnp.sum(total, axis=1, keepdims=True)
     second = jnp.sum(total.T, axis=0, keepdims=True)
     out_ref[...] = pixels.astype(jnp.float32) * gram / (first * second)
@@ -264,13 +273,13 @@
     smem = pl.BlockSpec(memory_space=pltpu.SMEM)
     params = pltpu.CompilerParams(vmem_limit_bytes=VMEM_LIMIT)
 
-    def widen(*given):
+    def widen(part, *given):
         return pl.pallas_call(
-            functools.partial(widen_kernel, len(given) - 1),
+            functools.partial(widen_kernel, part),
             out_shape=jax.ShapeDtypeStruct((2 * half, local_frames, LANE), jnp.float32),
             in_specs=[vmem] * len(given),
             out_specs=vmem,
-            input_output_aliases={1: 0} if len(given) > 1 else {},
+            input_output_aliases={1: 0} if part else {},
             compiler_params=params,
             name="widen",
         )(*given)
@@ -293,7 +302,7 @@
         compiler_params=params,
         name="plan",
     )(cycle_owner, block_cycle, block_valid)
-    pool = widen(far, widen(frames))
+    pool = widen(1, far, widen(0, frames))
 
     def branch(size):
         depth = size * local_frames
@@ -326,7 +335,11 @@
                 out_shape=jax.ShapeDtypeStruct((frame_count, frame_count), jnp.float32),
                 in_specs=[smem] + [vmem] * tm_count,
                 out_specs=vmem,
-                scratch_shapes=[pltpu.VMEM((frame_count, LANE), jnp.float32)],
+                scratch_shapes=[
+                    pltpu.VMEM((frame_count, LANE), jnp.float32),
+                    pltpu.VMEM((size, LANE), jnp.float32),
+                    pltpu.VMEM((frame_count, LANE), jnp.float32),
+                ],
                 compiler_params=params,
                 name="gram",
             )(scalars, *got)

time: 54.5 us -> 59 us (1.083)
  starting transfers between devices: 29 us -> 31.1 us
  waiting for transfers between devices: 7.35 us -> 8.89 us
  Pallas kernels: 15 us -> 16.2 us
    ppermute x15, starting transfers between devices: 28.5 us -> 30.6 us  [run(): got.append(lax.ppermute(part, 'tm', pairs) if apart else part)]
    ppermute x15, waiting for transfers between devices: 7.34 us -> 8.89 us  [run(): got.append(lax.ppermute(part, 'tm', pairs) if apart else part)]
    pallas_call x1, Pallas kernels: 3.55 us -> 4.79 us  [run(): pl.pallas_call(gram_kernel, out_shape=jax.ShapeDtypeStruct((frame_count,...]
  transfers between devices with their start and end apart: 16 -> 16, of which waited for: 4 -> 5; matrix products, arithmetic and copies ran while one was open for 0% -> 0% of each run, Pallas kernels for 14% -> 15%
where the time goes in v2:
time: 59 us; the launch traced here: 58.7 us
  starting transfers between devices  31.1 us (53%)
  Pallas kernels  16.2 us (27%)
  waiting for transfers between devices  8.89 us (15%)
  local copies, waits for them, and re-layouts  2.3 us (4%)
    ppermute x15, starting transfers between devices, run(): got.append(lax.ppermute(part, 'tm', pairs) if apart else part)  30.6 us
    ppermute x15, waiting for transfers between devices, run(): got.append(lax.ppermute(part, 'tm', pairs) if apart else part)  8.89 us
    pallas_call x2, Pallas kernels, run(): pl.pallas_call(functools.partial(pack_kernel, group, first), out_shape=(j...  7.62 us
    pallas_call x1, Pallas kernels, run(): pl.pallas_call(gram_kernel, out_shape=jax.ShapeDtypeStruct((frame_count,...  4.79 us
    unnamed x10, local copies, waits for them, and re-layouts  2.3 us
    pallas_call x2, Pallas kernels, widen(): pl.pallas_call(functools.partial(widen_kernel, part), out_shape=jax.Shape...  1.95 us
    pallas_call x1, Pallas kernels, on_device_routed(): pl.pallas_call(plan_kernel, out_shape=(jax.ShapeDtypeStruct((list_rows, L...  1.84 us
  transfers between devices with their start and end apart: 16, of which 5 were waited for; matrix products, arithmetic and copies ran while one was open for 0% of the time, Pallas kernels for 15%

profile of v2, /device:TPU:0, one launch (start us, length us, event | category | flops | bytes accessed | tf_op | source)
XLA Modules:
  0.0 58.7 jit_solution(1456208070401048051)
XLA Ops:
  0.0 0.5 collective-permute-start.105
  0.5 1.7 %copy-done = bf16[8,1152,128]{2,1,0:T(8,128)(2,1)S(1)} copy-done((bf16[8,1152,128]{2,1,0:T(8,128)(2,1)S(1)}, bf16[8,1152,128]{2,1,0:T(8,128)(2,1)}, u32[]{:S(2)}) %copy-start) | copy-done | bytes 2359320
  2.1 1.0 %widen.2.rest_0_ = f32[2304,8,128]{2,1,0:T(8,128)S(1)} custom-call(bf16[8,1152,128]{2,1,0:T(8,128)(2,1)S(1)} %copy-done), custom_call_target="tpu_custom_call" | custom-call | tf_op jit(solution)/shard_map/widen/pallas_call | solution.py:277
  3.1 1.8 %plan.1 = (s32[24,128]{1,0:T(8,128)S(1)}, s32[6]{0:T(128)S(1)}) custom-call(s32[32]{0:T(128)S(1)} %copy-done.3, s32[2304]{0:T(1024)S(1)} %copy-done.1, s32[2304]{0:T(1024)S(1)} %copy-done.2), custom_call_target="tpu_custom_call" | custom-call | tf_op jit(solution)/shard_map/plan/pallas_call | solution.py:288
  5.0 1.0 %widen.3 = f32[2304,8,128]{2,1,0:T(8,128)S(1)} custom-call(bf16[8,1152,128]{2,1,0:T(8,128)(2,1)S(1)} %collective-permute-done.105.in_ref, f32[2304,8,128]{2,1,0:T(8,128)S(1)} %widen.2.rest_0_), custom_call_target="tpu_custom_call", output_to_operand_aliasing={{}: (1, {})} | custom-call | tf_op jit(solution)/shard_map/widen/pallas_call | solution.py:277
  6.0 52.0 %conditional.1 = (f32[128,128]{1,0:T(8,128)S(1)}) conditional(s32[]{:T(128)} %bitcast.7, (s32[24,128]{1,0:T(8,128)S(1)}, s32[6]{0:T(128)S(1)}, f32[2304,8,128]{2,1,0:T(8,128)S(1)}) %tuple.26, (s32[24,128]{1,0:T(8,128)S(1)}, s32[6]{0:T(128)S(1)}, f32[2304,8,128]{2,1,0:T(8,128)S(1)}) %tuple.26, ...), branch_computations={%region_0.0_spmd, %region_1.0_spmd, %region_2.0_spmd, %region_3.0_... | conditional | flops 4000000 | bytes 49695328 | solution.py:349
  6.0 1.9 %pack.18 = (bf16[336,128]{1,0:T(8,128)(2,1)S(1)}, bf16[336,128]{1,0:T(8,128)(2,1)S(1)}, bf16[336,128]{1,0:T(8,128)(2,1)S(1)}) custom-call(s32[3072]{0:T(1024)S(1)} %bitcast.13, s32[6]{0:T(128)S(1)} %get-tuple-element.93.scalar_ref.after_ref, f32[2304,8,128]{2,1,0:T(8,128)S(1)} %get-tuple-element.95.pool_ref, s32[6]{0:T(128)S(1)} %get-tuple-element.93.scalar_ref.after_ref), custom_call_target="tpu_custom_call" | custom-call | flops 2000000 | bytes 16000000 | tf_op jit(solution)/shard_map/cond/branch_2_fun/pack/pallas_call | solution.py:315
  8.0 6.7 %collective-permute-start.30 = (bf16[336,128]{1,0:T(8,128)(2,1)S(1)}, bf16[336,128]{1,0:T(8,128)(2,1)S(1)}, u32[]{:S(2)}, u32[]{:S(2)}) collective-permute-start(bf16[336,128]{1,0:T(8,128)(2,1)S(1)} %get-tuple-element.96), channel_id=1, source_target_pairs={{0,30},{2,28},{4,26},{6,24},{8,22},{10,20},{12,18},{14,16},{16,14}... | collective-permute-start | bytes 258056 | tf_op jit(solution)/shard_map/cond/branch_2_fun/ppermute | solution.py:331
  14.7 0.2 collective-permute-start.31
  14.8 3.6 %collective-permute-start.32 = (bf16[336,128]{1,0:T(8,128)(2,1)S(1)}, bf16[336,128]{1,0:T(8,128)(2,1)S(1)}, u32[]{:S(2)}, u32[]{:S(2)}) collective-permute-start(bf16[336,128]{1,0:T(8,128)(2,1)S(1)} %get-tuple-element.98), channel_id=1, source_target_pairs={{0,26},{2,24},{4,30},{6,28},{8,18},{10,16},{12,22},{14,20},{16,10}... | collective-permute-start | bytes 258056 | tf_op jit(solution)/shard_map/cond/branch_2_fun/ppermute | solution.py:331
  18.4 0.0 collective-permute-done.30.after_ref.refs_0_
  18.4 5.7 %pack.19 = (bf16[336,128]{1,0:T(8,128)(2,1)S(1)}, bf16[336,128]{1,0:T(8,128)(2,1)S(1)}, bf16[336,128]{1,0:T(8,128)(2,1)S(1)}, bf16[336,128]{1,0:T(8,128)(2,1)S(1...) custom-call(s32[3072]{0:T(1024)S(1)} %bitcast.14, ...), custom_call_target="tpu_custom_call" | custom-call | flops 2000000 | bytes 16000000 | tf_op jit(solution)/shard_map/cond/branch_2_fun/pack/pallas_call | solution.py:315
  24.1 3.5 %collective-permute-start.33 = (bf16[336,128]{1,0:T(8,128)(2,1)S(1)}, bf16[336,128]{1,0:T(8,128)(2,1)S(1)}, u32[]{:S(2)}, u32[]{:S(2)}) collective-permute-start(bf16[336,128]{1,0:T(8,128)(2,1)S(1)} %get-tuple-element.99), channel_id=1, source_target_pairs={{0,24},{2,26},{4,28},{6,30},{8,16},{10,18},{12,20},{14,22},{16,8},... | collective-permute-start | bytes 258056 | tf_op jit(solution)/shard_map/cond/branch_2_fun/ppermute | solution.py:331
  27.6 5.1 %collective-permute-start.34 = (bf16[336,128]{1,0:T(8,128)(2,1)S(1)}, bf16[336,128]{1,0:T(8,128)(2,1)S(1)}, u32[]{:S(2)}, u32[]{:S(2)}) collective-permute-start(bf16[336,128]{1,0:T(8,128)(2,1)S(1)} %get-tuple-element.100), channel_id=1, source_target_pairs={{0,14},{2,12},{4,10},{6,8},{8,6},{10,4},{12,2},{14,0},{16,30},{18,... | collective-permute-start | bytes 258056 | tf_op jit(solution)/shard_map/cond/branch_2_fun/ppermute | solution.py:331
  32.8 2.7 %collective-permute-start.36 = (bf16[336,128]{1,0:T(8,128)(2,1)S(1)}, bf16[336,128]{1,0:T(8,128)(2,1)S(1)}, u32[]{:S(2)}, u32[]{:S(2)}) collective-permute-start(bf16[336,128]{1,0:T(8,128)(2,1)S(1)} %get-tuple-element.102), channel_id=1, source_target_pairs={{0,12},{2,14},{4,8},{6,10},{8,4},{10,6},{12,0},{14,2},{16,28},{18,... | collective-permute-start | bytes 258056 | tf_op jit(solution)/shard_map/cond/branch_2_fun/ppermute | solution.py:331
  35.5 1.1 %collective-permute-start.37 = (bf16[336,128]{1,0:T(8,128)(2,1)S(1)}, bf16[336,128]{1,0:T(8,128)(2,1)S(1)}, u32[]{:S(2)}, u32[]{:S(2)}) collective-permute-start(bf16[336,128]{1,0:T(8,128)(2,1)S(1)} %get-tuple-element.103), channel_id=1, source_target_pairs={{0,20},{2,22},{4,16},{6,18},{8,28},{10,30},{12,24},{14,26},{16,4},... | collective-permute-start | bytes 258056 | tf_op jit(solution)/shard_map/cond/branch_2_fun/ppermute | solution.py:331
  36.6 0.0 collective-permute-done.33.refs_3_
  36.6 1.0 %collective-permute-start.38 = (bf16[336,128]{1,0:T(8,128)(2,1)S(1)}, bf16[336,128]{1,0:T(8,128)(2,1)S(1)}, u32[]{:S(2)}, u32[]{:S(2)}) collective-permute-start(bf16[336,128]{1,0:T(8,128)(2,1)S(1)} %get-tuple-element.104), channel_id=1, source_target_pairs={{0,10},{2,8},{4,14},{6,12},{8,2},{10,0},{12,6},{14,4},{16,26},{18,... | collective-permute-start | bytes 258056 | tf_op jit(solution)/shard_map/cond/branch_2_fun/ppermute | solution.py:331
  37.6 0.0 collective-permute-done.34.refs_4_
  37.6 1.9 %collective-permute-start.39 = (bf16[336,128]{1,0:T(8,128)(2,1)S(1)}, bf16[336,128]{1,0:T(8,128)(2,1)S(1)}, u32[]{:S(2)}, u32[]{:S(2)}) collective-permute-start(bf16[336,128]{1,0:T(8,128)(2,1)S(1)} %get-tuple-element.105), channel_id=1, source_target_pairs={{0,18},{2,16},{4,22},{6,20},{8,26},{10,24},{12,30},{14,28},{16,2},... | collective-permute-start | bytes 258056 | tf_op jit(solution)/shard_map/cond/branch_2_fun/ppermute | solution.py:331
  39.5 3.5 %collective-permute-done.35.refs_5_ = bf16[336,128]{1,0:T(8,128)(2,1)S(1)} collective-permute-done((bf16[336,128]{1,0:T(8,128)(2,1)S(1)}, bf16[336,128]{1,0:T(8,128)(2,1)S(1)}, u32[]{:S(2)}, u32[]{:S(2)}) %collective-permute-start.35) | collective-permute-done | bytes 86048 | tf_op jit(solution)/shard_map/cond/branch_2_fun/ppermute | solution.py:331
  43.0 0.0 collective-permute-done.36.refs_6_
  43.0 0.6 %collective-permute-start.41 = (bf16[336,128]{1,0:T(8,128)(2,1)S(1)}, bf16[336,128]{1,0:T(8,128)(2,1)S(1)}, u32[]{:S(2)}, u32[]{:S(2)}) collective-permute-start(bf16[336,128]{1,0:T(8,128)(2,1)S(1)} %get-tuple-element.107), channel_id=1, source_target_pairs={{0,16},{2,18},{4,20},{6,22},{8,24},{10,26},{12,28},{14,30},{16,0},... | collective-permute-start | bytes 258056 | tf_op jit(solution)/shard_map/cond/branch_2_fun/ppermute | solution.py:331
  43.6 0.9 %collective-permute-done.37.refs_7_ = bf16[336,128]{1,0:T(8,128)(2,1)S(1)} collective-permute-done((bf16[336,128]{1,0:T(8,128)(2,1)S(1)}, bf16[336,128]{1,0:T(8,128)(2,1)S(1)}, u32[]{:S(2)}, u32[]{:S(2)}) %collective-permute-start.37) | collective-permute-done | bytes 86048 | tf_op jit(solution)/shard_map/cond/branch_2_fun/ppermute | solution.py:331
  44.6 0.3 collective-permute-start.42
  44.9 3.8 %collective-permute-start.43 = (bf16[336,128]{1,0:T(8,128)(2,1)S(1)}, bf16[336,128]{1,0:T(8,128)(2,1)S(1)}, u32[]{:S(2)}, u32[]{:S(2)}) collective-permute-start(bf16[336,128]{1,0:T(8,128)(2,1)S(1)} %get-tuple-element.109), channel_id=1, source_target_pairs={{0,4},{2,6},{4,0},{6,2},{8,12},{10,14},{12,8},{14,10},{16,20},{18,... | collective-permute-start | bytes 258056 | tf_op jit(solution)/shard_map/cond/branch_2_fun/ppermute | solution.py:331
  48.8 1.2 %collective-permute-done.42.refs_12_ = bf16[336,128]{1,0:T(8,128)(2,1)S(1)} collective-permute-done((bf16[336,128]{1,0:T(8,128)(2,1)S(1)}, bf16[336,128]{1,0:T(8,128)(2,1)S(1)}, u32[]{:S(2)}, u32[]{:S(2)}) %collective-permute-start.42) | collective-permute-done | bytes 86048 | tf_op jit(solution)/shard_map/cond/branch_2_fun/ppermute | solution.py:331
  50.0 1.2 %collective-permute-done.43.refs_13_ = bf16[336,128]{1,0:T(8,128)(2,1)S(1)} collective-permute-done((bf16[336,128]{1,0:T(8,128)(2,1)S(1)}, bf16[336,128]{1,0:T(8,128)(2,1)S(1)}, u32[]{:S(2)}, u32[]{:S(2)}) %collective-permute-start.43) | collective-permute-done | bytes 86048 | tf_op jit(solution)/shard_map/cond/branch_2_fun/ppermute | solution.py:331
  51.2 2.0 %collective-permute-done.44.refs_14_ = bf16[336,128]{1,0:T(8,128)(2,1)S(1)} collective-permute-done((bf16[336,128]{1,0:T(8,128)(2,1)S(1)}, bf16[336,128]{1,0:T(8,128)(2,1)S(1)}, u32[]{:S(2)}, u32[]{:S(2)}) %collective-permute-start.44) | collective-permute-done | bytes 86048 | tf_op jit(solution)/shard_map/cond/branch_2_fun/ppermute | solution.py:331
  53.2 4.8 %gram.9 = f32[128,128]{1,0:T(8,128)S(1)} custom-call(s32[6]{0:T(128)S(1)} %get-tuple-element.93.scalar_ref.after_ref, bf16[336,128]{1,0:T(8,128)(2,1)S(1)} %collective-permute-done.30.after_ref.refs_0_, bf16[336,128]{1,0:T(8,128)(2,1)S(1)} %collective-permute-done.31.refs_1_, bf16[336,128]{1,0:T(8,128)(2,1)S(1)} %collective-permute-done.32.refs_2_, ...), custom_call_target="tpu_custom_call" | custom-call | tf_op jit(solution)/shard_map/cond/branch_2_fun/gram/pallas_call | solution.py:333
  58.0 0.0 copy-start.4
  58.0 0.6 %copy-done.4 = f32[128,128]{1,0:T(8,128)} copy-done((f32[128,128]{1,0:T(8,128)}, f32[128,128]{1,0:T(8,128)S(1)}, u32[]{:S(2)}) %copy-start.4) | copy-done | bytes 65560
  (17 shorter events, 0.0 us)
Async XLA Ops:
  0.0 5.0 %collective-permute-start.105 = (bf16[8,1152,128]{2,1,0:T(8,128)(2,1)}, bf16[8,1152,128]{2,1,0:T(8,128)(2,1)S(1)}, u32[]{:S(2)}, u32[]{:S(2)}) collective-permute-start(bf16[8,1152,128]{2,1,0:T(8,128)(2,1)} %in_ref.1), channel_id=1, source_target_pairs={{0,1},{1,0},{2,3},{3,2},{4,5},{5,4},{6,7},{7,6},{8,9},{9,8},{10,11... | collective-permute-start | bytes 7077896 | tf_op jit(solution)/shard_map/ppermute | solution.py:287
  0.5 1.7 %copy-start = (bf16[8,1152,128]{2,1,0:T(8,128)(2,1)S(1)}, bf16[8,1152,128]{2,1,0:T(8,128)(2,1)}, u32[]{:S(2)}) copy-start(bf16[8,1152,128]{2,1,0:T(8,128)(2,1)} %in_ref.1) | copy-start | bytes 7077892
  2.1 1.0 %copy-start.1 = (s32[2304]{0:T(1024)S(1)}, s32[2304]{0:T(1024)}, u32[]{:S(2)}) copy-start(s32[2304]{0:T(1024)} %cycle_in.1) | copy-start | bytes 27652
  2.1 1.0 %copy-start.2 = (s32[2304]{0:T(1024)S(1)}, s32[2304]{0:T(1024)}, u32[]{:S(2)}) copy-start(s32[2304]{0:T(1024)} %valid_in.1) | copy-start | bytes 27652
  2.1 1.0 %copy-start.3 = (s32[32]{0:T(128)S(1)}, s32[32]{0:T(128)}, u32[]{:S(2)}) copy-start(s32[32]{0:T(128)} %owner_in.1) | copy-start | bytes 388
  8.0 10.5 %collective-permute-start.30 = (bf16[336,128]{1,0:T(8,128)(2,1)S(1)}, bf16[336,128]{1,0:T(8,128)(2,1)S(1)}, u32[]{:S(2)}, u32[]{:S(2)}) collective-permute-start(bf16[336,128]{1,0:T(8,128)(2,1)S(1)} %get-tuple-element.96), channel_id=1, source_target_pairs={{0,30},{2,28},{4,26},{6,24},{8,22},{10,20},{12,18},{14,16},{16,14}... | collective-permute-start | bytes 258056 | tf_op jit(solution)/shard_map/cond/branch_2_fun/ppermute | solution.py:331
  14.7 18.1 %collective-permute-start.31 = (bf16[336,128]{1,0:T(8,128)(2,1)S(1)}, bf16[336,128]{1,0:T(8,128)(2,1)S(1)}, u32[]{:S(2)}, u32[]{:S(2)}) collective-permute-start(bf16[336,128]{1,0:T(8,128)(2,1)S(1)} %get-tuple-element.97), channel_id=1, source_target_pairs={{0,28},{2,30},{4,24},{6,26},{8,20},{10,22},{12,16},{14,18},{16,12}... | collective-permute-start | bytes 258056 | tf_op jit(solution)/shard_map/cond/branch_2_fun/ppermute | solution.py:331
  14.8 20.6 %collective-permute-start.32 = (bf16[336,128]{1,0:T(8,128)(2,1)S(1)}, bf16[336,128]{1,0:T(8,128)(2,1)S(1)}, u32[]{:S(2)}, u32[]{:S(2)}) collective-permute-start(bf16[336,128]{1,0:T(8,128)(2,1)S(1)} %get-tuple-element.98), channel_id=1, source_target_pairs={{0,26},{2,24},{4,30},{6,28},{8,18},{10,16},{12,22},{14,20},{16,10}... | collective-permute-start | bytes 258056 | tf_op jit(solution)/shard_map/cond/branch_2_fun/ppermute | solution.py:331
  24.1 12.5 %collective-permute-start.33 = (bf16[336,128]{1,0:T(8,128)(2,1)S(1)}, bf16[336,128]{1,0:T(8,128)(2,1)S(1)}, u32[]{:S(2)}, u32[]{:S(2)}) collective-permute-start(bf16[336,128]{1,0:T(8,128)(2,1)S(1)} %get-tuple-element.99), channel_id=1, source_target_pairs={{0,24},{2,26},{4,28},{6,30},{8,16},{10,18},{12,20},{14,22},{16,8},... | collective-permute-start | bytes 258056 | tf_op jit(solution)/shard_map/cond/branch_2_fun/ppermute | solution.py:331
  27.6 10.0 %collective-permute-start.34 = (bf16[336,128]{1,0:T(8,128)(2,1)S(1)}, bf16[336,128]{1,0:T(8,128)(2,1)S(1)}, u32[]{:S(2)}, u32[]{:S(2)}) collective-permute-start(bf16[336,128]{1,0:T(8,128)(2,1)S(1)} %get-tuple-element.100), channel_id=1, source_target_pairs={{0,14},{2,12},{4,10},{6,8},{8,6},{10,4},{12,2},{14,0},{16,30},{18,... | collective-permute-start | bytes 258056 | tf_op jit(solution)/shard_map/cond/branch_2_fun/ppermute | solution.py:331
  32.8 10.2 %collective-permute-start.35 = (bf16[336,128]{1,0:T(8,128)(2,1)S(1)}, bf16[336,128]{1,0:T(8,128)(2,1)S(1)}, u32[]{:S(2)}, u32[]{:S(2)}) collective-permute-start(bf16[336,128]{1,0:T(8,128)(2,1)S(1)} %get-tuple-element.101), channel_id=1, source_target_pairs={{0,22},{2,20},{4,18},{6,16},{8,30},{10,28},{12,26},{14,24},{16,6},... | collective-permute-start | bytes 258056 | tf_op jit(solution)/shard_map/cond/branch_2_fun/ppermute | solution.py:331
  32.8 10.2 %collective-permute-start.36 = (bf16[336,128]{1,0:T(8,128)(2,1)S(1)}, bf16[336,128]{1,0:T(8,128)(2,1)S(1)}, u32[]{:S(2)}, u32[]{:S(2)}) collective-permute-start(bf16[336,128]{1,0:T(8,128)(2,1)S(1)} %get-tuple-element.102), channel_id=1, source_target_pairs={{0,12},{2,14},{4,8},{6,10},{8,4},{10,6},{12,0},{14,2},{16,28},{18,... | collective-permute-start | bytes 258056 | tf_op jit(solution)/shard_map/cond/branch_2_fun/ppermute | solution.py:331
  35.5 9.1 %collective-permute-start.37 = (bf16[336,128]{1,0:T(8,128)(2,1)S(1)}, bf16[336,128]{1,0:T(8,128)(2,1)S(1)}, u32[]{:S(2)}, u32[]{:S(2)}) collective-permute-start(bf16[336,128]{1,0:T(8,128)(2,1)S(1)} %get-tuple-element.103), channel_id=1, source_target_pairs={{0,20},{2,22},{4,16},{6,18},{8,28},{10,30},{12,24},{14,26},{16,4},... | collective-permute-start | bytes 258056 | tf_op jit(solution)/shard_map/cond/branch_2_fun/ppermute | solution.py:331
  36.6 8.3 %collective-permute-start.38 = (bf16[336,128]{1,0:T(8,128)(2,1)S(1)}, bf16[336,128]{1,0:T(8,128)(2,1)S(1)}, u32[]{:S(2)}, u32[]{:S(2)}) collective-permute-start(bf16[336,128]{1,0:T(8,128)(2,1)S(1)} %get-tuple-element.104), channel_id=1, source_target_pairs={{0,10},{2,8},{4,14},{6,12},{8,2},{10,0},{12,6},{14,4},{16,26},{18,... | collective-permute-start | bytes 258056 | tf_op jit(solution)/shard_map/cond/branch_2_fun/ppermute | solution.py:331
  37.6 11.1 %collective-permute-start.39 = (bf16[336,128]{1,0:T(8,128)(2,1)S(1)}, bf16[336,128]{1,0:T(8,128)(2,1)S(1)}, u32[]{:S(2)}, u32[]{:S(2)}) collective-permute-start(bf16[336,128]{1,0:T(8,128)(2,1)S(1)} %get-tuple-element.105), channel_id=1, source_target_pairs={{0,18},{2,16},{4,22},{6,20},{8,26},{10,24},{12,30},{14,28},{16,2},... | collective-permute-start | bytes 258056 | tf_op jit(solution)/shard_map/cond/branch_2_fun/ppermute | solution.py:331
  43.0 5.8 %collective-permute-start.40 = (bf16[336,128]{1,0:T(8,128)(2,1)S(1)}, bf16[336,128]{1,0:T(8,128)(2,1)S(1)}, u32[]{:S(2)}, u32[]{:S(2)}) collective-permute-start(bf16[336,128]{1,0:T(8,128)(2,1)S(1)} %get-tuple-element.106), channel_id=1, source_target_pairs={{0,8},{2,10},{4,12},{6,14},{8,0},{10,2},{12,4},{14,6},{16,24},{18,... | collective-permute-start | bytes 258056 | tf_op jit(solution)/shard_map/cond/branch_2_fun/ppermute | solution.py:331
  43.0 5.8 %collective-permute-start.41 = (bf16[336,128]{1,0:T(8,128)(2,1)S(1)}, bf16[336,128]{1,0:T(8,128)(2,1)S(1)}, u32[]{:S(2)}, u32[]{:S(2)}) collective-permute-start(bf16[336,128]{1,0:T(8,128)(2,1)S(1)} %get-tuple-element.107), channel_id=1, source_target_pairs={{0,16},{2,18},{4,20},{6,22},{8,24},{10,26},{12,28},{14,30},{16,0},... | collective-permute-start | bytes 258056 | tf_op jit(solution)/shard_map/cond/branch_2_fun/ppermute | solution.py:331
  44.6 5.4 %collective-permute-start.42 = (bf16[336,128]{1,0:T(8,128)(2,1)S(1)}, bf16[336,128]{1,0:T(8,128)(2,1)S(1)}, u32[]{:S(2)}, u32[]{:S(2)}) collective-permute-start(bf16[336,128]{1,0:T(8,128)(2,1)S(1)} %get-tuple-element.108), channel_id=1, source_target_pairs={{0,6},{2,4},{4,2},{6,0},{8,14},{10,12},{12,10},{14,8},{16,22},{18,... | collective-permute-start | bytes 258056 | tf_op jit(solution)/shard_map/cond/branch_2_fun/ppermute | solution.py:331
  44.9 6.3 %collective-permute-start.43 = (bf16[336,128]{1,0:T(8,128)(2,1)S(1)}, bf16[336,128]{1,0:T(8,128)(2,1)S(1)}, u32[]{:S(2)}, u32[]{:S(2)}) collective-permute-start(bf16[336,128]{1,0:T(8,128)(2,1)S(1)} %get-tuple-element.109), channel_id=1, source_target_pairs={{0,4},{2,6},{4,0},{6,2},{8,12},{10,14},{12,8},{14,10},{16,20},{18,... | collective-permute-start | bytes 258056 | tf_op jit(solution)/shard_map/cond/branch_2_fun/ppermute | solution.py:331
  48.7 4.5 %collective-permute-start.44 = (bf16[336,128]{1,0:T(8,128)(2,1)S(1)}, bf16[336,128]{1,0:T(8,128)(2,1)S(1)}, u32[]{:S(2)}, u32[]{:S(2)}) collective-permute-start(bf16[336,128]{1,0:T(8,128)(2,1)S(1)} %get-tuple-element.110), channel_id=1, source_target_pairs={{0,2},{2,0},{4,6},{6,4},{8,10},{10,8},{12,14},{14,12},{16,18},{18,... | collective-permute-start | bytes 258056 | tf_op jit(solution)/shard_map/cond/branch_2_fun/ppermute | solution.py:331
  58.0 0.6 %copy-start.4 = (f32[128,128]{1,0:T(8,128)}, f32[128,128]{1,0:T(8,128)S(1)}, u32[]{:S(2)}) copy-start(f32[128,128]{1,0:T(8,128)S(1)} %get-tuple-element.419) | copy-start | bytes 196612

commit v3 on v2

--- a/solution.py
+++ b/solution.py
@@ -8,26 +8,20 @@
 from jax.sharding import PartitionSpec as P
 
 LANE = 128
-UNROLL = 32
-FIRST = 3
+UNROLL = 64
+QUAD = 4
 STEP = 128
 VMEM_LIMIT = 24 * 1024 * 1024
-LADDER = (32, 40, 42, 44, 46, 56, 144)
+LADDER = (32, 38, 40, 42, 44, 46, 56, 144)
 NT = (((1,), (1,)), ((), ()))
 
 
 def exchange_order(count):
     side = count // 2
-    across = [count - 1 - i for i in range(side)]
-    beside = [side - 1 - i for i in range(side)]
-    order = across[:FIRST]
-    for far, near in zip(across[FIRST:], beside):
-        order += [far, near]
-    return order + [apart for apart in beside if apart not in order]
-
-
-def group_ends(count):
-    return (0, FIRST, count)
+    order = []
+    for i in range(side):
+        order += [count - 1 - i, side - 1 - i]
+    return order
 
 
 def plan_kernel(
@@ -138,9 +132,7 @@
     scalar_ref[0] = rung
     scalar_ref[1] = tm_index
     scalar_ref[2] = jnp.sum(jnp.where(slot == own_slot, pixels, 0.0)[:, :1]).astype(jnp.int32)
-    for group, end in enumerate(group_ends(slots // 2)):
-        ahead = jnp.where(turn < end, count * mine, 0.0)
-        scalar_ref[3 + group] = jnp.sum(ahead[:, :1]).astype(jnp.int32)
+    scalar_ref[3] = total
 
 
 def widen_kernel(part, in_ref, *rest):
@@ -156,15 +148,14 @@
     lax.fori_loop(0, half // STEP, widen, 0)
 
 
-def pack_kernel(group, first, word_ref, scalar_ref, pool_ref, after_ref, *rest):
+def pack_kernel(word_ref, scalar_ref, pool_ref, *rest):
     out_refs, stage = rest[:-1], rest[-1]
     depth = out_refs[0].shape[0]
     frames = pool_ref.shape[1]
     lane = lax.broadcasted_iota(jnp.int32, (frames, LANE), 1)
-    begin, end = scalar_ref[3 + group], scalar_ref[4 + group]
 
     def place(i, held):
-        at = begin + i * UNROLL
+        at = i * UNROLL
         turned = []
         for j in range(UNROLL):
             word = word_ref[at + j]
@@ -179,11 +170,11 @@
         return held
 
     held = jnp.zeros((frames, LANE), jnp.float32)
-    lax.fori_loop(0, (end - begin + UNROLL - 1) // UNROLL, place, held)
+    lax.fori_loop(0, (scalar_ref[3] + UNROLL - 1) // UNROLL, place, held)
 
     step = depth if depth <= 512 else LANE
     for d, out_ref in enumerate(out_refs):
-        base = (first + d) * depth
+        base = d * depth
 
         def narrow(i, _, out_ref=out_ref, base=base):
             row = pl.multiple_of(i * step, step)
@@ -197,54 +188,45 @@
 
 
 def gram_kernel(scalar_ref, *refs):
-    x_refs, (out_ref, turn, scales, totals) = refs[:-4], refs[-4:]
+    x_refs, (out_ref, turn, grams, totals) = refs[:-4], refs[-4:]
     sources = len(x_refs)
     frames = out_ref.shape[0]
     local = frames // sources
-    size = x_refs[0].shape[0] // local
+    last = x_refs[0].shape[0] // (2 * local) - 1
     tm_index, pixels = scalar_ref[1], scalar_ref[2]
-    pairs = (pixels + 2 * LANE - 1) // (2 * LANE)
     lane = lax.broadcasted_iota(jnp.int32, (1, LANE), 1)
-    row = lax.broadcasted_iota(jnp.int32, (8, LANE), 0)
-
-    def scale(i, _):
-        begin = jnp.minimum(8 * i, size - 8)
-        part = pl.ds(pl.multiple_of(begin * local, 2 * local), 8 * local)
-        each = x_refs[0][part, :].astype(jnp.float32)
-        for ref in x_refs[1:]:
-            each = each + ref[part, :].astype(jnp.float32)
-        mean = jnp.sum(each.reshape(8, local, LANE), axis=1) / frames
-        used = lane + (begin + row) * LANE < pixels
-        scales[pl.ds(begin, 8), :] = jnp.where(used, 1.0 / jnp.where(used, mean, 1.0), 0.0)
-        return 0
-
-    lax.fori_loop(0, (pairs + 3) // 4, scale, 0)
+    grams[...] = jnp.zeros(grams.shape, jnp.float32)
     totals[...] = jnp.zeros(totals.shape, jnp.float32)
 
-    def pair(j, gram):
-        rows = pl.ds(pl.multiple_of(j * 2 * local, 2 * local), 2 * local)
-        both = [ref[rows, :].astype(jnp.float32) for ref in x_refs]
+    def several(step, _):
         exact, high, low = [], [], []
         total = totals[...]
-        for i in range(2):
-            used = lane + (2 * j + i) * LANE < pixels
-            x = jnp.concatenate([part[i * local : (i + 1) * local] for part in both], axis=0)
-            x = jnp.where(used, x, 0.0)
-            factor = scales[pl.ds(2 * j + i, 1), :]
-            normed = x * factor
-            total = total + normed
-            y = normed * factor
-            top = y.astype(jnp.bfloat16)
-            exact.append(x.astype(jnp.bfloat16))
-            high.append(top)
-            low.append((y - top.astype(jnp.float32)).astype(jnp.bfloat16))
+        for k in range(QUAD):
+            j = QUAD * step + k
+            rows = pl.ds(pl.multiple_of(jnp.minimum(j, last) * 2 * local, 2 * local), 2 * local)
+            both = [ref[rows, :].astype(jnp.float32) for ref in x_refs]
+            for i in range(2):
+                used = lane + (2 * j + i) * LANE < pixels
+                x = jnp.concatenate([part[i * local : (i + 1) * local] for part in both], axis=0)
+                x = jnp.where(used, x, 0.0)
+                mean = jnp.where(used, jnp.sum(x, axis=0, keepdims=True) / frames, 1.0)
+                scale = 1.0 / mean
+                total = total + x * scale
+                y = x * (scale * scale)
+                top = y.astype(jnp.bfloat16)
+                exact.append(x.astype(jnp.bfloat16))
+                high.append(top)
+                low.append((y - top.astype(jnp.float32)).astype(jnp.bfloat16))
         totals[...] = total
         left = jnp.concatenate(exact, axis=1)
         right = jnp.concatenate(
             [jnp.concatenate(high, axis=1), jnp.concatenate(low, axis=1)], axis=0
         )
-        return gram + lax.dot_general(left, right, NT, preferred_element_type=jnp.float32)
-
+        grams[...] += lax.dot_general(left, right, NT, preferred_element_type=jnp.float32)
+        return 0
+
+    pairs = (pixels + 2 * LANE - 1) // (2 * LANE)
+    lax.fori_loop(0, (pairs + QUAD - 1) // QUAD, several, 0)
     order = exchange_order(sources)
 
     def in_order(value):
@@ -253,8 +235,7 @@
             turn[pl.ds(at, local), :] = value[j * local : (j + 1) * local]
         return turn[...]
 
-    gram = lax.fori_loop(0, pairs, pair, jnp.zeros((frames, 2 * frames), jnp.float32))
-    gram = in_order(gram[:, :frames] + gram[:, frames:])
+    gram = in_order(grams[:, :frames] + grams[:, frames:])
     gram = in_order(gram.T)
     total = in_order(totals[...])
     first = jnp.sum(total, axis=1, keepdims=True)
@@ -266,7 +247,6 @@
     tm_count = lax.axis_size("tm")
     local_frames, half, _ = frames.shape
     frame_count = tm_count * local_frames
-    ends = group_ends(tm_count)
     order = exchange_order(tm_count)
     list_rows = -(-(block_cycle.shape[0] + UNROLL) // (8 * LANE)) * 8
     vmem = pl.BlockSpec(memory_space=pltpu.VMEM)
@@ -289,7 +269,7 @@
         plan_kernel,
         out_shape=(
             jax.ShapeDtypeStruct((list_rows, LANE), jnp.int32),
-            jax.ShapeDtypeStruct((3 + len(ends),), jnp.int32),
+            jax.ShapeDtypeStruct((4,), jnp.int32),
         ),
         in_specs=[pl.BlockSpec(memory_space=pltpu.HBM)] * 3,
         out_specs=(vmem, smem),
@@ -308,28 +288,21 @@
         depth = size * local_frames
 
         def run(words, scalars, pool):
+            send = pl.pallas_call(
+                pack_kernel,
+                out_shape=(jax.ShapeDtypeStruct((depth, LANE), jnp.bfloat16),) * tm_count,
+                in_specs=[smem, smem, vmem],
+                out_specs=(vmem,) * tm_count,
+                scratch_shapes=[
+                    pltpu.VMEM(((tm_count * size + 2) * local_frames, LANE), jnp.float32)
+                ],
+                compiler_params=params,
+                name="pack",
+            )(words, scalars, pool)
             got = []
-            after = scalars
-            for group, (first, end) in enumerate(zip(ends[:-1], ends[1:])):
-                members = end - first
-                send = pl.pallas_call(
-                    functools.partial(pack_kernel, group, first),
-                    out_shape=(jax.ShapeDtypeStruct((depth, LANE), jnp.bfloat16),) * members,
-                    in_specs=[smem, smem, vmem, pl.BlockSpec(memory_space=pl.ANY)],
-                    out_specs=(vmem,) * members,
-                    scratch_shapes=[
-                        pltpu.VMEM(((tm_count * size + 2) * local_frames, LANE), jnp.float32)
-                    ],
-                    compiler_params=params,
-                    cost_estimate=pl.CostEstimate(
-                        flops=2_000_000, bytes_accessed=16_000_000, transcendentals=0
-                    ),
-                    name="pack",
-                )(words, scalars, pool, after)
-                for part, apart in zip(send, order[first:end]):
-                    pairs = [(i, i ^ apart) for i in range(tm_count)]
-                    got.append(lax.ppermute(part, "tm", pairs) if apart else part)
-                after = got[first]
+            for part, apart in zip(send, order):
+                pairs = [(i, i ^ apart) for i in range(tm_count)]
+                got.append(lax.ppermute(part, "tm", pairs) if apart else part)
             return pl.pallas_call(
                 gram_kernel,
                 out_shape=jax.ShapeDtypeStruct((frame_count, frame_count), jnp.float32),
@@ -337,7 +310,7 @@
                 out_specs=vmem,
                 scratch_shapes=[
                     pltpu.VMEM((frame_count, LANE), jnp.float32),
-                    pltpu.VMEM((size, LANE), jnp.float32),
+                    pltpu.VMEM((frame_count, 2 * frame_count), jnp.float32),
                     pltpu.VMEM((frame_count, LANE), jnp.float32),
                 ],
                 compiler_params=params,

time: 59 us -> 54.8 us (0.929); the launches traced: 58.7 us -> 55.5 us
  starting transfers between devices: 31.1 us -> 25.9 us
  waiting for transfers between devices: 8.89 us -> 13 us
  Pallas kernels: 16.2 us -> 13.8 us
    ppermute x15, starting transfers between devices: 30.6 us -> 25.5 us  [run(): got.append(lax.ppermute(part, 'tm', pairs) if apart else part)]
    ppermute x15, waiting for transfers between devices: 8.89 us -> 13 us  [run(): got.append(lax.ppermute(part, 'tm', pairs) if apart else part)]
    pallas_call x1, Pallas kernels: 4.79 us -> 3.23 us  [run(): pl.pallas_call(gram_kernel, out_shape=jax.ShapeDtypeStruct((frame_count,...]
    pallas_call x2 -> x1, Pallas kernels: 7.62 us -> 6.76 us  [run(): pl.pallas_call(pack_kernel, out_shape=(jax.ShapeDtypeStruct((depth, LANE)...]
  transfers between devices with their start and end apart: 16 -> 16, of which waited for: 5 -> 6; matrix products, arithmetic and copies ran while one was open for 0% -> 0% of each run, Pallas kernels for 15% -> 5%
where the time goes in v3:
time: 54.8 us; the launch traced here: 55.5 us
  starting transfers between devices  25.9 us (47%)
  Pallas kernels  13.8 us (25%)
  waiting for transfers between devices  13 us (24%)
  local copies, waits for them, and re-layouts  2.3 us (4%)
    ppermute x15, starting transfers between devices, run(): got.append(lax.ppermute(part, 'tm', pairs) if apart else part)  25.5 us
    ppermute x15, waiting for transfers between devices, run(): got.append(lax.ppermute(part, 'tm', pairs) if apart else part)  13 us
    pallas_call x1, Pallas kernels, run(): pl.pallas_call(pack_kernel, out_shape=(jax.ShapeDtypeStruct((depth, LANE)...  6.76 us
    pallas_call x1, Pallas kernels, run(): pl.pallas_call(gram_kernel, out_shape=jax.ShapeDtypeStruct((frame_count,...  3.23 us
    unnamed x10, local copies, waits for them, and re-layouts  2.3 us
    pallas_call x2, Pallas kernels, widen(): pl.pallas_call(functools.partial(widen_kernel, part), out_shape=jax.Shape...  1.95 us
    pallas_call x1, Pallas kernels, on_device_routed(): pl.pallas_call(plan_kernel, out_shape=(jax.ShapeDtypeStruct((list_rows, L...  1.84 us
  transfers between devices with their start and end apart: 16, of which 6 were waited for; matrix products, arithmetic and copies ran while one was open for 0% of the time, Pallas kernels for 5%

profile of v3, /device:TPU:0, one launch (start us, length us, event | category | flops | bytes accessed | tf_op | source)
XLA Modules:
  0.0 55.5 jit_solution(16932915659558122545)
XLA Ops:
  0.0 0.5 collective-permute-start.120
  0.5 1.7 %copy-done = bf16[8,1152,128]{2,1,0:T(8,128)(2,1)S(1)} copy-done((bf16[8,1152,128]{2,1,0:T(8,128)(2,1)S(1)}, bf16[8,1152,128]{2,1,0:T(8,128)(2,1)}, u32[]{:S(2)}) %copy-start) | copy-done | bytes 2359320
  2.1 1.0 %widen.2.rest_0_ = f32[2304,8,128]{2,1,0:T(8,128)S(1)} custom-call(bf16[8,1152,128]{2,1,0:T(8,128)(2,1)S(1)} %copy-done), custom_call_target="tpu_custom_call" | custom-call | tf_op jit(solution)/shard_map/widen/pallas_call | solution.py:257
  3.1 1.8 %plan.1 = (s32[24,128]{1,0:T(8,128)S(1)}, s32[4]{0:T(128)S(1)}) custom-call(s32[32]{0:T(128)S(1)} %copy-done.3, s32[2304]{0:T(1024)S(1)} %copy-done.1, s32[2304]{0:T(1024)S(1)} %copy-done.2), custom_call_target="tpu_custom_call" | custom-call | tf_op jit(solution)/shard_map/plan/pallas_call | solution.py:268
  5.0 0.0 collective-permute-done.120.in_ref
  5.0 1.0 %widen.3 = f32[2304,8,128]{2,1,0:T(8,128)S(1)} custom-call(bf16[8,1152,128]{2,1,0:T(8,128)(2,1)S(1)} %collective-permute-done.120.in_ref, f32[2304,8,128]{2,1,0:T(8,128)S(1)} %widen.2.rest_0_), custom_call_target="tpu_custom_call", output_to_operand_aliasing={{}: (1, {})} | custom-call | tf_op jit(solution)/shard_map/widen/pallas_call | solution.py:257
  6.0 48.9 %conditional.1 = (f32[128,128]{1,0:T(8,128)S(1)}) conditional(s32[]{:T(128)} %bitcast.8, (s32[24,128]{1,0:T(8,128)S(1)}, s32[4]{0:T(128)S(1)}, f32[2304,8,128]{2,1,0:T(8,128)S(1)}) %tuple.29, (s32[24,128]{1,0:T(8,128)S(1)}, s32[4]{0:T(128)S(1)}, f32[2304,8,128]{2,1,0:T(8,128)S(1)}) %tuple.29, ...), branch_computations={%region_0.0_spmd, %region_1.0_spmd, %region_2.0_spmd, %region_3.0_... | conditional | bytes 17695328 | solution.py:322
  6.0 6.8 %pack.12 = (bf16[352,128]{1,0:T(8,128)(2,1)S(1)}, bf16[352,128]{1,0:T(8,128)(2,1)S(1)}, bf16[352,128]{1,0:T(8,128)(2,1)S(1)}, bf16[352,128]{1,0:T(8,128)(2,1)S(1...) custom-call(s32[3072]{0:T(1024)S(1)} %bitcast.14, ...), custom_call_target="tpu_custom_call" | custom-call | tf_op jit(solution)/shard_map/cond/branch_4_fun/pack/pallas_call | solution.py:291
  12.8 6.7 %collective-permute-start.60 = (bf16[352,128]{1,0:T(8,128)(2,1)S(1)}, bf16[352,128]{1,0:T(8,128)(2,1)S(1)}, u32[]{:S(2)}, u32[]{:S(2)}) collective-permute-start(bf16[352,128]{1,0:T(8,128)(2,1)S(1)} %get-tuple-element.141), channel_id=1, source_target_pairs={{0,30},{2,28},{4,26},{6,24},{8,22},{10,20},{12,18},{14,16},{16,14}... | collective-permute-start | bytes 270344 | tf_op jit(solution)/shard_map/cond/branch_4_fun/ppermute | solution.py:305
  19.5 1.8 %collective-permute-start.62 = (bf16[352,128]{1,0:T(8,128)(2,1)S(1)}, bf16[352,128]{1,0:T(8,128)(2,1)S(1)}, u32[]{:S(2)}, u32[]{:S(2)}) collective-permute-start(bf16[352,128]{1,0:T(8,128)(2,1)S(1)} %get-tuple-element.143), channel_id=1, source_target_pairs={{0,28},{2,30},{4,24},{6,26},{8,20},{10,22},{12,16},{14,18},{16,12}... | collective-permute-start | bytes 270344 | tf_op jit(solution)/shard_map/cond/branch_4_fun/ppermute | solution.py:305
  21.3 1.1 %collective-permute-start.63 = (bf16[352,128]{1,0:T(8,128)(2,1)S(1)}, bf16[352,128]{1,0:T(8,128)(2,1)S(1)}, u32[]{:S(2)}, u32[]{:S(2)}) collective-permute-start(bf16[352,128]{1,0:T(8,128)(2,1)S(1)} %get-tuple-element.144), channel_id=1, source_target_pairs={{0,12},{2,14},{4,8},{6,10},{8,4},{10,6},{12,0},{14,2},{16,28},{18,... | collective-permute-start | bytes 270344 | tf_op jit(solution)/shard_map/cond/branch_4_fun/ppermute | solution.py:305
  22.4 3.8 %collective-permute-start.64 = (bf16[352,128]{1,0:T(8,128)(2,1)S(1)}, bf16[352,128]{1,0:T(8,128)(2,1)S(1)}, u32[]{:S(2)}, u32[]{:S(2)}) collective-permute-start(bf16[352,128]{1,0:T(8,128)(2,1)S(1)} %get-tuple-element.145), channel_id=1, source_target_pairs={{0,26},{2,24},{4,30},{6,28},{8,18},{10,16},{12,22},{14,20},{16,10}... | collective-permute-start | bytes 270344 | tf_op jit(solution)/shard_map/cond/branch_4_fun/ppermute | solution.py:305
  26.2 0.1 collective-permute-start.65
  26.3 3.7 %collective-permute-done.61.refs_1_ = bf16[352,128]{1,0:T(8,128)(2,1)S(1)} collective-permute-done((bf16[352,128]{1,0:T(8,128)(2,1)S(1)}, bf16[352,128]{1,0:T(8,128)(2,1)S(1)}, u32[]{:S(2)}, u32[]{:S(2)}) %collective-permute-start.61) | collective-permute-done | bytes 90144 | tf_op jit(solution)/shard_map/cond/branch_4_fun/ppermute | solution.py:305
  29.9 0.2 collective-permute-start.66
  30.1 0.3 collective-permute-start.67
  30.4 1.8 %collective-permute-done.63.refs_3_ = bf16[352,128]{1,0:T(8,128)(2,1)S(1)} collective-permute-done((bf16[352,128]{1,0:T(8,128)(2,1)S(1)}, bf16[352,128]{1,0:T(8,128)(2,1)S(1)}, u32[]{:S(2)}, u32[]{:S(2)}) %collective-permute-start.63) | collective-permute-done | bytes 90144 | tf_op jit(solution)/shard_map/cond/branch_4_fun/ppermute | solution.py:305
  32.3 1.0 %collective-permute-start.68 = (bf16[352,128]{1,0:T(8,128)(2,1)S(1)}, bf16[352,128]{1,0:T(8,128)(2,1)S(1)}, u32[]{:S(2)}, u32[]{:S(2)}) collective-permute-start(bf16[352,128]{1,0:T(8,128)(2,1)S(1)} %get-tuple-element.149), channel_id=1, source_target_pairs={{0,22},{2,20},{4,18},{6,16},{8,30},{10,28},{12,26},{14,24},{16,6},... | collective-permute-start | bytes 270344 | tf_op jit(solution)/shard_map/cond/branch_4_fun/ppermute | solution.py:305
  33.2 3.5 %collective-permute-start.69 = (bf16[352,128]{1,0:T(8,128)(2,1)S(1)}, bf16[352,128]{1,0:T(8,128)(2,1)S(1)}, u32[]{:S(2)}, u32[]{:S(2)}) collective-permute-start(bf16[352,128]{1,0:T(8,128)(2,1)S(1)} %get-tuple-element.150), channel_id=1, source_target_pairs={{0,6},{2,4},{4,2},{6,0},{8,14},{10,12},{12,10},{14,8},{16,22},{18,... | collective-permute-start | bytes 270344 | tf_op jit(solution)/shard_map/cond/branch_4_fun/ppermute | solution.py:305
  36.7 1.2 %collective-permute-start.70 = (bf16[352,128]{1,0:T(8,128)(2,1)S(1)}, bf16[352,128]{1,0:T(8,128)(2,1)S(1)}, u32[]{:S(2)}, u32[]{:S(2)}) collective-permute-start(bf16[352,128]{1,0:T(8,128)(2,1)S(1)} %get-tuple-element.151), channel_id=1, source_target_pairs={{0,20},{2,22},{4,16},{6,18},{8,28},{10,30},{12,24},{14,26},{16,4},... | collective-permute-start | bytes 270344 | tf_op jit(solution)/shard_map/cond/branch_4_fun/ppermute | solution.py:305
  37.9 1.1 %collective-permute-start.71 = (bf16[352,128]{1,0:T(8,128)(2,1)S(1)}, bf16[352,128]{1,0:T(8,128)(2,1)S(1)}, u32[]{:S(2)}, u32[]{:S(2)}) collective-permute-start(bf16[352,128]{1,0:T(8,128)(2,1)S(1)} %get-tuple-element.152), channel_id=1, source_target_pairs={{0,4},{2,6},{4,0},{6,2},{8,12},{10,14},{12,8},{14,10},{16,20},{18,... | collective-permute-start | bytes 270344 | tf_op jit(solution)/shard_map/cond/branch_4_fun/ppermute | solution.py:305
  39.0 1.4 %collective-permute-start.72 = (bf16[352,128]{1,0:T(8,128)(2,1)S(1)}, bf16[352,128]{1,0:T(8,128)(2,1)S(1)}, u32[]{:S(2)}, u32[]{:S(2)}) collective-permute-start(bf16[352,128]{1,0:T(8,128)(2,1)S(1)} %get-tuple-element.153), channel_id=1, source_target_pairs={{0,18},{2,16},{4,22},{6,20},{8,26},{10,24},{12,30},{14,28},{16,2},... | collective-permute-start | bytes 270344 | tf_op jit(solution)/shard_map/cond/branch_4_fun/ppermute | solution.py:305
  40.5 1.7 %collective-permute-done.68.refs_8_ = bf16[352,128]{1,0:T(8,128)(2,1)S(1)} collective-permute-done((bf16[352,128]{1,0:T(8,128)(2,1)S(1)}, bf16[352,128]{1,0:T(8,128)(2,1)S(1)}, u32[]{:S(2)}, u32[]{:S(2)}) %collective-permute-start.68) | collective-permute-done | bytes 90144 | tf_op jit(solution)/shard_map/cond/branch_4_fun/ppermute | solution.py:305
  42.2 0.9 %collective-permute-start.73 = (bf16[352,128]{1,0:T(8,128)(2,1)S(1)}, bf16[352,128]{1,0:T(8,128)(2,1)S(1)}, u32[]{:S(2)}, u32[]{:S(2)}) collective-permute-start(bf16[352,128]{1,0:T(8,128)(2,1)S(1)} %get-tuple-element.154), channel_id=1, source_target_pairs={{0,2},{2,0},{4,6},{6,4},{8,10},{10,8},{12,14},{14,12},{16,18},{18,... | collective-permute-start | bytes 270344 | tf_op jit(solution)/shard_map/cond/branch_4_fun/ppermute | solution.py:305
  43.1 0.0 collective-permute-done.69.refs_9_
  43.2 2.4 %collective-permute-start.74 = (bf16[352,128]{1,0:T(8,128)(2,1)S(1)}, bf16[352,128]{1,0:T(8,128)(2,1)S(1)}, u32[]{:S(2)}, u32[]{:S(2)}) collective-permute-start(bf16[352,128]{1,0:T(8,128)(2,1)S(1)} %get-tuple-element.155), channel_id=1, source_target_pairs={{0,16},{2,18},{4,20},{6,22},{8,24},{10,26},{12,28},{14,30},{16,0},... | collective-permute-start | bytes 270344 | tf_op jit(solution)/shard_map/cond/branch_4_fun/ppermute | solution.py:305
  45.5 0.8 %collective-permute-done.70.refs_10_ = bf16[352,128]{1,0:T(8,128)(2,1)S(1)} collective-permute-done((bf16[352,128]{1,0:T(8,128)(2,1)S(1)}, bf16[352,128]{1,0:T(8,128)(2,1)S(1)}, u32[]{:S(2)}, u32[]{:S(2)}) %collective-permute-start.70) | collective-permute-done | bytes 90144 | tf_op jit(solution)/shard_map/cond/branch_4_fun/ppermute | solution.py:305
  46.4 4.0 %collective-permute-done.72.refs_12_ = bf16[352,128]{1,0:T(8,128)(2,1)S(1)} collective-permute-done((bf16[352,128]{1,0:T(8,128)(2,1)S(1)}, bf16[352,128]{1,0:T(8,128)(2,1)S(1)}, u32[]{:S(2)}, u32[]{:S(2)}) %collective-permute-start.72) | collective-permute-done | bytes 90144 | tf_op jit(solution)/shard_map/cond/branch_4_fun/ppermute | solution.py:305
  50.4 0.9 %collective-permute-done.74.refs_14_ = bf16[352,128]{1,0:T(8,128)(2,1)S(1)} collective-permute-done((bf16[352,128]{1,0:T(8,128)(2,1)S(1)}, bf16[352,128]{1,0:T(8,128)(2,1)S(1)}, u32[]{:S(2)}, u32[]{:S(2)}) %collective-permute-start.74) | collective-permute-done | bytes 90144 | tf_op jit(solution)/shard_map/cond/branch_4_fun/ppermute | solution.py:305
  51.3 3.2 %gram.12 = f32[128,128]{1,0:T(8,128)S(1)} custom-call(s32[4]{0:T(128)S(1)} %get-tuple-element.138.scalar_ref, bf16[352,128]{1,0:T(8,128)(2,1)S(1)} %collective-permute-done.60.refs_0_, bf16[352,128]{1,0:T(8,128)(2,1)S(1)} %collective-permute-done.61.refs_1_, bf16[352,128]{1,0:T(8,128)(2,1)S(1)} %collective-permute-done.62.refs_2_, ...), custom_call_target="tpu_custom_call" | custom-call | tf_op jit(solution)/shard_map/cond/branch_4_fun/gram/pallas_call | solution.py:306
  54.9 0.0 copy-start.4
  54.9 0.6 %copy-done.4 = f32[128,128]{1,0:T(8,128)} copy-done((f32[128,128]{1,0:T(8,128)}, f32[128,128]{1,0:T(8,128)S(1)}, u32[]{:S(2)}) %copy-start.4) | copy-done | bytes 65560
  (16 shorter events, 0.0 us)
Async XLA Ops:
  0.0 5.0 %collective-permute-start.120 = (bf16[8,1152,128]{2,1,0:T(8,128)(2,1)}, bf16[8,1152,128]{2,1,0:T(8,128)(2,1)S(1)}, u32[]{:S(2)}, u32[]{:S(2)}) collective-permute-start(bf16[8,1152,128]{2,1,0:T(8,128)(2,1)} %in_ref.1), channel_id=1, source_target_pairs={{0,1},{1,0},{2,3},{3,2},{4,5},{5,4},{6,7},{7,6},{8,9},{9,8},{10,11... | collective-permute-start | bytes 7077896 | tf_op jit(solution)/shard_map/ppermute | solution.py:267
  0.5 1.7 %copy-start = (bf16[8,1152,128]{2,1,0:T(8,128)(2,1)S(1)}, bf16[8,1152,128]{2,1,0:T(8,128)(2,1)}, u32[]{:S(2)}) copy-start(bf16[8,1152,128]{2,1,0:T(8,128)(2,1)} %in_ref.1) | copy-start | bytes 7077892
  2.1 1.0 %copy-start.1 = (s32[2304]{0:T(1024)S(1)}, s32[2304]{0:T(1024)}, u32[]{:S(2)}) copy-start(s32[2304]{0:T(1024)} %cycle_in.1) | copy-start | bytes 27652
  2.1 1.0 %copy-start.2 = (s32[2304]{0:T(1024)S(1)}, s32[2304]{0:T(1024)}, u32[]{:S(2)}) copy-start(s32[2304]{0:T(1024)} %valid_in.1) | copy-start | bytes 27652
  2.1 1.0 %copy-start.3 = (s32[32]{0:T(128)S(1)}, s32[32]{0:T(128)}, u32[]{:S(2)}) copy-start(s32[32]{0:T(128)} %owner_in.1) | copy-start | bytes 388
  12.8 13.4 %collective-permute-start.60 = (bf16[352,128]{1,0:T(8,128)(2,1)S(1)}, bf16[352,128]{1,0:T(8,128)(2,1)S(1)}, u32[]{:S(2)}, u32[]{:S(2)}) collective-permute-start(bf16[352,128]{1,0:T(8,128)(2,1)S(1)} %get-tuple-element.141), channel_id=1, source_target_pairs={{0,30},{2,28},{4,26},{6,24},{8,22},{10,20},{12,18},{14,16},{16,14}... | collective-permute-start | bytes 270344 | tf_op jit(solution)/shard_map/cond/branch_4_fun/ppermute | solution.py:305
  19.5 10.4 %collective-permute-start.61 = (bf16[352,128]{1,0:T(8,128)(2,1)S(1)}, bf16[352,128]{1,0:T(8,128)(2,1)S(1)}, u32[]{:S(2)}, u32[]{:S(2)}) collective-permute-start(bf16[352,128]{1,0:T(8,128)(2,1)S(1)} %get-tuple-element.142), channel_id=1, source_target_pairs={{0,14},{2,12},{4,10},{6,8},{8,6},{10,4},{12,2},{14,0},{16,30},{18,... | collective-permute-start | bytes 270344 | tf_op jit(solution)/shard_map/cond/branch_4_fun/ppermute | solution.py:305
  19.5 10.6 %collective-permute-start.62 = (bf16[352,128]{1,0:T(8,128)(2,1)S(1)}, bf16[352,128]{1,0:T(8,128)(2,1)S(1)}, u32[]{:S(2)}, u32[]{:S(2)}) collective-permute-start(bf16[352,128]{1,0:T(8,128)(2,1)S(1)} %get-tuple-element.143), channel_id=1, source_target_pairs={{0,28},{2,30},{4,24},{6,26},{8,20},{10,22},{12,16},{14,18},{16,12}... | collective-permute-start | bytes 270344 | tf_op jit(solution)/shard_map/cond/branch_4_fun/ppermute | solution.py:305
  21.3 11.0 %collective-permute-start.63 = (bf16[352,128]{1,0:T(8,128)(2,1)S(1)}, bf16[352,128]{1,0:T(8,128)(2,1)S(1)}, u32[]{:S(2)}, u32[]{:S(2)}) collective-permute-start(bf16[352,128]{1,0:T(8,128)(2,1)S(1)} %get-tuple-element.144), channel_id=1, source_target_pairs={{0,12},{2,14},{4,8},{6,10},{8,4},{10,6},{12,0},{14,2},{16,28},{18,... | collective-permute-start | bytes 270344 | tf_op jit(solution)/shard_map/cond/branch_4_fun/ppermute | solution.py:305
  22.4 10.8 %collective-permute-start.64 = (bf16[352,128]{1,0:T(8,128)(2,1)S(1)}, bf16[352,128]{1,0:T(8,128)(2,1)S(1)}, u32[]{:S(2)}, u32[]{:S(2)}) collective-permute-start(bf16[352,128]{1,0:T(8,128)(2,1)S(1)} %get-tuple-element.145), channel_id=1, source_target_pairs={{0,26},{2,24},{4,30},{6,28},{8,18},{10,16},{12,22},{14,20},{16,10}... | collective-permute-start | bytes 270344 | tf_op jit(solution)/shard_map/cond/branch_4_fun/ppermute | solution.py:305
  26.2 10.5 %collective-permute-start.65 = (bf16[352,128]{1,0:T(8,128)(2,1)S(1)}, bf16[352,128]{1,0:T(8,128)(2,1)S(1)}, u32[]{:S(2)}, u32[]{:S(2)}) collective-permute-start(bf16[352,128]{1,0:T(8,128)(2,1)S(1)} %get-tuple-element.146), channel_id=1, source_target_pairs={{0,10},{2,8},{4,14},{6,12},{8,2},{10,0},{12,6},{14,4},{16,26},{18,... | collective-permute-start | bytes 270344 | tf_op jit(solution)/shard_map/cond/branch_4_fun/ppermute | solution.py:305
  29.9 7.9 %collective-permute-start.66 = (bf16[352,128]{1,0:T(8,128)(2,1)S(1)}, bf16[352,128]{1,0:T(8,128)(2,1)S(1)}, u32[]{:S(2)}, u32[]{:S(2)}) collective-permute-start(bf16[352,128]{1,0:T(8,128)(2,1)S(1)} %get-tuple-element.147), channel_id=1, source_target_pairs={{0,24},{2,26},{4,28},{6,30},{8,16},{10,18},{12,20},{14,22},{16,8},... | collective-permute-start | bytes 270344 | tf_op jit(solution)/shard_map/cond/branch_4_fun/ppermute | solution.py:305
  30.1 8.9 %collective-permute-start.67 = (bf16[352,128]{1,0:T(8,128)(2,1)S(1)}, bf16[352,128]{1,0:T(8,128)(2,1)S(1)}, u32[]{:S(2)}, u32[]{:S(2)}) collective-permute-start(bf16[352,128]{1,0:T(8,128)(2,1)S(1)} %get-tuple-element.148), channel_id=1, source_target_pairs={{0,8},{2,10},{4,12},{6,14},{8,0},{10,2},{12,4},{14,6},{16,24},{18,... | collective-permute-start | bytes 270344 | tf_op jit(solution)/shard_map/cond/branch_4_fun/ppermute | solution.py:305
  32.3 9.9 %collective-permute-start.68 = (bf16[352,128]{1,0:T(8,128)(2,1)S(1)}, bf16[352,128]{1,0:T(8,128)(2,1)S(1)}, u32[]{:S(2)}, u32[]{:S(2)}) collective-permute-start(bf16[352,128]{1,0:T(8,128)(2,1)S(1)} %get-tuple-element.149), channel_id=1, source_target_pairs={{0,22},{2,20},{4,18},{6,16},{8,30},{10,28},{12,26},{14,24},{16,6},... | collective-permute-start | bytes 270344 | tf_op jit(solution)/shard_map/cond/branch_4_fun/ppermute | solution.py:305
  33.2 9.9 %collective-permute-start.69 = (bf16[352,128]{1,0:T(8,128)(2,1)S(1)}, bf16[352,128]{1,0:T(8,128)(2,1)S(1)}, u32[]{:S(2)}, u32[]{:S(2)}) collective-permute-start(bf16[352,128]{1,0:T(8,128)(2,1)S(1)} %get-tuple-element.150), channel_id=1, source_target_pairs={{0,6},{2,4},{4,2},{6,0},{8,14},{10,12},{12,10},{14,8},{16,22},{18,... | collective-permute-start | bytes 270344 | tf_op jit(solution)/shard_map/cond/branch_4_fun/ppermute | solution.py:305
  36.7 9.7 %collective-permute-start.70 = (bf16[352,128]{1,0:T(8,128)(2,1)S(1)}, bf16[352,128]{1,0:T(8,128)(2,1)S(1)}, u32[]{:S(2)}, u32[]{:S(2)}) collective-permute-start(bf16[352,128]{1,0:T(8,128)(2,1)S(1)} %get-tuple-element.151), channel_id=1, source_target_pairs={{0,20},{2,22},{4,16},{6,18},{8,28},{10,30},{12,24},{14,26},{16,4},... | collective-permute-start | bytes 270344 | tf_op jit(solution)/shard_map/cond/branch_4_fun/ppermute | solution.py:305
  37.9 8.5 %collective-permute-start.71 = (bf16[352,128]{1,0:T(8,128)(2,1)S(1)}, bf16[352,128]{1,0:T(8,128)(2,1)S(1)}, u32[]{:S(2)}, u32[]{:S(2)}) collective-permute-start(bf16[352,128]{1,0:T(8,128)(2,1)S(1)} %get-tuple-element.152), channel_id=1, source_target_pairs={{0,4},{2,6},{4,0},{6,2},{8,12},{10,14},{12,8},{14,10},{16,20},{18,... | collective-permute-start | bytes 270344 | tf_op jit(solution)/shard_map/cond/branch_4_fun/ppermute | solution.py:305
  39.0 11.4 %collective-permute-start.72 = (bf16[352,128]{1,0:T(8,128)(2,1)S(1)}, bf16[352,128]{1,0:T(8,128)(2,1)S(1)}, u32[]{:S(2)}, u32[]{:S(2)}) collective-permute-start(bf16[352,128]{1,0:T(8,128)(2,1)S(1)} %get-tuple-element.153), channel_id=1, source_target_pairs={{0,18},{2,16},{4,22},{6,20},{8,26},{10,24},{12,30},{14,28},{16,2},... | collective-permute-start | bytes 270344 | tf_op jit(solution)/shard_map/cond/branch_4_fun/ppermute | solution.py:305
  42.2 8.2 %collective-permute-start.73 = (bf16[352,128]{1,0:T(8,128)(2,1)S(1)}, bf16[352,128]{1,0:T(8,128)(2,1)S(1)}, u32[]{:S(2)}, u32[]{:S(2)}) collective-permute-start(bf16[352,128]{1,0:T(8,128)(2,1)S(1)} %get-tuple-element.154), channel_id=1, source_target_pairs={{0,2},{2,0},{4,6},{6,4},{8,10},{10,8},{12,14},{14,12},{16,18},{18,... | collective-permute-start | bytes 270344 | tf_op jit(solution)/shard_map/cond/branch_4_fun/ppermute | solution.py:305
  43.2 8.1 %collective-permute-start.74 = (bf16[352,128]{1,0:T(8,128)(2,1)S(1)}, bf16[352,128]{1,0:T(8,128)(2,1)S(1)}, u32[]{:S(2)}, u32[]{:S(2)}) collective-permute-start(bf16[352,128]{1,0:T(8,128)(2,1)S(1)} %get-tuple-element.155), channel_id=1, source_target_pairs={{0,16},{2,18},{4,20},{6,22},{8,24},{10,26},{12,28},{14,30},{16,0},... | collective-permute-start | bytes 270344 | tf_op jit(solution)/shard_map/cond/branch_4_fun/ppermute | solution.py:305
  54.9 0.6 %copy-start.4 = (f32[128,128]{1,0:T(8,128)}, f32[128,128]{1,0:T(8,128)S(1)}, u32[]{:S(2)}) copy-start(f32[128,128]{1,0:T(8,128)S(1)} %get-tuple-element.477) | copy-start | bytes 196612

commit v4 on v3

--- a/solution.py
+++ b/solution.py
@@ -8,8 +8,9 @@
 from jax.sharding import PartitionSpec as P
 
 LANE = 128
-UNROLL = 64
+UNROLL = 32
 QUAD = 4
+FIRST = 5
 STEP = 128
 VMEM_LIMIT = 24 * 1024 * 1024
 LADDER = (32, 38, 40, 42, 44, 46, 56, 144)
@@ -24,9 +25,13 @@
     return order
 
 
-def plan_kernel(
-    owner_in, cycle_in, valid_in, word_ref, scalar_ref, owner_ref, cycle_ref, valid_ref, arrived
-):
+def group_ends(count):
+    return (0, FIRST, count)
+
+
+def plan_kernel(owner_in, cycle_in, valid_in, *rest):
+    block_ref, row_ref, lane_ref, cut_ref, scalar_ref = rest[:5]
+    owner_ref, cycle_ref, valid_ref, arrived = rest[5:]
     tm_index, tile_index = lax.axis_index("tm"), lax.axis_index("tile")
     fetches = [
         pltpu.make_async_copy(source, target, arrived.at[i])
@@ -41,7 +46,7 @@
     chunks = cycle_ref.shape[0] // LANE
     slots = owner_ref.shape[0]
     half = cycle_ref.shape[0] // 2
-    list_rows = word_ref.shape[0]
+    list_rows = block_ref.shape[0]
     slot = lax.broadcasted_iota(jnp.int32, (slots, LANE), 0)
     mine = (slot % 2 == tile_index).astype(jnp.float32)
     owner = jnp.zeros((slots, LANE), jnp.int32)
@@ -126,13 +131,20 @@
     index = LANE * lax.broadcasted_iota(jnp.int32, (list_rows, LANE), 0)
     index = index + lax.broadcasted_iota(jnp.int32, (list_rows, LANE), 1)
     total = jnp.sum(count[:, :1] * mine[:, :1]).astype(jnp.int32)
-    word_ref[...] = jnp.where(index < total, words, (slots // 2 * size) << 19)
+    words = jnp.where(index < total, words, (slots // 2 * size) << 19)
+    lane_of = (words >> 12) & (LANE - 1)
+    block_ref[...] = words & 4095
+    row_ref[...] = (words >> 19) & 4095
+    lane_ref[...] = lane_of
+    cut_ref[...] = jnp.where(words < 0, 0, lane_of)
 
     own_slot = 2 * tm_index + tile_index
     scalar_ref[0] = rung
     scalar_ref[1] = tm_index
     scalar_ref[2] = jnp.sum(jnp.where(slot == own_slot, pixels, 0.0)[:, :1]).astype(jnp.int32)
-    scalar_ref[3] = total
+    for group, end in enumerate(group_ends(slots // 2)):
+        ahead = jnp.where(turn < end, count * mine, 0.0)
+        scalar_ref[3 + group] = jnp.sum(ahead[:, :1]).astype(jnp.int32)
 
 
 def widen_kernel(part, in_ref, *rest):
@@ -148,37 +160,37 @@
     lax.fori_loop(0, half // STEP, widen, 0)
 
 
-def pack_kernel(word_ref, scalar_ref, pool_ref, *rest):
+def pack_kernel(
+    group, first, block_ref, row_ref, lane_ref, cut_ref, scalar_ref, pool_ref, after_ref, *rest
+):
     out_refs, stage = rest[:-1], rest[-1]
     depth = out_refs[0].shape[0]
     frames = pool_ref.shape[1]
     lane = lax.broadcasted_iota(jnp.int32, (frames, LANE), 1)
+    begin, end = scalar_ref[3 + group], scalar_ref[4 + group]
 
     def place(i, held):
-        at = i * UNROLL
-        turned = []
+        at = begin + i * UNROLL
+        turned = [
+            pltpu.roll(pool_ref[block_ref[at + j]], lane_ref[at + j], 1) for j in range(UNROLL)
+        ]
         for j in range(UNROLL):
-            word = word_ref[at + j]
-            turned.append(pltpu.roll(pool_ref[word & 4095], (word >> 12) & (LANE - 1), 1))
-        for j in range(UNROLL):
-            word = word_ref[at + j]
-            shift = (word >> 12) & (LANE - 1)
-            row = pl.multiple_of((word >> 16) & 0x7FF8, frames)
-            stage[pl.ds(row, frames), :] = jnp.where(lane >= shift, turned[j], held)
-            stage[pl.ds(row + frames, frames), :] = turned[j]
-            held = jnp.where(lane >= jnp.where(word < 0, 0, shift), turned[j], held)
+            row = row_ref[at + j]
+            stage[row] = jnp.where(lane >= lane_ref[at + j], turned[j], held)
+            stage[row + 1] = turned[j]
+            held = jnp.where(lane >= cut_ref[at + j], turned[j], held)
         return held
 
     held = jnp.zeros((frames, LANE), jnp.float32)
-    lax.fori_loop(0, (scalar_ref[3] + UNROLL - 1) // UNROLL, place, held)
+    lax.fori_loop(0, (end - begin + UNROLL - 1) // UNROLL, place, held)
 
     step = depth if depth <= 512 else LANE
     for d, out_ref in enumerate(out_refs):
-        base = d * depth
+        base = (first + d) * (depth // frames)
 
         def narrow(i, _, out_ref=out_ref, base=base):
-            row = pl.multiple_of(i * step, step)
-            out_ref[pl.ds(row, step), :] = stage[pl.ds(base + row, step), :].astype(jnp.bfloat16)
+            part = stage[pl.ds(base + i * (step // frames), step // frames)].reshape(step, LANE)
+            out_ref[pl.ds(pl.multiple_of(i * step, step), step), :] = part.astype(jnp.bfloat16)
             return 0
 
         if step == depth:
@@ -248,6 +260,7 @@
     local_frames, half, _ = frames.shape
     frame_count = tm_count * local_frames
     order = exchange_order(tm_count)
+    ends = group_ends(tm_count)
     list_rows = -(-(block_cycle.shape[0] + UNROLL) // (8 * LANE)) * 8
     vmem = pl.BlockSpec(memory_space=pltpu.VMEM)
     smem = pl.BlockSpec(memory_space=pltpu.SMEM)
@@ -265,14 +278,14 @@
         )(*given)
 
     far = lax.ppermute(frames, "tile", [(0, 1), (1, 0)])
-    words, scalars = pl.pallas_call(
+    *lists, scalars = pl.pallas_call(
         plan_kernel,
         out_shape=(
-            jax.ShapeDtypeStruct((list_rows, LANE), jnp.int32),
-            jax.ShapeDtypeStruct((4,), jnp.int32),
+            *[jax.ShapeDtypeStruct((list_rows, LANE), jnp.int32)] * 4,
+            jax.ShapeDtypeStruct((3 + len(ends),), jnp.int32),
         ),
         in_specs=[pl.BlockSpec(memory_space=pltpu.HBM)] * 3,
-        out_specs=(vmem, smem),
+        out_specs=(vmem,) * 4 + (smem,),
         scratch_shapes=[
             pltpu.SMEM(cycle_owner.shape, jnp.int32),
             pltpu.VMEM(block_cycle.shape, jnp.int32),
@@ -287,22 +300,25 @@
     def branch(size):
         depth = size * local_frames
 
-        def run(words, scalars, pool):
-            send = pl.pallas_call(
-                pack_kernel,
-                out_shape=(jax.ShapeDtypeStruct((depth, LANE), jnp.bfloat16),) * tm_count,
-                in_specs=[smem, smem, vmem],
-                out_specs=(vmem,) * tm_count,
-                scratch_shapes=[
-                    pltpu.VMEM(((tm_count * size + 2) * local_frames, LANE), jnp.float32)
-                ],
-                compiler_params=params,
-                name="pack",
-            )(words, scalars, pool)
+        def run(lists, scalars, pool):
             got = []
-            for part, apart in zip(send, order):
-                pairs = [(i, i ^ apart) for i in range(tm_count)]
-                got.append(lax.ppermute(part, "tm", pairs) if apart else part)
+            after = scalars
+            for group, (first, end) in enumerate(zip(ends[:-1], ends[1:])):
+                send = pl.pallas_call(
+                    functools.partial(pack_kernel, group, first),
+                    out_shape=(jax.ShapeDtypeStruct((depth, LANE), jnp.bfloat16),) * (end - first),
+                    in_specs=[smem] * 5 + [vmem, pl.BlockSpec(memory_space=pl.ANY)],
+                    out_specs=(vmem,) * (end - first),
+                    scratch_shapes=[
+                        pltpu.VMEM((tm_count * size + 2, local_frames, LANE), jnp.float32)
+                    ],
+                    compiler_params=params,
+                    name="pack",
+                )(*lists, scalars, pool, after)
+                for part, apart in zip(send, order[first:end]):
+                    pairs = [(i, i ^ apart) for i in range(tm_count)]
+                    got.append(lax.ppermute(part, "tm", pairs) if apart else part)
+                after = got[first]
             return pl.pallas_call(
                 gram_kernel,
                 out_shape=jax.ShapeDtypeStruct((frame_count, frame_count), jnp.float32),
@@ -322,7 +338,7 @@
     return lax.switch(
         scalars[0],
         [branch(size) for size in LADDER],
-        words.reshape(-1),
+        [each.reshape(-1) for each in lists],
         scalars,
         pool,
     )

time: 54.8 us -> 54.7 us (level); the launches traced: 55.5 us -> 54.4 us
  waiting for transfers between devices: 13 us -> 10 us
  starting transfers between devices: 25.9 us -> 27.2 us
  Pallas kernels: 13.8 us -> 14.4 us
    ppermute x15, waiting for transfers between devices: 13 us -> 10 us  [run(): got.append(lax.ppermute(part, 'tm', pairs) if apart else part)]
    ppermute x15, starting transfers between devices: 25.5 us -> 26.8 us  [run(): got.append(lax.ppermute(part, 'tm', pairs) if apart else part)]
    pallas_call x2 -> x3, Pallas kernels: 8.6 us -> 9.62 us  [the longest x2 7.79 us: run(): pl.pallas_call(functools.partial(pack_kernel, group, first), out_shape=(j...]
  transfers between devices with their start and end apart: 16 -> 16, of which waited for: 6 -> 4; matrix products, arithmetic and copies ran while one was open for 0% -> 0% of each run, Pallas kernels for 5% -> 14%
where the time goes in v4:
time: 54.7 us; the launch traced here: 54.4 us
  starting transfers between devices  27.2 us (50%)
  Pallas kernels  14.4 us (26%)
  waiting for transfers between devices  10 us (18%)
  local copies, waits for them, and re-layouts  2.3 us (4%)
    ppermute x15, starting transfers between devices, run(): got.append(lax.ppermute(part, 'tm', pairs) if apart else part)  26.8 us
    ppermute x15, waiting for transfers between devices, run(): got.append(lax.ppermute(part, 'tm', pairs) if apart else part)  10 us
    pallas_call x2, Pallas kernels, run(): pl.pallas_call(functools.partial(pack_kernel, group, first), out_shape=(j...  7.79 us
    pallas_call x1, Pallas kernels, run(): pl.pallas_call(gram_kernel, out_shape=jax.ShapeDtypeStruct((frame_count,...  2.83 us
    unnamed x10, local copies, waits for them, and re-layouts  2.3 us
    pallas_call x2, Pallas kernels, widen(): pl.pallas_call(functools.partial(widen_kernel, part), out_shape=jax.Shape...  1.95 us
    pallas_call x1, Pallas kernels, on_device_routed(): pl.pallas_call(plan_kernel, out_shape=(*[jax.ShapeDtypeStruct((list_rows,...  1.84 us
  transfers between devices with their start and end apart: 16, of which 4 were waited for; matrix products, arithmetic and copies ran while one was open for 0% of the time, Pallas kernels for 14%

profile of v4, /device:TPU:0, one launch (start us, length us, event | category | flops | bytes accessed | tf_op | source)
XLA Modules:
  0.0 54.4 jit_solution(1796809404000161251)
XLA Ops:
  0.0 0.5 collective-permute-start.120
  0.5 1.7 %copy-done = bf16[8,1152,128]{2,1,0:T(8,128)(2,1)S(1)} copy-done((bf16[8,1152,128]{2,1,0:T(8,128)(2,1)S(1)}, bf16[8,1152,128]{2,1,0:T(8,128)(2,1)}, u32[]{:S(2)}) %copy-start) | copy-done | bytes 2359320
  2.1 1.0 %widen.2.rest_0_ = f32[2304,8,128]{2,1,0:T(8,128)S(1)} custom-call(bf16[8,1152,128]{2,1,0:T(8,128)(2,1)S(1)} %copy-done), custom_call_target="tpu_custom_call" | custom-call | tf_op jit(solution)/shard_map/widen/pallas_call | solution.py:270
  3.1 1.8 %plan.1 = (s32[24,128]{1,0:T(8,128)S(1)}, s32[24,128]{1,0:T(8,128)S(1)}, s32[24,128]{1,0:T(8,128)S(1)}, s32[24,128]{1,0:T(8,128)S(1)}, s32[6]{0:T(128)S(1)}) custom-call(s32[32]{0:T(128)S(1)} %copy-done.3, s32[2304]{0:T(1024)S(1)} %copy-done.1, s32[2304]{0:T(1024)S(1)} %copy-done.2), custom_call_target="tpu_custom_call" | custom-call | tf_op jit(solution)/shard_map/plan/pallas_call | solution.py:281
  5.0 1.0 %widen.3 = f32[2304,8,128]{2,1,0:T(8,128)S(1)} custom-call(bf16[8,1152,128]{2,1,0:T(8,128)(2,1)S(1)} %collective-permute-done.120.in_ref, f32[2304,8,128]{2,1,0:T(8,128)S(1)} %widen.2.rest_0_), custom_call_target="tpu_custom_call", output_to_operand_aliasing={{}: (1, {})} | custom-call | tf_op jit(solution)/shard_map/widen/pallas_call | solution.py:270
  6.0 47.7 %conditional.1 = (f32[128,128]{1,0:T(8,128)S(1)}) conditional(s32[]{:T(128)} %bitcast.32, (s32[24,128]{1,0:T(8,128)S(1)}, s32[24,128]{1,0:T(8,128)S(1)}, s32[24,128]{1,0:T(8,128)S(1)}, s32[24,128]{1,0:T(8,128)S(1)}, s32[6]{0:T(128)S(1)}, /*index=5*/f32[2304,8,128]{2,1,0:T(8,128)S(1)}) %tuple.29, ...), branch_computations={%region_0.0_spmd, %region_1.0_spmd, %region_2.0_spmd, %region_3.0_... | conditional | bytes 17695328 | solution.py:338
  6.0 3.0 %pack.22 = (bf16[336,128]{1,0:T(8,128)(2,1)S(1)}, bf16[336,128]{1,0:T(8,128)(2,1)S(1)}, bf16[336,128]{1,0:T(8,128)(2,1)S(1)}, bf16[336,128]{1,0:T(8,128)(2,1)S(1)}, bf16[336,128]{1,0:T(8,128)(2,1)S(1)}) custom-call(s32[3072]{0:T(1024)S(1)} %bitcast.40, s32[3072]{0:T(1024)S(1)} %bitcast.56, s32[3072]{0:T(1024)S(1)} %bitcast.72, s32[3072]{0:T(1024)S(1)} %bitcast.88, ...), custom_call_target="tpu_custom_call" | custom-call | tf_op jit(solution)/shard_map/cond/branch_3_fun/pack/pallas_call | solution.py:307
  9.1 6.7 %collective-permute-start.45 = (bf16[336,128]{1,0:T(8,128)(2,1)S(1)}, bf16[336,128]{1,0:T(8,128)(2,1)S(1)}, u32[]{:S(2)}, u32[]{:S(2)}) collective-permute-start(bf16[336,128]{1,0:T(8,128)(2,1)S(1)} %get-tuple-element.182), channel_id=1, source_target_pairs={{0,30},{2,28},{4,26},{6,24},{8,22},{10,20},{12,18},{14,16},{16,14}... | collective-permute-start | bytes 258056 | tf_op jit(solution)/shard_map/cond/branch_3_fun/ppermute | solution.py:320
  15.8 0.0 collective-permute-start.46
  15.8 1.8 %collective-permute-start.47 = (bf16[336,128]{1,0:T(8,128)(2,1)S(1)}, bf16[336,128]{1,0:T(8,128)(2,1)S(1)}, u32[]{:S(2)}, u32[]{:S(2)}) collective-permute-start(bf16[336,128]{1,0:T(8,128)(2,1)S(1)} %get-tuple-element.184), channel_id=1, source_target_pairs={{0,28},{2,30},{4,24},{6,26},{8,20},{10,22},{12,16},{14,18},{16,12}... | collective-permute-start | bytes 258056 | tf_op jit(solution)/shard_map/cond/branch_3_fun/ppermute | solution.py:320
  17.5 1.1 %collective-permute-start.48 = (bf16[336,128]{1,0:T(8,128)(2,1)S(1)}, bf16[336,128]{1,0:T(8,128)(2,1)S(1)}, u32[]{:S(2)}, u32[]{:S(2)}) collective-permute-start(bf16[336,128]{1,0:T(8,128)(2,1)S(1)} %get-tuple-element.185), channel_id=1, source_target_pairs={{0,12},{2,14},{4,8},{6,10},{8,4},{10,6},{12,0},{14,2},{16,28},{18,... | collective-permute-start | bytes 258056 | tf_op jit(solution)/shard_map/cond/branch_3_fun/ppermute | solution.py:320
  18.7 3.8 %collective-permute-start.49 = (bf16[336,128]{1,0:T(8,128)(2,1)S(1)}, bf16[336,128]{1,0:T(8,128)(2,1)S(1)}, u32[]{:S(2)}, u32[]{:S(2)}) collective-permute-start(bf16[336,128]{1,0:T(8,128)(2,1)S(1)} %get-tuple-element.186), channel_id=1, source_target_pairs={{0,26},{2,24},{4,30},{6,28},{8,18},{10,16},{12,22},{14,20},{16,10}... | collective-permute-start | bytes 258056 | tf_op jit(solution)/shard_map/cond/branch_3_fun/ppermute | solution.py:320
  22.5 0.0 collective-permute-done.45.after_ref.refs_0_
  22.5 4.8 %pack.23 = (bf16[336,128]{1,0:T(8,128)(2,1)S(1)}, bf16[336,128]{1,0:T(8,128)(2,1)S(1)}, bf16[336,128]{1,0:T(8,128)(2,1)S(1)}, bf16[336,128]{1,0:T(8,128)(2,1)S(1...) custom-call(s32[3072]{0:T(1024)S(1)} %bitcast.41, ...), custom_call_target="tpu_custom_call" | custom-call | tf_op jit(solution)/shard_map/cond/branch_3_fun/pack/pallas_call | solution.py:307
  27.3 0.1 collective-permute-start.50
  27.4 0.0 collective-permute-done.46.refs_1_
  27.4 1.0 %collective-permute-start.51 = (bf16[336,128]{1,0:T(8,128)(2,1)S(1)}, bf16[336,128]{1,0:T(8,128)(2,1)S(1)}, u32[]{:S(2)}, u32[]{:S(2)}) collective-permute-start(bf16[336,128]{1,0:T(8,128)(2,1)S(1)} %get-tuple-element.188), channel_id=1, source_target_pairs={{0,24},{2,26},{4,28},{6,30},{8,16},{10,18},{12,20},{14,22},{16,8},... | collective-permute-start | bytes 258056 | tf_op jit(solution)/shard_map/cond/branch_3_fun/ppermute | solution.py:320
  28.4 1.5 %collective-permute-start.52 = (bf16[336,128]{1,0:T(8,128)(2,1)S(1)}, bf16[336,128]{1,0:T(8,128)(2,1)S(1)}, u32[]{:S(2)}, u32[]{:S(2)}) collective-permute-start(bf16[336,128]{1,0:T(8,128)(2,1)S(1)} %get-tuple-element.189), channel_id=1, source_target_pairs={{0,8},{2,10},{4,12},{6,14},{8,0},{10,2},{12,4},{14,6},{16,24},{18,... | collective-permute-start | bytes 258056 | tf_op jit(solution)/shard_map/cond/branch_3_fun/ppermute | solution.py:320
  29.9 3.3 %collective-permute-start.53 = (bf16[336,128]{1,0:T(8,128)(2,1)S(1)}, bf16[336,128]{1,0:T(8,128)(2,1)S(1)}, u32[]{:S(2)}, u32[]{:S(2)}) collective-permute-start(bf16[336,128]{1,0:T(8,128)(2,1)S(1)} %get-tuple-element.190), channel_id=1, source_target_pairs={{0,22},{2,20},{4,18},{6,16},{8,30},{10,28},{12,26},{14,24},{16,6},... | collective-permute-start | bytes 258056 | tf_op jit(solution)/shard_map/cond/branch_3_fun/ppermute | solution.py:320
  33.1 1.0 %collective-permute-start.54 = (bf16[336,128]{1,0:T(8,128)(2,1)S(1)}, bf16[336,128]{1,0:T(8,128)(2,1)S(1)}, u32[]{:S(2)}, u32[]{:S(2)}) collective-permute-start(bf16[336,128]{1,0:T(8,128)(2,1)S(1)} %get-tuple-element.191), channel_id=1, source_target_pairs={{0,6},{2,4},{4,2},{6,0},{8,14},{10,12},{12,10},{14,8},{16,22},{18,... | collective-permute-start | bytes 258056 | tf_op jit(solution)/shard_map/cond/branch_3_fun/ppermute | solution.py:320
  34.2 0.0 collective-permute-done.50.refs_5_
  34.2 2.1 %collective-permute-start.55 = (bf16[336,128]{1,0:T(8,128)(2,1)S(1)}, bf16[336,128]{1,0:T(8,128)(2,1)S(1)}, u32[]{:S(2)}, u32[]{:S(2)}) collective-permute-start(bf16[336,128]{1,0:T(8,128)(2,1)S(1)} %get-tuple-element.192), channel_id=1, source_target_pairs={{0,20},{2,22},{4,16},{6,18},{8,28},{10,30},{12,24},{14,26},{16,4},... | collective-permute-start | bytes 258056 | tf_op jit(solution)/shard_map/cond/branch_3_fun/ppermute | solution.py:320
  36.3 0.4 collective-permute-start.56
  36.6 0.0 collective-permute-done.52.refs_7_
  36.6 4.0 %collective-permute-start.57 = (bf16[336,128]{1,0:T(8,128)(2,1)S(1)}, bf16[336,128]{1,0:T(8,128)(2,1)S(1)}, u32[]{:S(2)}, u32[]{:S(2)}) collective-permute-start(bf16[336,128]{1,0:T(8,128)(2,1)S(1)} %get-tuple-element.194), channel_id=1, source_target_pairs={{0,18},{2,16},{4,22},{6,20},{8,26},{10,24},{12,30},{14,28},{16,2},... | collective-permute-start | bytes 258056 | tf_op jit(solution)/shard_map/cond/branch_3_fun/ppermute | solution.py:320
  40.7 4.6 %collective-permute-done.53.refs_8_ = bf16[336,128]{1,0:T(8,128)(2,1)S(1)} collective-permute-done((bf16[336,128]{1,0:T(8,128)(2,1)S(1)}, bf16[336,128]{1,0:T(8,128)(2,1)S(1)}, u32[]{:S(2)}, u32[]{:S(2)}) %collective-permute-start.53) | collective-permute-done | bytes 86048 | tf_op jit(solution)/shard_map/cond/branch_3_fun/ppermute | solution.py:320
  45.3 3.6 %collective-permute-done.57.refs_12_ = bf16[336,128]{1,0:T(8,128)(2,1)S(1)} collective-permute-done((bf16[336,128]{1,0:T(8,128)(2,1)S(1)}, bf16[336,128]{1,0:T(8,128)(2,1)S(1)}, u32[]{:S(2)}, u32[]{:S(2)}) %collective-permute-start.57) | collective-permute-done | bytes 86048 | tf_op jit(solution)/shard_map/cond/branch_3_fun/ppermute | solution.py:320
  49.0 0.8 %collective-permute-done.58.refs_13_ = bf16[336,128]{1,0:T(8,128)(2,1)S(1)} collective-permute-done((bf16[336,128]{1,0:T(8,128)(2,1)S(1)}, bf16[336,128]{1,0:T(8,128)(2,1)S(1)}, u32[]{:S(2)}, u32[]{:S(2)}) %collective-permute-start.58) | collective-permute-done | bytes 86048 | tf_op jit(solution)/shard_map/cond/branch_3_fun/ppermute | solution.py:320
  49.8 0.9 %collective-permute-done.59.refs_14_ = bf16[336,128]{1,0:T(8,128)(2,1)S(1)} collective-permute-done((bf16[336,128]{1,0:T(8,128)(2,1)S(1)}, bf16[336,128]{1,0:T(8,128)(2,1)S(1)}, u32[]{:S(2)}, u32[]{:S(2)}) %collective-permute-start.59) | collective-permute-done | bytes 86048 | tf_op jit(solution)/shard_map/cond/branch_3_fun/ppermute | solution.py:320
  50.7 2.8 %gram.11 = f32[128,128]{1,0:T(8,128)S(1)} custom-call(s32[6]{0:T(128)S(1)} %get-tuple-element.176.scalar_ref.after_ref, bf16[336,128]{1,0:T(8,128)(2,1)S(1)} %collective-permute-done.45.after_ref.refs_0_, bf16[336,128]{1,0:T(8,128)(2,1)S(1)} %collective-permute-done.46.refs_1_, bf16[336,128]{1,0:T(8,128)(2,1)S(1)} %collective-permute-done.47.refs_2_, ...), custom_call_target="tpu_custom_call" | custom-call | tf_op jit(solution)/shard_map/cond/branch_3_fun/gram/pallas_call | solution.py:322
  53.8 0.0 copy-start.4
  53.8 0.6 %copy-done.4 = f32[128,128]{1,0:T(8,128)} copy-done((f32[128,128]{1,0:T(8,128)}, f32[128,128]{1,0:T(8,128)S(1)}, u32[]{:S(2)}) %copy-start.4) | copy-done | bytes 65560
  (17 shorter events, 0.0 us)
Async XLA Ops:
  0.0 5.0 %collective-permute-start.120 = (bf16[8,1152,128]{2,1,0:T(8,128)(2,1)}, bf16[8,1152,128]{2,1,0:T(8,128)(2,1)S(1)}, u32[]{:S(2)}, u32[]{:S(2)}) collective-permute-start(bf16[8,1152,128]{2,1,0:T(8,128)(2,1)} %in_ref.1), channel_id=1, source_target_pairs={{0,1},{1,0},{2,3},{3,2},{4,5},{5,4},{6,7},{7,6},{8,9},{9,8},{10,11... | collective-permute-start | bytes 7077896 | tf_op jit(solution)/shard_map/ppermute | solution.py:280
  0.5 1.7 %copy-start = (bf16[8,1152,128]{2,1,0:T(8,128)(2,1)S(1)}, bf16[8,1152,128]{2,1,0:T(8,128)(2,1)}, u32[]{:S(2)}) copy-start(bf16[8,1152,128]{2,1,0:T(8,128)(2,1)} %in_ref.1) | copy-start | bytes 7077892
  2.1 1.0 %copy-start.1 = (s32[2304]{0:T(1024)S(1)}, s32[2304]{0:T(1024)}, u32[]{:S(2)}) copy-start(s32[2304]{0:T(1024)} %cycle_in.1) | copy-start | bytes 27652
  2.1 1.0 %copy-start.2 = (s32[2304]{0:T(1024)S(1)}, s32[2304]{0:T(1024)}, u32[]{:S(2)}) copy-start(s32[2304]{0:T(1024)} %valid_in.1) | copy-start | bytes 27652
  2.1 1.0 %copy-start.3 = (s32[32]{0:T(128)S(1)}, s32[32]{0:T(128)}, u32[]{:S(2)}) copy-start(s32[32]{0:T(128)} %owner_in.1) | copy-start | bytes 388
  9.1 13.4 %collective-permute-start.45 = (bf16[336,128]{1,0:T(8,128)(2,1)S(1)}, bf16[336,128]{1,0:T(8,128)(2,1)S(1)}, u32[]{:S(2)}, u32[]{:S(2)}) collective-permute-start(bf16[336,128]{1,0:T(8,128)(2,1)S(1)} %get-tuple-element.182), channel_id=1, source_target_pairs={{0,30},{2,28},{4,26},{6,24},{8,22},{10,20},{12,18},{14,16},{16,14}... | collective-permute-start | bytes 258056 | tf_op jit(solution)/shard_map/cond/branch_3_fun/ppermute | solution.py:320
  15.8 11.6 %collective-permute-start.46 = (bf16[336,128]{1,0:T(8,128)(2,1)S(1)}, bf16[336,128]{1,0:T(8,128)(2,1)S(1)}, u32[]{:S(2)}, u32[]{:S(2)}) collective-permute-start(bf16[336,128]{1,0:T(8,128)(2,1)S(1)} %get-tuple-element.183), channel_id=1, source_target_pairs={{0,14},{2,12},{4,10},{6,8},{8,6},{10,4},{12,2},{14,0},{16,30},{18,... | collective-permute-start | bytes 258056 | tf_op jit(solution)/shard_map/cond/branch_3_fun/ppermute | solution.py:320
  15.8 12.6 %collective-permute-start.47 = (bf16[336,128]{1,0:T(8,128)(2,1)S(1)}, bf16[336,128]{1,0:T(8,128)(2,1)S(1)}, u32[]{:S(2)}, u32[]{:S(2)}) collective-permute-start(bf16[336,128]{1,0:T(8,128)(2,1)S(1)} %get-tuple-element.184), channel_id=1, source_target_pairs={{0,28},{2,30},{4,24},{6,26},{8,20},{10,22},{12,16},{14,18},{16,12}... | collective-permute-start | bytes 258056 | tf_op jit(solution)/shard_map/cond/branch_3_fun/ppermute | solution.py:320
  17.5 12.3 %collective-permute-start.48 = (bf16[336,128]{1,0:T(8,128)(2,1)S(1)}, bf16[336,128]{1,0:T(8,128)(2,1)S(1)}, u32[]{:S(2)}, u32[]{:S(2)}) collective-permute-start(bf16[336,128]{1,0:T(8,128)(2,1)S(1)} %get-tuple-element.185), channel_id=1, source_target_pairs={{0,12},{2,14},{4,8},{6,10},{8,4},{10,6},{12,0},{14,2},{16,28},{18,... | collective-permute-start | bytes 258056 | tf_op jit(solution)/shard_map/cond/branch_3_fun/ppermute | solution.py:320
  18.7 14.5 %collective-permute-start.49 = (bf16[336,128]{1,0:T(8,128)(2,1)S(1)}, bf16[336,128]{1,0:T(8,128)(2,1)S(1)}, u32[]{:S(2)}, u32[]{:S(2)}) collective-permute-start(bf16[336,128]{1,0:T(8,128)(2,1)S(1)} %get-tuple-element.186), channel_id=1, source_target_pairs={{0,26},{2,24},{4,30},{6,28},{8,18},{10,16},{12,22},{14,20},{16,10}... | collective-permute-start | bytes 258056 | tf_op jit(solution)/shard_map/cond/branch_3_fun/ppermute | solution.py:320
  27.3 6.9 %collective-permute-start.50 = (bf16[336,128]{1,0:T(8,128)(2,1)S(1)}, bf16[336,128]{1,0:T(8,128)(2,1)S(1)}, u32[]{:S(2)}, u32[]{:S(2)}) collective-permute-start(bf16[336,128]{1,0:T(8,128)(2,1)S(1)} %get-tuple-element.187), channel_id=1, source_target_pairs={{0,10},{2,8},{4,14},{6,12},{8,2},{10,0},{12,6},{14,4},{16,26},{18,... | collective-permute-start | bytes 258056 | tf_op jit(solution)/shard_map/cond/branch_3_fun/ppermute | solution.py:320
  27.4 8.9 %collective-permute-start.51 = (bf16[336,128]{1,0:T(8,128)(2,1)S(1)}, bf16[336,128]{1,0:T(8,128)(2,1)S(1)}, u32[]{:S(2)}, u32[]{:S(2)}) collective-permute-start(bf16[336,128]{1,0:T(8,128)(2,1)S(1)} %get-tuple-element.188), channel_id=1, source_target_pairs={{0,24},{2,26},{4,28},{6,30},{8,16},{10,18},{12,20},{14,22},{16,8},... | collective-permute-start | bytes 258056 | tf_op jit(solution)/shard_map/cond/branch_3_fun/ppermute | solution.py:320
  28.4 8.3 %collective-permute-start.52 = (bf16[336,128]{1,0:T(8,128)(2,1)S(1)}, bf16[336,128]{1,0:T(8,128)(2,1)S(1)}, u32[]{:S(2)}, u32[]{:S(2)}) collective-permute-start(bf16[336,128]{1,0:T(8,128)(2,1)S(1)} %get-tuple-element.189), channel_id=1, source_target_pairs={{0,8},{2,10},{4,12},{6,14},{8,0},{10,2},{12,4},{14,6},{16,24},{18,... | collective-permute-start | bytes 258056 | tf_op jit(solution)/shard_map/cond/branch_3_fun/ppermute | solution.py:320
  29.9 15.4 %collective-permute-start.53 = (bf16[336,128]{1,0:T(8,128)(2,1)S(1)}, bf16[336,128]{1,0:T(8,128)(2,1)S(1)}, u32[]{:S(2)}, u32[]{:S(2)}) collective-permute-start(bf16[336,128]{1,0:T(8,128)(2,1)S(1)} %get-tuple-element.190), channel_id=1, source_target_pairs={{0,22},{2,20},{4,18},{6,16},{8,30},{10,28},{12,26},{14,24},{16,6},... | collective-permute-start | bytes 258056 | tf_op jit(solution)/shard_map/cond/branch_3_fun/ppermute | solution.py:320
  33.1 12.2 %collective-permute-start.54 = (bf16[336,128]{1,0:T(8,128)(2,1)S(1)}, bf16[336,128]{1,0:T(8,128)(2,1)S(1)}, u32[]{:S(2)}, u32[]{:S(2)}) collective-permute-start(bf16[336,128]{1,0:T(8,128)(2,1)S(1)} %get-tuple-element.191), channel_id=1, source_target_pairs={{0,6},{2,4},{4,2},{6,0},{8,14},{10,12},{12,10},{14,8},{16,22},{18,... | collective-permute-start | bytes 258056 | tf_op jit(solution)/shard_map/cond/branch_3_fun/ppermute | solution.py:320
  34.2 11.1 %collective-permute-start.55 = (bf16[336,128]{1,0:T(8,128)(2,1)S(1)}, bf16[336,128]{1,0:T(8,128)(2,1)S(1)}, u32[]{:S(2)}, u32[]{:S(2)}) collective-permute-start(bf16[336,128]{1,0:T(8,128)(2,1)S(1)} %get-tuple-element.192), channel_id=1, source_target_pairs={{0,20},{2,22},{4,16},{6,18},{8,28},{10,30},{12,24},{14,26},{16,4},... | collective-permute-start | bytes 258056 | tf_op jit(solution)/shard_map/cond/branch_3_fun/ppermute | solution.py:320
  36.3 9.1 %collective-permute-start.56 = (bf16[336,128]{1,0:T(8,128)(2,1)S(1)}, bf16[336,128]{1,0:T(8,128)(2,1)S(1)}, u32[]{:S(2)}, u32[]{:S(2)}) collective-permute-start(bf16[336,128]{1,0:T(8,128)(2,1)S(1)} %get-tuple-element.193), channel_id=1, source_target_pairs={{0,4},{2,6},{4,0},{6,2},{8,12},{10,14},{12,8},{14,10},{16,20},{18,... | collective-permute-start | bytes 258056 | tf_op jit(solution)/shard_map/cond/branch_3_fun/ppermute | solution.py:320
  36.6 12.4 %collective-permute-start.57 = (bf16[336,128]{1,0:T(8,128)(2,1)S(1)}, bf16[336,128]{1,0:T(8,128)(2,1)S(1)}, u32[]{:S(2)}, u32[]{:S(2)}) collective-permute-start(bf16[336,128]{1,0:T(8,128)(2,1)S(1)} %get-tuple-element.194), channel_id=1, source_target_pairs={{0,18},{2,16},{4,22},{6,20},{8,26},{10,24},{12,30},{14,28},{16,2},... | collective-permute-start | bytes 258056 | tf_op jit(solution)/shard_map/cond/branch_3_fun/ppermute | solution.py:320
  45.3 4.5 %collective-permute-start.58 = (bf16[336,128]{1,0:T(8,128)(2,1)S(1)}, bf16[336,128]{1,0:T(8,128)(2,1)S(1)}, u32[]{:S(2)}, u32[]{:S(2)}) collective-permute-start(bf16[336,128]{1,0:T(8,128)(2,1)S(1)} %get-tuple-element.195), channel_id=1, source_target_pairs={{0,2},{2,0},{4,6},{6,4},{8,10},{10,8},{12,14},{14,12},{16,18},{18,... | collective-permute-start | bytes 258056 | tf_op jit(solution)/shard_map/cond/branch_3_fun/ppermute | solution.py:320
  45.3 5.4 %collective-permute-start.59 = (bf16[336,128]{1,0:T(8,128)(2,1)S(1)}, bf16[336,128]{1,0:T(8,128)(2,1)S(1)}, u32[]{:S(2)}, u32[]{:S(2)}) collective-permute-start(bf16[336,128]{1,0:T(8,128)(2,1)S(1)} %get-tuple-element.196), channel_id=1, source_target_pairs={{0,16},{2,18},{4,20},{6,22},{8,24},{10,26},{12,28},{14,30},{16,0},... | collective-permute-start | bytes 258056 | tf_op jit(solution)/shard_map/cond/branch_3_fun/ppermute | solution.py:320
  53.8 0.6 %copy-start.4 = (f32[128,128]{1,0:T(8,128)}, f32[128,128]{1,0:T(8,128)S(1)}, u32[]{:S(2)}) copy-start(f32[128,128]{1,0:T(8,128)S(1)} %get-tuple-element.579) | copy-start | bytes 196612

commit v5 on v4

--- a/solution.py
+++ b/solution.py
@@ -11,7 +11,7 @@
 UNROLL = 32
 QUAD = 4
 FIRST = 5
-STEP = 128
+STEP = 384
 VMEM_LIMIT = 24 * 1024 * 1024
 LADDER = (32, 38, 40, 42, 44, 46, 56, 144)
 NT = (((1,), (1,)), ((), ()))
@@ -149,15 +149,16 @@
 
 def widen_kernel(part, in_ref, *rest):
     out_ref = rest[-1]
-    half = in_ref.shape[1]
-
-    def widen(i, _):
-        begin = pl.multiple_of(i * STEP, STEP)
-        rows = in_ref[:, pl.ds(begin, STEP), :].astype(jnp.float32)
-        out_ref[pl.ds(part * half + begin, STEP)] = jnp.transpose(rows, (1, 0, 2))
-        return 0
-
-    lax.fori_loop(0, half // STEP, widen, 0)
+    frames, half, _ = in_ref.shape
+    for f in range(frames):
+
+        def widen(i, _, f=f):
+            begin = pl.multiple_of(i * STEP, STEP)
+            rows = in_ref[f, pl.ds(begin, STEP), :].astype(jnp.float32)
+            out_ref[pl.ds(f * (2 * half + 1) + part * half + begin, STEP), :] = rows
+            return 0
+
+        lax.fori_loop(0, half // STEP, widen, 0)
 
 
 def pack_kernel(
@@ -165,14 +166,21 @@
 ):
     out_refs, stage = rest[:-1], rest[-1]
     depth = out_refs[0].shape[0]
-    frames = pool_ref.shape[1]
+    frames = 8
+    stride = pool_ref.shape[0] // frames
     lane = lax.broadcasted_iota(jnp.int32, (frames, LANE), 1)
     begin, end = scalar_ref[3 + group], scalar_ref[4 + group]
 
     def place(i, held):
         at = begin + i * UNROLL
         turned = [
-            pltpu.roll(pool_ref[block_ref[at + j]], lane_ref[at + j], 1) for j in range(UNROLL)
+            jnp.take_along_axis(
+                pool_ref[pl.ds(block_ref[at + j], frames, stride=stride), :],
+                (lane - lane_ref[at + j]) & (LANE - 1),
+                axis=1,
+                mode="promise_in_bounds",
+            )
+            for j in range(UNROLL)
         ]
         for j in range(UNROLL):
             row = row_ref[at + j]
@@ -269,7 +277,7 @@
     def widen(part, *given):
         return pl.pallas_call(
             functools.partial(widen_kernel, part),
-            out_shape=jax.ShapeDtypeStruct((2 * half, local_frames, LANE), jnp.float32),
+            out_shape=jax.ShapeDtypeStruct((local_frames * (2 * half + 1), LANE), jnp.float32),
             in_specs=[vmem] * len(given),
             out_specs=vmem,
             input_output_aliases={1: 0} if part else {},

time: 54.7 us -> 54.9 us (level)
    pallas_call x2, Pallas kernels: 1.95 us -> 0.8 us  [widen(): pl.pallas_call(functools.partial(widen_kernel, part), out_shape=jax.Shape...]
    pallas_call x2, Pallas kernels: 7.79 us -> 8.77 us  [run(): pl.pallas_call(functools.partial(pack_kernel, group, first), out_shape=(j...]
  transfers between devices with their start and end apart: 16 -> 16, of which waited for: 4 -> 7; matrix products, arithmetic and copies ran while one was open for 0% -> 0% of each run, Pallas kernels for 14% -> 14%
where the time goes in v5:
time: 54.9 us; the launch traced here: 54.6 us
  starting transfers between devices  27.4 us (50%)
  Pallas kernels  14.2 us (26%)
  waiting for transfers between devices  9.78 us (18%)
  local copies, waits for them, and re-layouts  2.61 us (5%)
    ppermute x15, starting transfers between devices, run(): got.append(lax.ppermute(part, 'tm', pairs) if apart else part)  27 us
    ppermute x15, waiting for transfers between devices, run(): got.append(lax.ppermute(part, 'tm', pairs) if apart else part)  9.68 us
    pallas_call x2, Pallas kernels, run(): pl.pallas_call(functools.partial(pack_kernel, group, first), out_shape=(j...  8.77 us
    pallas_call x1, Pallas kernels, run(): pl.pallas_call(gram_kernel, out_shape=jax.ShapeDtypeStruct((frame_count,...  2.83 us
    unnamed x10, local copies, waits for them, and re-layouts  2.61 us
    pallas_call x1, Pallas kernels, on_device_routed(): pl.pallas_call(plan_kernel, out_shape=(*[jax.ShapeDtypeStruct((list_rows,...  1.83 us
  transfers between devices with their start and end apart: 16, of which 7 were waited for; matrix products, arithmetic and copies ran while one was open for 0% of the time, Pallas kernels for 14%

profile of v5, /device:TPU:0, one launch (start us, length us, event | category | flops | bytes accessed | tf_op | source)
XLA Modules:
  0.0 54.6 jit_solution(5213790108984583985)
XLA Ops:
  0.0 0.5 collective-permute-start.120
  0.5 1.7 %copy-done = bf16[8,1152,128]{2,1,0:T(8,128)(2,1)S(1)} copy-done((bf16[8,1152,128]{2,1,0:T(8,128)(2,1)S(1)}, bf16[8,1152,128]{2,1,0:T(8,128)(2,1)}, u32[]{:S(2)}) %copy-start) | copy-done | bytes 2359320
  2.1 0.4 widen.2.rest_0_
  2.5 0.3 copy-done.1
  2.8 0.0 copy-done.2
  2.8 1.8 %plan.1 = (s32[24,128]{1,0:T(8,128)S(1)}, s32[24,128]{1,0:T(8,128)S(1)}, s32[24,128]{1,0:T(8,128)S(1)}, s32[24,128]{1,0:T(8,128)S(1)}, s32[6]{0:T(128)S(1)}) custom-call(s32[32]{0:T(128)S(1)} %copy-done.3, s32[2304]{0:T(1024)S(1)} %copy-done.1, s32[2304]{0:T(1024)S(1)} %copy-done.2), custom_call_target="tpu_custom_call" | custom-call | tf_op jit(solution)/shard_map/plan/pallas_call | solution.py:289
  4.7 0.1 collective-permute-done.120.in_ref
  4.8 0.4 widen.3
  5.2 48.7 %conditional.1 = (f32[128,128]{1,0:T(8,128)S(1)}) conditional(s32[]{:T(128)} %bitcast.32, (s32[24,128]{1,0:T(8,128)S(1)}, s32[24,128]{1,0:T(8,128)S(1)}, s32[24,128]{1,0:T(8,128)S(1)}, s32[24,128]{1,0:T(8,128)S(1)}, s32[6]{0:T(128)S(1)}, /*index=5*/f32[18440,128]{1,0:T(8,128)S(1)}) %tuple.29, ...), branch_computations={%region_0.0_spmd, %region_1.0_spmd, %region_2.0_spmd, %region_3.0_... | conditional | bytes 17695328 | solution.py:346
  5.3 3.3 %pack.24 = (bf16[352,128]{1,0:T(8,128)(2,1)S(1)}, bf16[352,128]{1,0:T(8,128)(2,1)S(1)}, bf16[352,128]{1,0:T(8,128)(2,1)S(1)}, bf16[352,128]{1,0:T(8,128)(2,1)S(1)}, bf16[352,128]{1,0:T(8,128)(2,1)S(1)}) custom-call(s32[3072]{0:T(1024)S(1)} %bitcast.42, s32[3072]{0:T(1024)S(1)} %bitcast.58, s32[3072]{0:T(1024)S(1)} %bitcast.74, s32[3072]{0:T(1024)S(1)} %bitcast.90, ...), custom_call_target="tpu_custom_call" | custom-call | tf_op jit(solution)/shard_map/cond/branch_4_fun/pack/pallas_call | solution.py:315
  8.6 6.9 %collective-permute-start.60 = (bf16[352,128]{1,0:T(8,128)(2,1)S(1)}, bf16[352,128]{1,0:T(8,128)(2,1)S(1)}, u32[]{:S(2)}, u32[]{:S(2)}) collective-permute-start(bf16[352,128]{1,0:T(8,128)(2,1)S(1)} %get-tuple-element.204), channel_id=1, source_target_pairs={{0,30},{2,28},{4,26},{6,24},{8,22},{10,20},{12,18},{14,16},{16,14}... | collective-permute-start | bytes 270344 | tf_op jit(solution)/shard_map/cond/branch_4_fun/ppermute | solution.py:328
  15.5 1.8 %collective-permute-start.62 = (bf16[352,128]{1,0:T(8,128)(2,1)S(1)}, bf16[352,128]{1,0:T(8,128)(2,1)S(1)}, u32[]{:S(2)}, u32[]{:S(2)}) collective-permute-start(bf16[352,128]{1,0:T(8,128)(2,1)S(1)} %get-tuple-element.206), channel_id=1, source_target_pairs={{0,28},{2,30},{4,24},{6,26},{8,20},{10,22},{12,16},{14,18},{16,12}... | collective-permute-start | bytes 270344 | tf_op jit(solution)/shard_map/cond/branch_4_fun/ppermute | solution.py:328
  17.3 1.1 %collective-permute-start.63 = (bf16[352,128]{1,0:T(8,128)(2,1)S(1)}, bf16[352,128]{1,0:T(8,128)(2,1)S(1)}, u32[]{:S(2)}, u32[]{:S(2)}) collective-permute-start(bf16[352,128]{1,0:T(8,128)(2,1)S(1)} %get-tuple-element.207), channel_id=1, source_target_pairs={{0,12},{2,14},{4,8},{6,10},{8,4},{10,6},{12,0},{14,2},{16,28},{18,... | collective-permute-start | bytes 270344 | tf_op jit(solution)/shard_map/cond/branch_4_fun/ppermute | solution.py:328
  18.4 3.8 %collective-permute-start.64 = (bf16[352,128]{1,0:T(8,128)(2,1)S(1)}, bf16[352,128]{1,0:T(8,128)(2,1)S(1)}, u32[]{:S(2)}, u32[]{:S(2)}) collective-permute-start(bf16[352,128]{1,0:T(8,128)(2,1)S(1)} %get-tuple-element.208), channel_id=1, source_target_pairs={{0,26},{2,24},{4,30},{6,28},{8,18},{10,16},{12,22},{14,20},{16,10}... | collective-permute-start | bytes 270344 | tf_op jit(solution)/shard_map/cond/branch_4_fun/ppermute | solution.py:328
  22.2 5.4 %pack.25 = (bf16[352,128]{1,0:T(8,128)(2,1)S(1)}, bf16[352,128]{1,0:T(8,128)(2,1)S(1)}, bf16[352,128]{1,0:T(8,128)(2,1)S(1)}, bf16[352,128]{1,0:T(8,128)(2,1)S(1...) custom-call(s32[3072]{0:T(1024)S(1)} %bitcast.43, ...), custom_call_target="tpu_custom_call" | custom-call | tf_op jit(solution)/shard_map/cond/branch_4_fun/pack/pallas_call | solution.py:315
  27.7 0.1 collective-permute-start.65
  27.8 1.0 %collective-permute-start.66 = (bf16[352,128]{1,0:T(8,128)(2,1)S(1)}, bf16[352,128]{1,0:T(8,128)(2,1)S(1)}, u32[]{:S(2)}, u32[]{:S(2)}) collective-permute-start(bf16[352,128]{1,0:T(8,128)(2,1)S(1)} %get-tuple-element.210), channel_id=1, source_target_pairs={{0,24},{2,26},{4,28},{6,30},{8,16},{10,18},{12,20},{14,22},{16,8},... | collective-permute-start | bytes 270344 | tf_op jit(solution)/shard_map/cond/branch_4_fun/ppermute | solution.py:328
  28.8 1.8 %collective-permute-start.67 = (bf16[352,128]{1,0:T(8,128)(2,1)S(1)}, bf16[352,128]{1,0:T(8,128)(2,1)S(1)}, u32[]{:S(2)}, u32[]{:S(2)}) collective-permute-start(bf16[352,128]{1,0:T(8,128)(2,1)S(1)} %get-tuple-element.211), channel_id=1, source_target_pairs={{0,8},{2,10},{4,12},{6,14},{8,0},{10,2},{12,4},{14,6},{16,24},{18,... | collective-permute-start | bytes 270344 | tf_op jit(solution)/shard_map/cond/branch_4_fun/ppermute | solution.py:328
  30.5 3.0 %collective-permute-start.68 = (bf16[352,128]{1,0:T(8,128)(2,1)S(1)}, bf16[352,128]{1,0:T(8,128)(2,1)S(1)}, u32[]{:S(2)}, u32[]{:S(2)}) collective-permute-start(bf16[352,128]{1,0:T(8,128)(2,1)S(1)} %get-tuple-element.212), channel_id=1, source_target_pairs={{0,22},{2,20},{4,18},{6,16},{8,30},{10,28},{12,26},{14,24},{16,6},... | collective-permute-start | bytes 270344 | tf_op jit(solution)/shard_map/cond/branch_4_fun/ppermute | solution.py:328
  33.5 1.0 %collective-permute-start.69 = (bf16[352,128]{1,0:T(8,128)(2,1)S(1)}, bf16[352,128]{1,0:T(8,128)(2,1)S(1)}, u32[]{:S(2)}, u32[]{:S(2)}) collective-permute-start(bf16[352,128]{1,0:T(8,128)(2,1)S(1)} %get-tuple-element.213), channel_id=1, source_target_pairs={{0,6},{2,4},{4,2},{6,0},{8,14},{10,12},{12,10},{14,8},{16,22},{18,... | collective-permute-start | bytes 270344 | tf_op jit(solution)/shard_map/cond/branch_4_fun/ppermute | solution.py:328
  34.6 0.3 collective-permute-done.65.refs_5_
  34.9 1.9 %collective-permute-start.70 = (bf16[352,128]{1,0:T(8,128)(2,1)S(1)}, bf16[352,128]{1,0:T(8,128)(2,1)S(1)}, u32[]{:S(2)}, u32[]{:S(2)}) collective-permute-start(bf16[352,128]{1,0:T(8,128)(2,1)S(1)} %get-tuple-element.214), channel_id=1, source_target_pairs={{0,20},{2,22},{4,16},{6,18},{8,28},{10,30},{12,24},{14,26},{16,4},... | collective-permute-start | bytes 270344 | tf_op jit(solution)/shard_map/cond/branch_4_fun/ppermute | solution.py:328
  36.8 0.5 collective-permute-start.71
  37.3 4.1 %collective-permute-start.72 = (bf16[352,128]{1,0:T(8,128)(2,1)S(1)}, bf16[352,128]{1,0:T(8,128)(2,1)S(1)}, u32[]{:S(2)}, u32[]{:S(2)}) collective-permute-start(bf16[352,128]{1,0:T(8,128)(2,1)S(1)} %get-tuple-element.216), channel_id=1, source_target_pairs={{0,18},{2,16},{4,22},{6,20},{8,26},{10,24},{12,30},{14,28},{16,2},... | collective-permute-start | bytes 270344 | tf_op jit(solution)/shard_map/cond/branch_4_fun/ppermute | solution.py:328
  41.4 3.9 %collective-permute-done.68.refs_8_ = bf16[352,128]{1,0:T(8,128)(2,1)S(1)} collective-permute-done((bf16[352,128]{1,0:T(8,128)(2,1)S(1)}, bf16[352,128]{1,0:T(8,128)(2,1)S(1)}, u32[]{:S(2)}, u32[]{:S(2)}) %collective-permute-start.68) | collective-permute-done | bytes 90144 | tf_op jit(solution)/shard_map/cond/branch_4_fun/ppermute | solution.py:328
  45.3 0.7 %collective-permute-done.70.refs_10_ = bf16[352,128]{1,0:T(8,128)(2,1)S(1)} collective-permute-done((bf16[352,128]{1,0:T(8,128)(2,1)S(1)}, bf16[352,128]{1,0:T(8,128)(2,1)S(1)}, u32[]{:S(2)}, u32[]{:S(2)}) %collective-permute-start.70) | collective-permute-done | bytes 90144 | tf_op jit(solution)/shard_map/cond/branch_4_fun/ppermute | solution.py:328
  46.0 3.8 %collective-permute-done.72.refs_12_ = bf16[352,128]{1,0:T(8,128)(2,1)S(1)} collective-permute-done((bf16[352,128]{1,0:T(8,128)(2,1)S(1)}, bf16[352,128]{1,0:T(8,128)(2,1)S(1)}, u32[]{:S(2)}, u32[]{:S(2)}) %collective-permute-start.72) | collective-permute-done | bytes 90144 | tf_op jit(solution)/shard_map/cond/branch_4_fun/ppermute | solution.py:328
  49.8 0.5 collective-permute-done.73.refs_13_
  50.3 0.4 collective-permute-done.74.refs_14_
  50.7 2.8 %gram.12 = f32[128,128]{1,0:T(8,128)S(1)} custom-call(s32[6]{0:T(128)S(1)} %get-tuple-element.198.scalar_ref.after_ref, bf16[352,128]{1,0:T(8,128)(2,1)S(1)} %collective-permute-done.60.after_ref.refs_0_, bf16[352,128]{1,0:T(8,128)(2,1)S(1)} %collective-permute-done.61.refs_1_, bf16[352,128]{1,0:T(8,128)(2,1)S(1)} %collective-permute-done.62.refs_2_, ...), custom_call_target="tpu_custom_call" | custom-call | tf_op jit(solution)/shard_map/cond/branch_4_fun/gram/pallas_call | solution.py:330
  54.0 0.0 copy-start.4
  54.0 0.6 %copy-done.4 = f32[128,128]{1,0:T(8,128)} copy-done((f32[128,128]{1,0:T(8,128)}, f32[128,128]{1,0:T(8,128)S(1)}, u32[]{:S(2)}) %copy-start.4) | copy-done | bytes 65560
  (17 shorter events, 0.0 us)
Async XLA Ops:
  0.0 4.8 %collective-permute-start.120 = (bf16[8,1152,128]{2,1,0:T(8,128)(2,1)}, bf16[8,1152,128]{2,1,0:T(8,128)(2,1)S(1)}, u32[]{:S(2)}, u32[]{:S(2)}) collective-permute-start(bf16[8,1152,128]{2,1,0:T(8,128)(2,1)} %in_ref.1), channel_id=1, source_target_pairs={{0,1},{1,0},{2,3},{3,2},{4,5},{5,4},{6,7},{7,6},{8,9},{9,8},{10,11... | collective-permute-start | bytes 7077896 | tf_op jit(solution)/shard_map/ppermute | solution.py:288
  0.5 1.7 %copy-start = (bf16[8,1152,128]{2,1,0:T(8,128)(2,1)S(1)}, bf16[8,1152,128]{2,1,0:T(8,128)(2,1)}, u32[]{:S(2)}) copy-start(bf16[8,1152,128]{2,1,0:T(8,128)(2,1)} %in_ref.1) | copy-start | bytes 7077892
  2.1 0.7 %copy-start.1 = (s32[2304]{0:T(1024)S(1)}, s32[2304]{0:T(1024)}, u32[]{:S(2)}) copy-start(s32[2304]{0:T(1024)} %cycle_in.1) | copy-start | bytes 27652
  2.1 0.7 %copy-start.2 = (s32[2304]{0:T(1024)S(1)}, s32[2304]{0:T(1024)}, u32[]{:S(2)}) copy-start(s32[2304]{0:T(1024)} %valid_in.1) | copy-start | bytes 27652
  2.1 0.7 %copy-start.3 = (s32[32]{0:T(128)S(1)}, s32[32]{0:T(128)}, u32[]{:S(2)}) copy-start(s32[32]{0:T(128)} %owner_in.1) | copy-start | bytes 388
  8.6 13.6 %collective-permute-start.60 = (bf16[352,128]{1,0:T(8,128)(2,1)S(1)}, bf16[352,128]{1,0:T(8,128)(2,1)S(1)}, u32[]{:S(2)}, u32[]{:S(2)}) collective-permute-start(bf16[352,128]{1,0:T(8,128)(2,1)S(1)} %get-tuple-element.204), channel_id=1, source_target_pairs={{0,30},{2,28},{4,26},{6,24},{8,22},{10,20},{12,18},{14,16},{16,14}... | collective-permute-start | bytes 270344 | tf_op jit(solution)/shard_map/cond/branch_4_fun/ppermute | solution.py:328
  15.5 12.3 %collective-permute-start.61 = (bf16[352,128]{1,0:T(8,128)(2,1)S(1)}, bf16[352,128]{1,0:T(8,128)(2,1)S(1)}, u32[]{:S(2)}, u32[]{:S(2)}) collective-permute-start(bf16[352,128]{1,0:T(8,128)(2,1)S(1)} %get-tuple-element.205), channel_id=1, source_target_pairs={{0,14},{2,12},{4,10},{6,8},{8,6},{10,4},{12,2},{14,0},{16,30},{18,... | collective-permute-start | bytes 270344 | tf_op jit(solution)/shard_map/cond/branch_4_fun/ppermute | solution.py:328
  15.5 13.3 %collective-permute-start.62 = (bf16[352,128]{1,0:T(8,128)(2,1)S(1)}, bf16[352,128]{1,0:T(8,128)(2,1)S(1)}, u32[]{:S(2)}, u32[]{:S(2)}) collective-permute-start(bf16[352,128]{1,0:T(8,128)(2,1)S(1)} %get-tuple-element.206), channel_id=1, source_target_pairs={{0,28},{2,30},{4,24},{6,26},{8,20},{10,22},{12,16},{14,18},{16,12}... | collective-permute-start | bytes 270344 | tf_op jit(solution)/shard_map/cond/branch_4_fun/ppermute | solution.py:328
  17.3 13.3 %collective-permute-start.63 = (bf16[352,128]{1,0:T(8,128)(2,1)S(1)}, bf16[352,128]{1,0:T(8,128)(2,1)S(1)}, u32[]{:S(2)}, u32[]{:S(2)}) collective-permute-start(bf16[352,128]{1,0:T(8,128)(2,1)S(1)} %get-tuple-element.207), channel_id=1, source_target_pairs={{0,12},{2,14},{4,8},{6,10},{8,4},{10,6},{12,0},{14,2},{16,28},{18,... | collective-permute-start | bytes 270344 | tf_op jit(solution)/shard_map/cond/branch_4_fun/ppermute | solution.py:328
  18.4 15.1 %collective-permute-start.64 = (bf16[352,128]{1,0:T(8,128)(2,1)S(1)}, bf16[352,128]{1,0:T(8,128)(2,1)S(1)}, u32[]{:S(2)}, u32[]{:S(2)}) collective-permute-start(bf16[352,128]{1,0:T(8,128)(2,1)S(1)} %get-tuple-element.208), channel_id=1, source_target_pairs={{0,26},{2,24},{4,30},{6,28},{8,18},{10,16},{12,22},{14,20},{16,10}... | collective-permute-start | bytes 270344 | tf_op jit(solution)/shard_map/cond/branch_4_fun/ppermute | solution.py:328
  27.7 7.3 %collective-permute-start.65 = (bf16[352,128]{1,0:T(8,128)(2,1)S(1)}, bf16[352,128]{1,0:T(8,128)(2,1)S(1)}, u32[]{:S(2)}, u32[]{:S(2)}) collective-permute-start(bf16[352,128]{1,0:T(8,128)(2,1)S(1)} %get-tuple-element.209), channel_id=1, source_target_pairs={{0,10},{2,8},{4,14},{6,12},{8,2},{10,0},{12,6},{14,4},{16,26},{18,... | collective-permute-start | bytes 270344 | tf_op jit(solution)/shard_map/cond/branch_4_fun/ppermute | solution.py:328
  27.8 9.0 %collective-permute-start.66 = (bf16[352,128]{1,0:T(8,128)(2,1)S(1)}, bf16[352,128]{1,0:T(8,128)(2,1)S(1)}, u32[]{:S(2)}, u32[]{:S(2)}) collective-permute-start(bf16[352,128]{1,0:T(8,128)(2,1)S(1)} %get-tuple-element.210), channel_id=1, source_target_pairs={{0,24},{2,26},{4,28},{6,30},{8,16},{10,18},{12,20},{14,22},{16,8},... | collective-permute-start | bytes 270344 | tf_op jit(solution)/shard_map/cond/branch_4_fun/ppermute | solution.py:328
  28.8 8.5 %collective-permute-start.67 = (bf16[352,128]{1,0:T(8,128)(2,1)S(1)}, bf16[352,128]{1,0:T(8,128)(2,1)S(1)}, u32[]{:S(2)}, u32[]{:S(2)}) collective-permute-start(bf16[352,128]{1,0:T(8,128)(2,1)S(1)} %get-tuple-element.211), channel_id=1, source_target_pairs={{0,8},{2,10},{4,12},{6,14},{8,0},{10,2},{12,4},{14,6},{16,24},{18,... | collective-permute-start | bytes 270344 | tf_op jit(solution)/shard_map/cond/branch_4_fun/ppermute | solution.py:328
  30.5 14.7 %collective-permute-start.68 = (bf16[352,128]{1,0:T(8,128)(2,1)S(1)}, bf16[352,128]{1,0:T(8,128)(2,1)S(1)}, u32[]{:S(2)}, u32[]{:S(2)}) collective-permute-start(bf16[352,128]{1,0:T(8,128)(2,1)S(1)} %get-tuple-element.212), channel_id=1, source_target_pairs={{0,22},{2,20},{4,18},{6,16},{8,30},{10,28},{12,26},{14,24},{16,6},... | collective-permute-start | bytes 270344 | tf_op jit(solution)/shard_map/cond/branch_4_fun/ppermute | solution.py:328
  33.5 11.8 %collective-permute-start.69 = (bf16[352,128]{1,0:T(8,128)(2,1)S(1)}, bf16[352,128]{1,0:T(8,128)(2,1)S(1)}, u32[]{:S(2)}, u32[]{:S(2)}) collective-permute-start(bf16[352,128]{1,0:T(8,128)(2,1)S(1)} %get-tuple-element.213), channel_id=1, source_target_pairs={{0,6},{2,4},{4,2},{6,0},{8,14},{10,12},{12,10},{14,8},{16,22},{18,... | collective-permute-start | bytes 270344 | tf_op jit(solution)/shard_map/cond/branch_4_fun/ppermute | solution.py:328
  34.9 11.1 %collective-permute-start.70 = (bf16[352,128]{1,0:T(8,128)(2,1)S(1)}, bf16[352,128]{1,0:T(8,128)(2,1)S(1)}, u32[]{:S(2)}, u32[]{:S(2)}) collective-permute-start(bf16[352,128]{1,0:T(8,128)(2,1)S(1)} %get-tuple-element.214), channel_id=1, source_target_pairs={{0,20},{2,22},{4,16},{6,18},{8,28},{10,30},{12,24},{14,26},{16,4},... | collective-permute-start | bytes 270344 | tf_op jit(solution)/shard_map/cond/branch_4_fun/ppermute | solution.py:328
  36.8 9.3 %collective-permute-start.71 = (bf16[352,128]{1,0:T(8,128)(2,1)S(1)}, bf16[352,128]{1,0:T(8,128)(2,1)S(1)}, u32[]{:S(2)}, u32[]{:S(2)}) collective-permute-start(bf16[352,128]{1,0:T(8,128)(2,1)S(1)} %get-tuple-element.215), channel_id=1, source_target_pairs={{0,4},{2,6},{4,0},{6,2},{8,12},{10,14},{12,8},{14,10},{16,20},{18,... | collective-permute-start | bytes 270344 | tf_op jit(solution)/shard_map/cond/branch_4_fun/ppermute | solution.py:328
  37.3 12.5 %collective-permute-start.72 = (bf16[352,128]{1,0:T(8,128)(2,1)S(1)}, bf16[352,128]{1,0:T(8,128)(2,1)S(1)}, u32[]{:S(2)}, u32[]{:S(2)}) collective-permute-start(bf16[352,128]{1,0:T(8,128)(2,1)S(1)} %get-tuple-element.216), channel_id=1, source_target_pairs={{0,18},{2,16},{4,22},{6,20},{8,26},{10,24},{12,30},{14,28},{16,2},... | collective-permute-start | bytes 270344 | tf_op jit(solution)/shard_map/cond/branch_4_fun/ppermute | solution.py:328
  45.3 5.0 %collective-permute-start.73 = (bf16[352,128]{1,0:T(8,128)(2,1)S(1)}, bf16[352,128]{1,0:T(8,128)(2,1)S(1)}, u32[]{:S(2)}, u32[]{:S(2)}) collective-permute-start(bf16[352,128]{1,0:T(8,128)(2,1)S(1)} %get-tuple-element.217), channel_id=1, source_target_pairs={{0,2},{2,0},{4,6},{6,4},{8,10},{10,8},{12,14},{14,12},{16,18},{18,... | collective-permute-start | bytes 270344 | tf_op jit(solution)/shard_map/cond/branch_4_fun/ppermute | solution.py:328
  45.3 5.4 %collective-permute-start.74 = (bf16[352,128]{1,0:T(8,128)(2,1)S(1)}, bf16[352,128]{1,0:T(8,128)(2,1)S(1)}, u32[]{:S(2)}, u32[]{:S(2)}) collective-permute-start(bf16[352,128]{1,0:T(8,128)(2,1)S(1)} %get-tuple-element.218), channel_id=1, source_target_pairs={{0,16},{2,18},{4,20},{6,22},{8,24},{10,26},{12,28},{14,30},{16,0},... | collective-permute-start | bytes 270344 | tf_op jit(solution)/shard_map/cond/branch_4_fun/ppermute | solution.py:328
  54.0 0.6 %copy-start.4 = (f32[128,128]{1,0:T(8,128)}, f32[128,128]{1,0:T(8,128)S(1)}, u32[]{:S(2)}) copy-start(f32[128,128]{1,0:T(8,128)S(1)} %get-tuple-element.579) | copy-start | bytes 196612

commit v6 on v4

--- a/solution.py
+++ b/solution.py
@@ -10,23 +10,25 @@
 LANE = 128
 UNROLL = 32
 QUAD = 4
-FIRST = 5
+PARCELS = (
+    ((15,), (1, 5, 3, 7), (14,), (13,)),
+    ((12,), (2,), (6,), (11,), (4,), (10,), (9,), (8,), (0,)),
+)
 STEP = 128
 VMEM_LIMIT = 24 * 1024 * 1024
 LADDER = (32, 38, 40, 42, 44, 46, 56, 144)
 NT = (((1,), (1,)), ((), ()))
 
 
-def exchange_order(count):
-    side = count // 2
-    order = []
-    for i in range(side):
-        order += [count - 1 - i, side - 1 - i]
-    return order
-
-
-def group_ends(count):
-    return (0, FIRST, count)
+def turn_order():
+    return [apart for group in PARCELS for parcel in group for apart in parcel]
+
+
+def group_ends():
+    ends = [0]
+    for group in PARCELS:
+        ends.append(ends[-1] + sum(len(parcel) for parcel in group))
+    return ends
 
 
 def plan_kernel(owner_in, cycle_in, valid_in, *rest):
@@ -86,7 +88,7 @@
     def turn_of(index):
         apart = (index // 2) ^ tm_index
         turn = jnp.zeros_like(apart)
-        for place, each in enumerate(exchange_order(slots // 2)):
+        for place, each in enumerate(turn_order()):
             turn = jnp.where(apart == each, place, turn)
         return turn
 
@@ -142,7 +144,7 @@
     scalar_ref[0] = rung
     scalar_ref[1] = tm_index
     scalar_ref[2] = jnp.sum(jnp.where(slot == own_slot, pixels, 0.0)[:, :1]).astype(jnp.int32)
-    for group, end in enumerate(group_ends(slots // 2)):
+    for group, end in enumerate(group_ends()):
         ahead = jnp.where(turn < end, count * mine, 0.0)
         scalar_ref[3 + group] = jnp.sum(ahead[:, :1]).astype(jnp.int32)
 
@@ -161,10 +163,9 @@
 
 
 def pack_kernel(
-    group, first, block_ref, row_ref, lane_ref, cut_ref, scalar_ref, pool_ref, after_ref, *rest
+    group, first, size, block_ref, row_ref, lane_ref, cut_ref, scalar_ref, pool_ref, after_ref, *rest
 ):
     out_refs, stage = rest[:-1], rest[-1]
-    depth = out_refs[0].shape[0]
     frames = pool_ref.shape[1]
     lane = lax.broadcasted_iota(jnp.int32, (frames, LANE), 1)
     begin, end = scalar_ref[3 + group], scalar_ref[4 + group]
@@ -184,11 +185,12 @@
     held = jnp.zeros((frames, LANE), jnp.float32)
     lax.fori_loop(0, (end - begin + UNROLL - 1) // UNROLL, place, held)
 
-    step = depth if depth <= 512 else LANE
-    for d, out_ref in enumerate(out_refs):
-        base = (first + d) * (depth // frames)
-
-        def narrow(i, _, out_ref=out_ref, base=base):
+    base = first * size
+    for out_ref in out_refs:
+        depth = out_ref.shape[0]
+        step = depth if depth <= 512 else 2 * size * frames // (4 if size % 4 == 0 else 2)
+
+        def narrow(i, _, out_ref=out_ref, base=base, step=step):
             part = stage[pl.ds(base + i * (step // frames), step // frames)].reshape(step, LANE)
             out_ref[pl.ds(pl.multiple_of(i * step, step), step), :] = part.astype(jnp.bfloat16)
             return 0
@@ -197,14 +199,21 @@
             narrow(0, 0)
         else:
             lax.fori_loop(0, depth // step, narrow, 0)
-
-
-def gram_kernel(scalar_ref, *refs):
+        base += depth // frames
+
+
+def join_kernel(picks, *refs):
+    out_ref = refs[-1]
+    depth = out_ref.shape[0] // len(picks)
+    for i, (source, block) in enumerate(picks):
+        out_ref[i * depth : (i + 1) * depth, :] = refs[source][block * depth : (block + 1) * depth, :]
+
+
+def gram_kernel(picks, size, scalar_ref, *refs):
     x_refs, (out_ref, turn, grams, totals) = refs[:-4], refs[-4:]
-    sources = len(x_refs)
     frames = out_ref.shape[0]
-    local = frames // sources
-    last = x_refs[0].shape[0] // (2 * local) - 1
+    local = frames // len(picks)
+    last = size // 2 - 1
     tm_index, pixels = scalar_ref[1], scalar_ref[2]
     lane = lax.broadcasted_iota(jnp.int32, (1, LANE), 1)
     grams[...] = jnp.zeros(grams.shape, jnp.float32)
@@ -215,8 +224,11 @@
         total = totals[...]
         for k in range(QUAD):
             j = QUAD * step + k
-            rows = pl.ds(pl.multiple_of(jnp.minimum(j, last) * 2 * local, 2 * local), 2 * local)
-            both = [ref[rows, :].astype(jnp.float32) for ref in x_refs]
+            row = pl.multiple_of(jnp.minimum(j, last) * 2 * local, 2 * local)
+            both = [
+                x_refs[ref][pl.ds(block * size * local + row, 2 * local), :].astype(jnp.float32)
+                for ref, block, _ in picks
+            ]
             for i in range(2):
                 used = lane + (2 * j + i) * LANE < pixels
                 x = jnp.concatenate([part[i * local : (i + 1) * local] for part in both], axis=0)
@@ -239,11 +251,9 @@
 
     pairs = (pixels + 2 * LANE - 1) // (2 * LANE)
     lax.fori_loop(0, (pairs + QUAD - 1) // QUAD, several, 0)
-    order = exchange_order(sources)
-
     def in_order(value):
-        for j in range(sources):
-            at = pl.multiple_of((tm_index ^ order[j]) * local, local)
+        for j, (_, _, apart) in enumerate(picks):
+            at = pl.multiple_of((tm_index ^ apart) * local, local)
             turn[pl.ds(at, local), :] = value[j * local : (j + 1) * local]
         return turn[...]
 
@@ -259,8 +269,7 @@
     tm_count = lax.axis_size("tm")
     local_frames, half, _ = frames.shape
     frame_count = tm_count * local_frames
-    order = exchange_order(tm_count)
-    ends = group_ends(tm_count)
+    ends = group_ends()
     list_rows = -(-(block_cycle.shape[0] + UNROLL) // (8 * LANE)) * 8
     vmem = pl.BlockSpec(memory_space=pltpu.VMEM)
     smem = pl.BlockSpec(memory_space=pltpu.SMEM)
@@ -301,28 +310,63 @@
         depth = size * local_frames
 
         def run(lists, scalars, pool):
-            got = []
+            def send(parcel, apart):
+                pairs = [(i, i ^ apart) for i in range(tm_count)]
+                return lax.ppermute(parcel, "tm", pairs)
+
+            def join(picks, after, *parts):
+                return pl.pallas_call(
+                    functools.partial(join_kernel, picks),
+                    out_shape=jax.ShapeDtypeStruct((len(picks) * depth, LANE), jnp.bfloat16),
+                    in_specs=[vmem] * len(parts) + [pl.BlockSpec(memory_space=pl.ANY)] * len(after),
+                    out_specs=vmem,
+                    compiler_params=params,
+                    name="join",
+                )(*parts, *after)
+
+            packed, got, picks = {}, [], []
             after = scalars
-            for group, (first, end) in enumerate(zip(ends[:-1], ends[1:])):
-                send = pl.pallas_call(
-                    functools.partial(pack_kernel, group, first),
-                    out_shape=(jax.ShapeDtypeStruct((depth, LANE), jnp.bfloat16),) * (end - first),
+            for group, parcels in enumerate(PARCELS):
+                parts = pl.pallas_call(
+                    functools.partial(pack_kernel, group, ends[group], size),
+                    out_shape=[
+                        jax.ShapeDtypeStruct((len(each) * depth, LANE), jnp.bfloat16)
+                        for each in parcels
+                    ],
                     in_specs=[smem] * 5 + [vmem, pl.BlockSpec(memory_space=pl.ANY)],
-                    out_specs=(vmem,) * (end - first),
+                    out_specs=[vmem] * len(parcels),
                     scratch_shapes=[
                         pltpu.VMEM((tm_count * size + 2, local_frames, LANE), jnp.float32)
                     ],
                     compiler_params=params,
                     name="pack",
                 )(*lists, scalars, pool, after)
-                for part, apart in zip(send, order[first:end]):
-                    pairs = [(i, i ^ apart) for i in range(tm_count)]
-                    got.append(lax.ppermute(part, "tm", pairs) if apart else part)
-                after = got[first]
+                for part, (apart, *_) in zip(parts, parcels):
+                    if apart >= 8:
+                        picks.append((len(got), 0, apart))
+                        got.append(send(part, apart))
+                    else:
+                        packed[apart] = part
+                after = got[1]
+            along_x = send(packed[1], 1)
+            picks_y = ((0, 0), (2, 2), (1, 0), (2, 3))
+            parcel = join(picks_y, (got[0], got[2]), packed[2], packed[6], along_x)
+            along_y = send(parcel, 2)
+            picks_z = ((0, 0), (1, 1), (2, 2), (2, 3))
+            parcel = join(picks_z, (got[3], got[4]), packed[4], along_x, along_y)
+            along_z = send(parcel, 4)
+            for part, sources in (
+                (packed[0], (0,)),
+                (along_x, (1,)),
+                (along_y, (2, 3)),
+                (along_z, (4, 5, 6, 7)),
+            ):
+                picks += [(len(got), block, apart) for block, apart in enumerate(sources)]
+                got.append(part)
             return pl.pallas_call(
-                gram_kernel,
+                functools.partial(gram_kernel, tuple(picks), size),
                 out_shape=jax.ShapeDtypeStruct((frame_count, frame_count), jnp.float32),
-                in_specs=[smem] + [vmem] * tm_count,
+                in_specs=[smem] + [vmem] * len(got),
                 out_specs=vmem,
                 scratch_shapes=[
                     pltpu.VMEM((frame_count, LANE), jnp.float32),

time: 54.7 us -> 57.6 us (1.053)
  waiting for transfers between devices: 10 us -> 12.9 us
    ppermute x15 -> x11, waiting for transfers between devices: 10 us -> 12.9 us  [send(): return lax.ppermute(parcel, 'tm', pairs)]
    pallas_call x3 -> x5, Pallas kernels: 10.6 us -> 11.1 us  [the longest x2 7.8 us: run(): pl.pallas_call(functools.partial(pack_kernel, group, ends[group], size),...]
    ppermute x15 -> x11, starting transfers between devices: 26.8 us -> 26.5 us  [send(): return lax.ppermute(parcel, 'tm', pairs)]
  transfers between devices with their start and end apart: 16 -> 12, of which waited for: 4 -> 5; matrix products, arithmetic and copies ran while one was open for 0% -> 0% of each run, Pallas kernels for 14% -> 12%
where the time goes in v6:
time: 57.6 us; the launch traced here: 57.5 us
  starting transfers between devices  27 us (47%)
  Pallas kernels  14.9 us (26%)
  waiting for transfers between devices  12.9 us (22%)
  local copies, waits for them, and re-layouts  2.3 us (4%)
    ppermute x11, starting transfers between devices, send(): return lax.ppermute(parcel, 'tm', pairs)  26.5 us
    ppermute x11, waiting for transfers between devices, send(): return lax.ppermute(parcel, 'tm', pairs)  12.9 us
    pallas_call x2, Pallas kernels, run(): pl.pallas_call(functools.partial(pack_kernel, group, ends[group], size),...  7.8 us
    pallas_call x1, Pallas kernels, run(): pl.pallas_call(functools.partial(gram_kernel, tuple(picks), size), out_sh...  3.28 us
    unnamed x10, local copies, waits for them, and re-layouts  2.3 us
    pallas_call x2, Pallas kernels, widen(): pl.pallas_call(functools.partial(widen_kernel, part), out_shape=jax.Shape...  1.95 us
    pallas_call x1, Pallas kernels, on_device_routed(): pl.pallas_call(plan_kernel, out_shape=(*[jax.ShapeDtypeStruct((list_rows,...  1.84 us
  transfers between devices with their start and end apart: 12, of which 5 were waited for; matrix products, arithmetic and copies ran while one was open for 0% of the time, Pallas kernels for 12%

profile of v6, /device:TPU:0, one launch (start us, length us, event | category | flops | bytes accessed | tf_op | source)
XLA Modules:
  0.0 57.5 jit_solution(7562225057046345869)
XLA Ops:
  0.0 0.5 collective-permute-start.88
  0.5 1.7 %copy-done = bf16[8,1152,128]{2,1,0:T(8,128)(2,1)S(1)} copy-done((bf16[8,1152,128]{2,1,0:T(8,128)(2,1)S(1)}, bf16[8,1152,128]{2,1,0:T(8,128)(2,1)}, u32[]{:S(2)}) %copy-start) | copy-done | bytes 2359320
  2.1 1.0 %widen.2.rest_0_ = f32[2304,8,128]{2,1,0:T(8,128)S(1)} custom-call(bf16[8,1152,128]{2,1,0:T(8,128)(2,1)S(1)} %copy-done), custom_call_target="tpu_custom_call" | custom-call | tf_op jit(solution)/shard_map/widen/pallas_call | solution.py:279
  3.1 1.8 %plan.1 = (s32[24,128]{1,0:T(8,128)S(1)}, s32[24,128]{1,0:T(8,128)S(1)}, s32[24,128]{1,0:T(8,128)S(1)}, s32[24,128]{1,0:T(8,128)S(1)}, s32[6]{0:T(128)S(1)}) custom-call(s32[32]{0:T(128)S(1)} %copy-done.3, s32[2304]{0:T(1024)S(1)} %copy-done.1, s32[2304]{0:T(1024)S(1)} %copy-done.2), custom_call_target="tpu_custom_call" | custom-call | tf_op jit(solution)/shard_map/plan/pallas_call | solution.py:290
  5.0 0.0 collective-permute-done.88.in_ref
  5.0 1.0 %widen.3 = f32[2304,8,128]{2,1,0:T(8,128)S(1)} custom-call(bf16[8,1152,128]{2,1,0:T(8,128)(2,1)S(1)} %collective-permute-done.88.in_ref, f32[2304,8,128]{2,1,0:T(8,128)S(1)} %widen.2.rest_0_), custom_call_target="tpu_custom_call", output_to_operand_aliasing={{}: (1, {})} | custom-call | tf_op jit(solution)/shard_map/widen/pallas_call | solution.py:279
  6.0 50.9 %conditional.1 = (f32[128,128]{1,0:T(8,128)S(1)}) conditional(s32[]{:T(128)} %bitcast.32, (s32[24,128]{1,0:T(8,128)S(1)}, s32[24,128]{1,0:T(8,128)S(1)}, s32[24,128]{1,0:T(8,128)S(1)}, s32[24,128]{1,0:T(8,128)S(1)}, s32[6]{0:T(128)S(1)}, /*index=5*/f32[2304,8,128]{2,1,0:T(8,128)S(1)}) %tuple.29, ...), branch_computations={%region_0.0_spmd, %region_1.0_spmd, %region_2.0_spmd, %region_3.0_... | conditional | bytes 23593408 | solution.py:382
  6.0 3.6 %pack.22 = (bf16[336,128]{1,0:T(8,128)(2,1)S(1)}, bf16[1344,128]{1,0:T(8,128)(2,1)S(1)}, bf16[336,128]{1,0:T(8,128)(2,1)S(1)}, bf16[336,128]{1,0:T(8,128)(2,1)S(1)}) custom-call(s32[3072]{0:T(1024)S(1)} %bitcast.40, s32[3072]{0:T(1024)S(1)} %bitcast.56, s32[3072]{0:T(1024)S(1)} %bitcast.72, s32[3072]{0:T(1024)S(1)} %bitcast.88, ...), custom_call_target="tpu_custom_call" | custom-call | tf_op jit(solution)/shard_map/cond/branch_3_fun/pack/pallas_call | solution.py:330
  9.6 2.7 %collective-permute-start.41 = (bf16[1344,128]{1,0:T(8,128)(2,1)S(1)}, bf16[1344,128]{1,0:T(8,128)(2,1)S(1)}, u32[]{:S(2)}, u32[]{:S(2)}) collective-permute-start(bf16[1344,128]{1,0:T(8,128)(2,1)S(1)} %get-tuple-element.182), channel_id=1, source_target_pairs={{0,2},{2,0},{4,6},{6,4},{8,10},{10,8},{12,14},{14,12},{16,18},{18,... | collective-permute-start | bytes 1032200 | tf_op jit(solution)/shard_map/cond/branch_3_fun/ppermute | solution.py:315
  12.3 4.6 %collective-permute-start.34 = (bf16[336,128]{1,0:T(8,128)(2,1)S(1)}, bf16[336,128]{1,0:T(8,128)(2,1)S(1)}, u32[]{:S(2)}, u32[]{:S(2)}) collective-permute-start(bf16[336,128]{1,0:T(8,128)(2,1)S(1)} %get-tuple-element.174), channel_id=1, source_target_pairs={{0,28},{2,30},{4,24},{6,26},{8,20},{10,22},{12,16},{14,18},{16,12}... | collective-permute-start | bytes 258056 | tf_op jit(solution)/shard_map/cond/branch_3_fun/ppermute | solution.py:315
  16.9 0.0 collective-permute-start.33
  16.9 4.7 %collective-permute-start.35 = (bf16[336,128]{1,0:T(8,128)(2,1)S(1)}, bf16[336,128]{1,0:T(8,128)(2,1)S(1)}, u32[]{:S(2)}, u32[]{:S(2)}) collective-permute-start(bf16[336,128]{1,0:T(8,128)(2,1)S(1)} %get-tuple-element.175), channel_id=1, source_target_pairs={{0,26},{2,24},{4,30},{6,28},{8,18},{10,16},{12,22},{14,20},{16,10}... | collective-permute-start | bytes 258056 | tf_op jit(solution)/shard_map/cond/branch_3_fun/ppermute | solution.py:315
  21.6 0.0 collective-permute-done.34.after_ref.refs_1_
  21.6 4.2 %pack.23 = (bf16[336,128]{1,0:T(8,128)(2,1)S(1)}, bf16[336,128]{1,0:T(8,128)(2,1)S(1)}, bf16[336,128]{1,0:T(8,128)(2,1)S(1)}, bf16[336,128]{1,0:T(8,128)(2,1)S(1...) custom-call(s32[3072]{0:T(1024)S(1)} %bitcast.41, ...), custom_call_target="tpu_custom_call" | custom-call | tf_op jit(solution)/shard_map/cond/branch_3_fun/pack/pallas_call | solution.py:330
  25.8 0.0 collective-permute-done.33.refs_3_.refs_0_
  25.8 0.0 collective-permute-done.35.refs_4_.refs_2_
  25.8 0.0 collective-permute-done.41.refs_2_.refs_1_.refs_9_
  25.9 1.6 %collective-permute-start.42 = (bf16[1344,128]{1,0:T(8,128)(2,1)S(1)}, bf16[1344,128]{1,0:T(8,128)(2,1)S(1)}, u32[]{:S(2)}, u32[]{:S(2)}) collective-permute-start(bf16[1344,128]{1,0:T(8,128)(2,1)S(1)} %join.22), channel_id=1, source_target_pairs={{0,4},{2,6},{4,0},{6,2},{8,12},{10,14},{12,8},{14,10},{16,20},{18,... | collective-permute-start | bytes 1032200 | tf_op jit(solution)/shard_map/cond/branch_3_fun/ppermute | solution.py:315
  27.5 2.6 %collective-permute-start.36 = (bf16[336,128]{1,0:T(8,128)(2,1)S(1)}, bf16[336,128]{1,0:T(8,128)(2,1)S(1)}, u32[]{:S(2)}, u32[]{:S(2)}) collective-permute-start(bf16[336,128]{1,0:T(8,128)(2,1)S(1)} %get-tuple-element.176), channel_id=1, source_target_pairs={{0,24},{2,26},{4,28},{6,30},{8,16},{10,18},{12,20},{14,22},{16,8},... | collective-permute-start | bytes 258056 | tf_op jit(solution)/shard_map/cond/branch_3_fun/ppermute | solution.py:315
  30.1 2.5 %collective-permute-start.37 = (bf16[336,128]{1,0:T(8,128)(2,1)S(1)}, bf16[336,128]{1,0:T(8,128)(2,1)S(1)}, u32[]{:S(2)}, u32[]{:S(2)}) collective-permute-start(bf16[336,128]{1,0:T(8,128)(2,1)S(1)} %get-tuple-element.177), channel_id=1, source_target_pairs={{0,22},{2,20},{4,18},{6,16},{8,30},{10,28},{12,26},{14,24},{16,6},... | collective-permute-start | bytes 258056 | tf_op jit(solution)/shard_map/cond/branch_3_fun/ppermute | solution.py:315
  32.5 1.3 %collective-permute-done.36.refs_3_ = bf16[336,128]{1,0:T(8,128)(2,1)S(1)} collective-permute-done((bf16[336,128]{1,0:T(8,128)(2,1)S(1)}, bf16[336,128]{1,0:T(8,128)(2,1)S(1)}, u32[]{:S(2)}, u32[]{:S(2)}) %collective-permute-start.36) | collective-permute-done | bytes 86048 | tf_op jit(solution)/shard_map/cond/branch_3_fun/ppermute | solution.py:315
  33.8 3.7 %collective-permute-done.37.refs_4_ = bf16[336,128]{1,0:T(8,128)(2,1)S(1)} collective-permute-done((bf16[336,128]{1,0:T(8,128)(2,1)S(1)}, bf16[336,128]{1,0:T(8,128)(2,1)S(1)}, u32[]{:S(2)}, u32[]{:S(2)}) %collective-permute-start.37) | collective-permute-done | bytes 86048 | tf_op jit(solution)/shard_map/cond/branch_3_fun/ppermute | solution.py:315
  37.6 2.2 %collective-permute-start.43 = (bf16[1344,128]{1,0:T(8,128)(2,1)S(1)}, bf16[1344,128]{1,0:T(8,128)(2,1)S(1)}, u32[]{:S(2)}, u32[]{:S(2)}) collective-permute-start(bf16[1344,128]{1,0:T(8,128)(2,1)S(1)} %join.23), channel_id=1, source_target_pairs={{0,8},{2,10},{4,12},{6,14},{8,0},{10,2},{12,4},{14,6},{16,24},{18,... | collective-permute-start | bytes 1032200 | tf_op jit(solution)/shard_map/cond/branch_3_fun/ppermute | solution.py:315
  39.8 2.8 %collective-permute-start.38 = (bf16[336,128]{1,0:T(8,128)(2,1)S(1)}, bf16[336,128]{1,0:T(8,128)(2,1)S(1)}, u32[]{:S(2)}, u32[]{:S(2)}) collective-permute-start(bf16[336,128]{1,0:T(8,128)(2,1)S(1)} %get-tuple-element.178), channel_id=1, source_target_pairs={{0,20},{2,22},{4,16},{6,18},{8,28},{10,30},{12,24},{14,26},{16,4},... | collective-permute-start | bytes 258056 | tf_op jit(solution)/shard_map/cond/branch_3_fun/ppermute | solution.py:315
  42.6 1.0 %collective-permute-start.39 = (bf16[336,128]{1,0:T(8,128)(2,1)S(1)}, bf16[336,128]{1,0:T(8,128)(2,1)S(1)}, u32[]{:S(2)}, u32[]{:S(2)}) collective-permute-start(bf16[336,128]{1,0:T(8,128)(2,1)S(1)} %get-tuple-element.179), channel_id=1, source_target_pairs={{0,18},{2,16},{4,22},{6,20},{8,26},{10,24},{12,30},{14,28},{16,2},... | collective-permute-start | bytes 258056 | tf_op jit(solution)/shard_map/cond/branch_3_fun/ppermute | solution.py:315
  43.6 1.9 %collective-permute-start.40 = (bf16[336,128]{1,0:T(8,128)(2,1)S(1)}, bf16[336,128]{1,0:T(8,128)(2,1)S(1)}, u32[]{:S(2)}, u32[]{:S(2)}) collective-permute-start(bf16[336,128]{1,0:T(8,128)(2,1)S(1)} %get-tuple-element.180), channel_id=1, source_target_pairs={{0,16},{2,18},{4,20},{6,22},{8,24},{10,26},{12,28},{14,30},{16,0},... | collective-permute-start | bytes 258056 | tf_op jit(solution)/shard_map/cond/branch_3_fun/ppermute | solution.py:315
  45.6 2.7 %collective-permute-done.38.refs_5_ = bf16[336,128]{1,0:T(8,128)(2,1)S(1)} collective-permute-done((bf16[336,128]{1,0:T(8,128)(2,1)S(1)}, bf16[336,128]{1,0:T(8,128)(2,1)S(1)}, u32[]{:S(2)}, u32[]{:S(2)}) %collective-permute-start.38) | collective-permute-done | bytes 86048 | tf_op jit(solution)/shard_map/cond/branch_3_fun/ppermute | solution.py:315
  48.3 2.8 %collective-permute-done.39.refs_6_ = bf16[336,128]{1,0:T(8,128)(2,1)S(1)} collective-permute-done((bf16[336,128]{1,0:T(8,128)(2,1)S(1)}, bf16[336,128]{1,0:T(8,128)(2,1)S(1)}, u32[]{:S(2)}, u32[]{:S(2)}) %collective-permute-start.39) | collective-permute-done | bytes 86048 | tf_op jit(solution)/shard_map/cond/branch_3_fun/ppermute | solution.py:315
  51.1 2.3 %collective-permute-done.40.refs_7_ = bf16[336,128]{1,0:T(8,128)(2,1)S(1)} collective-permute-done((bf16[336,128]{1,0:T(8,128)(2,1)S(1)}, bf16[336,128]{1,0:T(8,128)(2,1)S(1)}, u32[]{:S(2)}, u32[]{:S(2)}) %collective-permute-start.40) | collective-permute-done | bytes 86048 | tf_op jit(solution)/shard_map/cond/branch_3_fun/ppermute | solution.py:315
  53.3 3.3 %gram.11 = f32[128,128]{1,0:T(8,128)S(1)} custom-call(s32[6]{0:T(128)S(1)} %get-tuple-element.167.scalar_ref.after_ref, bf16[336,128]{1,0:T(8,128)(2,1)S(1)} %collective-permute-done.33.refs_3_.refs_0_, bf16[336,128]{1,0:T(8,128)(2,1)S(1)} %collective-permute-done.34.after_ref.refs_1_, bf16[336,128]{1,0:T(8,128)(2,1)S(1)} %collective-permute-done.35.refs_4_.refs_2_, ...), custom_call_target="tpu_custom_call" | custom-call | tf_op jit(solution)/shard_map/cond/branch_3_fun/gram/pallas_call | solution.py:366
  56.9 0.0 copy-start.4
  56.9 0.6 %copy-done.4 = f32[128,128]{1,0:T(8,128)} copy-done((f32[128,128]{1,0:T(8,128)}, f32[128,128]{1,0:T(8,128)S(1)}, u32[]{:S(2)}) %copy-start.4) | copy-done | bytes 65560
  (11 shorter events, 0.1 us)
Async XLA Ops:
  0.0 5.0 %collective-permute-start.88 = (bf16[8,1152,128]{2,1,0:T(8,128)(2,1)}, bf16[8,1152,128]{2,1,0:T(8,128)(2,1)S(1)}, u32[]{:S(2)}, u32[]{:S(2)}) collective-permute-start(bf16[8,1152,128]{2,1,0:T(8,128)(2,1)} %in_ref.1), channel_id=1, source_target_pairs={{0,1},{1,0},{2,3},{3,2},{4,5},{5,4},{6,7},{7,6},{8,9},{9,8},{10,11... | collective-permute-start | bytes 7077896 | tf_op jit(solution)/shard_map/ppermute | solution.py:289
  0.5 1.7 %copy-start = (bf16[8,1152,128]{2,1,0:T(8,128)(2,1)S(1)}, bf16[8,1152,128]{2,1,0:T(8,128)(2,1)}, u32[]{:S(2)}) copy-start(bf16[8,1152,128]{2,1,0:T(8,128)(2,1)} %in_ref.1) | copy-start | bytes 7077892
  2.1 1.0 %copy-start.1 = (s32[2304]{0:T(1024)S(1)}, s32[2304]{0:T(1024)}, u32[]{:S(2)}) copy-start(s32[2304]{0:T(1024)} %cycle_in.1) | copy-start | bytes 27652
  2.1 1.0 %copy-start.2 = (s32[2304]{0:T(1024)S(1)}, s32[2304]{0:T(1024)}, u32[]{:S(2)}) copy-start(s32[2304]{0:T(1024)} %valid_in.1) | copy-start | bytes 27652
  2.1 1.0 %copy-start.3 = (s32[32]{0:T(128)S(1)}, s32[32]{0:T(128)}, u32[]{:S(2)}) copy-start(s32[32]{0:T(128)} %owner_in.1) | copy-start | bytes 388
  9.6 16.2 %collective-permute-start.41 = (bf16[1344,128]{1,0:T(8,128)(2,1)S(1)}, bf16[1344,128]{1,0:T(8,128)(2,1)S(1)}, u32[]{:S(2)}, u32[]{:S(2)}) collective-permute-start(bf16[1344,128]{1,0:T(8,128)(2,1)S(1)} %get-tuple-element.182), channel_id=1, source_target_pairs={{0,2},{2,0},{4,6},{6,4},{8,10},{10,8},{12,14},{14,12},{16,18},{18,... | collective-permute-start | bytes 1032200 | tf_op jit(solution)/shard_map/cond/branch_3_fun/ppermute | solution.py:315
  12.3 9.2 %collective-permute-start.34 = (bf16[336,128]{1,0:T(8,128)(2,1)S(1)}, bf16[336,128]{1,0:T(8,128)(2,1)S(1)}, u32[]{:S(2)}, u32[]{:S(2)}) collective-permute-start(bf16[336,128]{1,0:T(8,128)(2,1)S(1)} %get-tuple-element.174), channel_id=1, source_target_pairs={{0,28},{2,30},{4,24},{6,26},{8,20},{10,22},{12,16},{14,18},{16,12}... | collective-permute-start | bytes 258056 | tf_op jit(solution)/shard_map/cond/branch_3_fun/ppermute | solution.py:315
  16.9 8.9 %collective-permute-start.33 = (bf16[336,128]{1,0:T(8,128)(2,1)S(1)}, bf16[336,128]{1,0:T(8,128)(2,1)S(1)}, u32[]{:S(2)}, u32[]{:S(2)}) collective-permute-start(bf16[336,128]{1,0:T(8,128)(2,1)S(1)} %get-tuple-element.173), channel_id=1, source_target_pairs={{0,30},{2,28},{4,26},{6,24},{8,22},{10,20},{12,18},{14,16},{16,14}... | collective-permute-start | bytes 258056 | tf_op jit(solution)/shard_map/cond/branch_3_fun/ppermute | solution.py:315
  16.9 8.9 %collective-permute-start.35 = (bf16[336,128]{1,0:T(8,128)(2,1)S(1)}, bf16[336,128]{1,0:T(8,128)(2,1)S(1)}, u32[]{:S(2)}, u32[]{:S(2)}) collective-permute-start(bf16[336,128]{1,0:T(8,128)(2,1)S(1)} %get-tuple-element.175), channel_id=1, source_target_pairs={{0,26},{2,24},{4,30},{6,28},{8,18},{10,16},{12,22},{14,20},{16,10}... | collective-permute-start | bytes 258056 | tf_op jit(solution)/shard_map/cond/branch_3_fun/ppermute | solution.py:315
  25.9 11.7 %collective-permute-start.42 = (bf16[1344,128]{1,0:T(8,128)(2,1)S(1)}, bf16[1344,128]{1,0:T(8,128)(2,1)S(1)}, u32[]{:S(2)}, u32[]{:S(2)}) collective-permute-start(bf16[1344,128]{1,0:T(8,128)(2,1)S(1)} %join.22), channel_id=1, source_target_pairs={{0,4},{2,6},{4,0},{6,2},{8,12},{10,14},{12,8},{14,10},{16,20},{18,... | collective-permute-start | bytes 1032200 | tf_op jit(solution)/shard_map/cond/branch_3_fun/ppermute | solution.py:315
  27.5 6.4 %collective-permute-start.36 = (bf16[336,128]{1,0:T(8,128)(2,1)S(1)}, bf16[336,128]{1,0:T(8,128)(2,1)S(1)}, u32[]{:S(2)}, u32[]{:S(2)}) collective-permute-start(bf16[336,128]{1,0:T(8,128)(2,1)S(1)} %get-tuple-element.176), channel_id=1, source_target_pairs={{0,24},{2,26},{4,28},{6,30},{8,16},{10,18},{12,20},{14,22},{16,8},... | collective-permute-start | bytes 258056 | tf_op jit(solution)/shard_map/cond/branch_3_fun/ppermute | solution.py:315
  30.1 7.5 %collective-permute-start.37 = (bf16[336,128]{1,0:T(8,128)(2,1)S(1)}, bf16[336,128]{1,0:T(8,128)(2,1)S(1)}, u32[]{:S(2)}, u32[]{:S(2)}) collective-permute-start(bf16[336,128]{1,0:T(8,128)(2,1)S(1)} %get-tuple-element.177), channel_id=1, source_target_pairs={{0,22},{2,20},{4,18},{6,16},{8,30},{10,28},{12,26},{14,24},{16,6},... | collective-permute-start | bytes 258056 | tf_op jit(solution)/shard_map/cond/branch_3_fun/ppermute | solution.py:315
  37.6 15.7 %collective-permute-start.43 = (bf16[1344,128]{1,0:T(8,128)(2,1)S(1)}, bf16[1344,128]{1,0:T(8,128)(2,1)S(1)}, u32[]{:S(2)}, u32[]{:S(2)}) collective-permute-start(bf16[1344,128]{1,0:T(8,128)(2,1)S(1)} %join.23), channel_id=1, source_target_pairs={{0,8},{2,10},{4,12},{6,14},{8,0},{10,2},{12,4},{14,6},{16,24},{18,... | collective-permute-start | bytes 1032200 | tf_op jit(solution)/shard_map/cond/branch_3_fun/ppermute | solution.py:315
  39.8 8.5 %collective-permute-start.38 = (bf16[336,128]{1,0:T(8,128)(2,1)S(1)}, bf16[336,128]{1,0:T(8,128)(2,1)S(1)}, u32[]{:S(2)}, u32[]{:S(2)}) collective-permute-start(bf16[336,128]{1,0:T(8,128)(2,1)S(1)} %get-tuple-element.178), channel_id=1, source_target_pairs={{0,20},{2,22},{4,16},{6,18},{8,28},{10,30},{12,24},{14,26},{16,4},... | collective-permute-start | bytes 258056 | tf_op jit(solution)/shard_map/cond/branch_3_fun/ppermute | solution.py:315
  42.6 8.4 %collective-permute-start.39 = (bf16[336,128]{1,0:T(8,128)(2,1)S(1)}, bf16[336,128]{1,0:T(8,128)(2,1)S(1)}, u32[]{:S(2)}, u32[]{:S(2)}) collective-permute-start(bf16[336,128]{1,0:T(8,128)(2,1)S(1)} %get-tuple-element.179), channel_id=1, source_target_pairs={{0,18},{2,16},{4,22},{6,20},{8,26},{10,24},{12,30},{14,28},{16,2},... | collective-permute-start | bytes 258056 | tf_op jit(solution)/shard_map/cond/branch_3_fun/ppermute | solution.py:315
  43.6 9.7 %collective-permute-start.40 = (bf16[336,128]{1,0:T(8,128)(2,1)S(1)}, bf16[336,128]{1,0:T(8,128)(2,1)S(1)}, u32[]{:S(2)}, u32[]{:S(2)}) collective-permute-start(bf16[336,128]{1,0:T(8,128)(2,1)S(1)} %get-tuple-element.180), channel_id=1, source_target_pairs={{0,16},{2,18},{4,20},{6,22},{8,24},{10,26},{12,28},{14,30},{16,0},... | collective-permute-start | bytes 258056 | tf_op jit(solution)/shard_map/cond/branch_3_fun/ppermute | solution.py:315
  56.9 0.6 %copy-start.4 = (f32[128,128]{1,0:T(8,128)}, f32[128,128]{1,0:T(8,128)S(1)}, u32[]{:S(2)}) copy-start(f32[128,128]{1,0:T(8,128)S(1)} %get-tuple-element.491) | copy-start | bytes 196612

commit v7 on v1

--- a/solution.py
+++ b/solution.py
@@ -10,9 +10,10 @@
 LANE = 128
 UNROLL = 32
 FIRST = 5
+QUAD = 4
 STEP = 128
 VMEM_LIMIT = 24 * 1024 * 1024
-LADDER = (24, 32, 36, 40, 42, 44, 46, 50, 64, 96, 144)
+LADDER = (32, 38, 40, 42, 44, 46, 56, 144)
 NT = (((1,), (1,)), ((), ()))
 
 
@@ -197,43 +198,45 @@
 
 
 def gram_kernel(scalar_ref, *refs):
-    x_refs, (out_ref, turn) = refs[:-2], refs[-2:]
+    x_refs, (out_ref, turn, grams, totals) = refs[:-4], refs[-4:]
     sources = len(x_refs)
     frames = out_ref.shape[0]
     local = frames // sources
-    pixels = scalar_ref[2]
-    tm_index = scalar_ref[1]
+    last = x_refs[0].shape[0] // (2 * local) - 1
+    tm_index, pixels = scalar_ref[1], scalar_ref[2]
     lane = lax.broadcasted_iota(jnp.int32, (1, LANE), 1)
-
-    last = x_refs[0].shape[0] // (2 * local) - 1
-
-    def pair(j, carry):
-        gram, total = carry
-        rows = pl.ds(pl.multiple_of(jnp.minimum(j, last) * 2 * local, 2 * local), 2 * local)
-        both = [ref[rows, :].astype(jnp.float32) for ref in x_refs]
+    grams[...] = jnp.zeros(grams.shape, jnp.float32)
+    totals[...] = jnp.zeros(totals.shape, jnp.float32)
+
+    def several(step, _):
         exact, high, low = [], [], []
-        for i in range(2):
-            used = lane + (2 * j + i) * LANE < pixels
-            x = jnp.concatenate([part[i * local : (i + 1) * local] for part in both], axis=0)
-            x = jnp.where(used, x, 0.0)
-            mean = jnp.where(used, jnp.sum(x, axis=0, keepdims=True) / frames, 1.0)
-            scale = 1.0 / mean
-            total = total + x * scale
-            y = x * (scale * scale)
-            top = y.astype(jnp.bfloat16)
-            exact.append(x.astype(jnp.bfloat16))
-            high.append(top)
-            low.append((y - top.astype(jnp.float32)).astype(jnp.bfloat16))
+        total = totals[...]
+        for k in range(QUAD):
+            j = QUAD * step + k
+            rows = pl.ds(pl.multiple_of(jnp.minimum(j, last) * 2 * local, 2 * local), 2 * local)
+            both = [ref[rows, :].astype(jnp.float32) for ref in x_refs]
+            for i in range(2):
+                used = lane + (2 * j + i) * LANE < pixels
+                x = jnp.concatenate([part[i * local : (i + 1) * local] for part in both], axis=0)
+                x = jnp.where(used, x, 0.0)
+                mean = jnp.where(used, jnp.sum(x, axis=0, keepdims=True) / frames, 1.0)
+                scale = 1.0 / mean
+                total = total + x * scale
+                y = x * (scale * scale)
+                top = y.astype(jnp.bfloat16)
+                exact.append(x.astype(jnp.bfloat16))
+                high.append(top)
+                low.append((y - top.astype(jnp.float32)).astype(jnp.bfloat16))
+        totals[...] = total
         left = jnp.concatenate(exact, axis=1)
         right = jnp.concatenate(
             [jnp.concatenate(high, axis=1), jnp.concatenate(low, axis=1)], axis=0
         )
-        gram = gram + lax.dot_general(left, right, NT, preferred_element_type=jnp.float32)
-        return gram, total
-
-    def two_pairs(j, carry):
-        return pair(2 * j + 1, pair(2 * j, carry))
-
+        grams[...] += lax.dot_general(left, right, NT, preferred_element_type=jnp.float32)
+        return 0
+
+    pairs = (pixels + 2 * LANE - 1) // (2 * LANE)
+    lax.fori_loop(0, (pairs + QUAD - 1) // QUAD, several, 0)
     order = exchange_order(sources)
 
     def in_order(value):
@@ -242,12 +245,9 @@
             turn[pl.ds(at, local), :] = value[j * local : (j + 1) * local]
         return turn[...]
 
-    carry = (jnp.zeros((frames, 2 * frames), jnp.float32), jnp.zeros((frames, LANE), jnp.float32))
-    pairs = (pixels + 2 * LANE - 1) // (2 * LANE)
-    gram, total = lax.fori_loop(0, (pairs + 1) // 2, two_pairs, carry)
-    gram = in_order(gram[:, :frames] + gram[:, frames:])
+    gram = in_order(grams[:, :frames] + grams[:, frames:])
     gram = in_order(gram.T)
-    total = in_order(total)
+    total = in_order(totals[...])
     first = jnp.sum(total, axis=1, keepdims=True)
     second = jnp.sum(total.T, axis=0, keepdims=True)
     out_ref[...] = pixels.astype(jnp.float32) * gram / (first * second)
@@ -326,7 +326,11 @@
                 out_shape=jax.ShapeDtypeStruct((frame_count, frame_count), jnp.float32),
                 in_specs=[smem] + [vmem] * tm_count,
                 out_specs=vmem,
-                scratch_shapes=[pltpu.VMEM((frame_count, LANE), jnp.float32)],
+                scratch_shapes=[
+                    pltpu.VMEM((frame_count, LANE), jnp.float32),
+                    pltpu.VMEM((frame_count, 2 * frame_count), jnp.float32),
+                    pltpu.VMEM((frame_count, LANE), jnp.float32),
+                ],
                 compiler_params=params,
                 name="gram",
             )(scalars, *got)

time: 54.5 us -> 53.4 us (0.980)
  Pallas kernels: 15 us -> 14.2 us
    pallas_call x1, Pallas kernels: 3.55 us -> 2.83 us  [run(): pl.pallas_call(gram_kernel, out_shape=jax.ShapeDtypeStruct((frame_count,...]
where the time goes in v7:
time: 53.4 us; the launch traced here: 53.3 us
  starting transfers between devices  29 us (54%)
  Pallas kernels  14.2 us (27%)
  waiting for transfers between devices  7.34 us (14%)
  local copies, waits for them, and re-layouts  2.3 us (4%)
    ppermute x15, starting transfers between devices, run(): got.append(lax.ppermute(part, 'tm', pairs) if apart else part)  28.5 us
    pallas_call x2, Pallas kernels, run(): pl.pallas_call(functools.partial(pack_kernel, group, first), out_shape=(j...  7.62 us
    ppermute x15, waiting for transfers between devices, run(): got.append(lax.ppermute(part, 'tm', pairs) if apart else part)  7.33 us
    pallas_call x1, Pallas kernels, run(): pl.pallas_call(gram_kernel, out_shape=jax.ShapeDtypeStruct((frame_count,...  2.83 us
    unnamed x10, local copies, waits for them, and re-layouts  2.3 us
    pallas_call x2, Pallas kernels, widen(): pl.pallas_call(functools.partial(widen_kernel, len(given) - 1), out_shape...  1.95 us
    pallas_call x1, Pallas kernels, on_device_routed(): pl.pallas_call(plan_kernel, out_shape=(jax.ShapeDtypeStruct((list_rows, L...  1.83 us
  transfers between devices with their start and end apart: 16, of which 4 were waited for; matrix products, arithmetic and copies ran while one was open for 0% of the time, Pallas kernels for 14%

profile of v7, /device:TPU:0, one launch (start us, length us, event | category | flops | bytes accessed | tf_op | source)
XLA Modules:
  0.0 53.3 jit_solution(18006719042817246703)
XLA Ops:
  0.0 0.5 collective-permute-start.120
  0.5 1.7 %copy-done = bf16[8,1152,128]{2,1,0:T(8,128)(2,1)S(1)} copy-done((bf16[8,1152,128]{2,1,0:T(8,128)(2,1)S(1)}, bf16[8,1152,128]{2,1,0:T(8,128)(2,1)}, u32[]{:S(2)}) %copy-start) | copy-done | bytes 2359320
  2.1 1.0 %widen.2.rest_0_ = f32[2304,8,128]{2,1,0:T(8,128)S(1)} custom-call(bf16[8,1152,128]{2,1,0:T(8,128)(2,1)S(1)} %copy-done), custom_call_target="tpu_custom_call" | custom-call | tf_op jit(solution)/shard_map/widen/pallas_call | solution.py:268
  3.1 1.8 %plan.1 = (s32[24,128]{1,0:T(8,128)S(1)}, s32[6]{0:T(128)S(1)}) custom-call(s32[32]{0:T(128)S(1)} %copy-done.3, s32[2304]{0:T(1024)S(1)} %copy-done.1, s32[2304]{0:T(1024)S(1)} %copy-done.2), custom_call_target="tpu_custom_call" | custom-call | tf_op jit(solution)/shard_map/plan/pallas_call | solution.py:279
  5.0 0.0 collective-permute-done.120.in_ref
  5.0 1.0 %widen.3 = f32[2304,8,128]{2,1,0:T(8,128)S(1)} custom-call(bf16[8,1152,128]{2,1,0:T(8,128)(2,1)S(1)} %collective-permute-done.120.in_ref, f32[2304,8,128]{2,1,0:T(8,128)S(1)} %widen.2.rest_0_), custom_call_target="tpu_custom_call", output_to_operand_aliasing={{}: (1, {})} | custom-call | tf_op jit(solution)/shard_map/widen/pallas_call | solution.py:268
  6.0 46.6 %conditional.1 = (f32[128,128]{1,0:T(8,128)S(1)}) conditional(s32[]{:T(128)} %bitcast.8, (s32[24,128]{1,0:T(8,128)S(1)}, s32[6]{0:T(128)S(1)}, f32[2304,8,128]{2,1,0:T(8,128)S(1)}) %tuple.29, (s32[24,128]{1,0:T(8,128)S(1)}, s32[6]{0:T(128)S(1)}, f32[2304,8,128]{2,1,0:T(8,128)S(1)}) %tuple.29, ...), branch_computations={%region_0.0_spmd, %region_1.0_spmd, %region_2.0_spmd, %region_3.0_... | conditional | flops 4000000 | bytes 49695328 | solution.py:340
  6.0 2.7 %pack.22 = (bf16[336,128]{1,0:T(8,128)(2,1)S(1)}, bf16[336,128]{1,0:T(8,128)(2,1)S(1)}, bf16[336,128]{1,0:T(8,128)(2,1)S(1)}, bf16[336,128]{1,0:T(8,128)(2,1)S(1)}, bf16[336,128]{1,0:T(8,128)(2,1)S(1)}) custom-call(s32[3072]{0:T(1024)S(1)} %bitcast.16, s32[6]{0:T(128)S(1)} %get-tuple-element.119.scalar_ref.after_ref, ...), custom_call_target="tpu_custom_call" | custom-call | flops 2000000 | bytes 16000000 | tf_op jit(solution)/shard_map/cond/branch_3_fun/pack/pallas_call | solution.py:306
  8.8 6.7 %collective-permute-start.45 = (bf16[336,128]{1,0:T(8,128)(2,1)S(1)}, bf16[336,128]{1,0:T(8,128)(2,1)S(1)}, u32[]{:S(2)}, u32[]{:S(2)}) collective-permute-start(bf16[336,128]{1,0:T(8,128)(2,1)S(1)} %get-tuple-element.122), channel_id=1, source_target_pairs={{0,30},{2,28},{4,26},{6,24},{8,22},{10,20},{12,18},{14,16},{16,14}... | collective-permute-start | bytes 258056 | tf_op jit(solution)/shard_map/cond/branch_3_fun/ppermute | solution.py:322
  15.5 0.2 collective-permute-start.46
  15.7 3.6 %collective-permute-start.47 = (bf16[336,128]{1,0:T(8,128)(2,1)S(1)}, bf16[336,128]{1,0:T(8,128)(2,1)S(1)}, u32[]{:S(2)}, u32[]{:S(2)}) collective-permute-start(bf16[336,128]{1,0:T(8,128)(2,1)S(1)} %get-tuple-element.124), channel_id=1, source_target_pairs={{0,26},{2,24},{4,30},{6,28},{8,18},{10,16},{12,22},{14,20},{16,10}... | collective-permute-start | bytes 258056 | tf_op jit(solution)/shard_map/cond/branch_3_fun/ppermute | solution.py:322
  19.2 0.0 collective-permute-start.48
  19.2 1.0 %collective-permute-start.49 = (bf16[336,128]{1,0:T(8,128)(2,1)S(1)}, bf16[336,128]{1,0:T(8,128)(2,1)S(1)}, u32[]{:S(2)}, u32[]{:S(2)}) collective-permute-start(bf16[336,128]{1,0:T(8,128)(2,1)S(1)} %get-tuple-element.126), channel_id=1, source_target_pairs={{0,24},{2,26},{4,28},{6,30},{8,16},{10,18},{12,20},{14,22},{16,8},... | collective-permute-start | bytes 258056 | tf_op jit(solution)/shard_map/cond/branch_3_fun/ppermute | solution.py:322
  20.2 4.9 %pack.23 = (bf16[336,128]{1,0:T(8,128)(2,1)S(1)}, bf16[336,128]{1,0:T(8,128)(2,1)S(1)}, bf16[336,128]{1,0:T(8,128)(2,1)S(1)}, bf16[336,128]{1,0:T(8,128)(2,1)S(1...) custom-call(s32[3072]{0:T(1024)S(1)} %bitcast.17, ...), custom_call_target="tpu_custom_call" | custom-call | flops 2000000 | bytes 16000000 | tf_op jit(solution)/shard_map/cond/branch_3_fun/pack/pallas_call | solution.py:306
  25.1 4.4 %collective-permute-start.50 = (bf16[336,128]{1,0:T(8,128)(2,1)S(1)}, bf16[336,128]{1,0:T(8,128)(2,1)S(1)}, u32[]{:S(2)}, u32[]{:S(2)}) collective-permute-start(bf16[336,128]{1,0:T(8,128)(2,1)S(1)} %get-tuple-element.127), channel_id=1, source_target_pairs={{0,12},{2,14},{4,8},{6,10},{8,4},{10,6},{12,0},{14,2},{16,28},{18,... | collective-permute-start | bytes 258056 | tf_op jit(solution)/shard_map/cond/branch_3_fun/ppermute | solution.py:322
  29.5 2.6 %collective-permute-start.51 = (bf16[336,128]{1,0:T(8,128)(2,1)S(1)}, bf16[336,128]{1,0:T(8,128)(2,1)S(1)}, u32[]{:S(2)}, u32[]{:S(2)}) collective-permute-start(bf16[336,128]{1,0:T(8,128)(2,1)S(1)} %get-tuple-element.128), channel_id=1, source_target_pairs={{0,22},{2,20},{4,18},{6,16},{8,30},{10,28},{12,26},{14,24},{16,6},... | collective-permute-start | bytes 258056 | tf_op jit(solution)/shard_map/cond/branch_3_fun/ppermute | solution.py:322
  32.1 0.0 collective-permute-done.47.refs_2_
  32.1 1.3 %collective-permute-start.52 = (bf16[336,128]{1,0:T(8,128)(2,1)S(1)}, bf16[336,128]{1,0:T(8,128)(2,1)S(1)}, u32[]{:S(2)}, u32[]{:S(2)}) collective-permute-start(bf16[336,128]{1,0:T(8,128)(2,1)S(1)} %get-tuple-element.129), channel_id=1, source_target_pairs={{0,10},{2,8},{4,14},{6,12},{8,2},{10,0},{12,6},{14,4},{16,26},{18,... | collective-permute-start | bytes 258056 | tf_op jit(solution)/shard_map/cond/branch_3_fun/ppermute | solution.py:322
  33.4 0.9 %collective-permute-start.53 = (bf16[336,128]{1,0:T(8,128)(2,1)S(1)}, bf16[336,128]{1,0:T(8,128)(2,1)S(1)}, u32[]{:S(2)}, u32[]{:S(2)}) collective-permute-start(bf16[336,128]{1,0:T(8,128)(2,1)S(1)} %get-tuple-element.130), channel_id=1, source_target_pairs={{0,20},{2,22},{4,16},{6,18},{8,28},{10,30},{12,24},{14,26},{16,4},... | collective-permute-start | bytes 258056 | tf_op jit(solution)/shard_map/cond/branch_3_fun/ppermute | solution.py:322
  34.3 0.0 collective-permute-done.49.refs_4_
  34.3 2.0 %collective-permute-start.54 = (bf16[336,128]{1,0:T(8,128)(2,1)S(1)}, bf16[336,128]{1,0:T(8,128)(2,1)S(1)}, u32[]{:S(2)}, u32[]{:S(2)}) collective-permute-start(bf16[336,128]{1,0:T(8,128)(2,1)S(1)} %get-tuple-element.131), channel_id=1, source_target_pairs={{0,8},{2,10},{4,12},{6,14},{8,0},{10,2},{12,4},{14,6},{16,24},{18,... | collective-permute-start | bytes 258056 | tf_op jit(solution)/shard_map/cond/branch_3_fun/ppermute | solution.py:322
  36.3 2.6 %collective-permute-start.55 = (bf16[336,128]{1,0:T(8,128)(2,1)S(1)}, bf16[336,128]{1,0:T(8,128)(2,1)S(1)}, u32[]{:S(2)}, u32[]{:S(2)}) collective-permute-start(bf16[336,128]{1,0:T(8,128)(2,1)S(1)} %get-tuple-element.132), channel_id=1, source_target_pairs={{0,18},{2,16},{4,22},{6,20},{8,26},{10,24},{12,30},{14,28},{16,2},... | collective-permute-start | bytes 258056 | tf_op jit(solution)/shard_map/cond/branch_3_fun/ppermute | solution.py:322
  38.9 1.2 %collective-permute-done.51.refs_6_ = bf16[336,128]{1,0:T(8,128)(2,1)S(1)} collective-permute-done((bf16[336,128]{1,0:T(8,128)(2,1)S(1)}, bf16[336,128]{1,0:T(8,128)(2,1)S(1)}, u32[]{:S(2)}, u32[]{:S(2)}) %collective-permute-start.51) | collective-permute-done | bytes 86048 | tf_op jit(solution)/shard_map/cond/branch_3_fun/ppermute | solution.py:322
  40.1 0.9 %collective-permute-start.57 = (bf16[336,128]{1,0:T(8,128)(2,1)S(1)}, bf16[336,128]{1,0:T(8,128)(2,1)S(1)}, u32[]{:S(2)}, u32[]{:S(2)}) collective-permute-start(bf16[336,128]{1,0:T(8,128)(2,1)S(1)} %get-tuple-element.134), channel_id=1, source_target_pairs={{0,16},{2,18},{4,20},{6,22},{8,24},{10,26},{12,28},{14,30},{16,0},... | collective-permute-start | bytes 258056 | tf_op jit(solution)/shard_map/cond/branch_3_fun/ppermute | solution.py:322
  40.9 3.6 %collective-permute-done.53.refs_8_ = bf16[336,128]{1,0:T(8,128)(2,1)S(1)} collective-permute-done((bf16[336,128]{1,0:T(8,128)(2,1)S(1)}, bf16[336,128]{1,0:T(8,128)(2,1)S(1)}, u32[]{:S(2)}, u32[]{:S(2)}) %collective-permute-start.53) | collective-permute-done | bytes 86048 | tf_op jit(solution)/shard_map/cond/branch_3_fun/ppermute | solution.py:322
  44.6 0.5 collective-permute-start.58
  45.1 2.0 %collective-permute-start.59 = (bf16[336,128]{1,0:T(8,128)(2,1)S(1)}, bf16[336,128]{1,0:T(8,128)(2,1)S(1)}, u32[]{:S(2)}, u32[]{:S(2)}) collective-permute-start(bf16[336,128]{1,0:T(8,128)(2,1)S(1)} %get-tuple-element.136), channel_id=1, source_target_pairs={{0,2},{2,0},{4,6},{6,4},{8,10},{10,8},{12,14},{14,12},{16,18},{18,... | collective-permute-start | bytes 258056 | tf_op jit(solution)/shard_map/cond/branch_3_fun/ppermute | solution.py:322
  47.1 2.0 %collective-permute-done.58.refs_13_ = bf16[336,128]{1,0:T(8,128)(2,1)S(1)} collective-permute-done((bf16[336,128]{1,0:T(8,128)(2,1)S(1)}, bf16[336,128]{1,0:T(8,128)(2,1)S(1)}, u32[]{:S(2)}, u32[]{:S(2)}) %collective-permute-start.58) | collective-permute-done | bytes 86048 | tf_op jit(solution)/shard_map/cond/branch_3_fun/ppermute | solution.py:322
  49.1 0.5 collective-permute-done.59.refs_14_
  49.6 2.8 %gram.11 = f32[128,128]{1,0:T(8,128)S(1)} custom-call(s32[6]{0:T(128)S(1)} %get-tuple-element.119.scalar_ref.after_ref, bf16[336,128]{1,0:T(8,128)(2,1)S(1)} %collective-permute-done.45.after_ref.refs_0_, bf16[336,128]{1,0:T(8,128)(2,1)S(1)} %collective-permute-done.46.refs_1_, bf16[336,128]{1,0:T(8,128)(2,1)S(1)} %collective-permute-done.47.refs_2_, ...), custom_call_target="tpu_custom_call" | custom-call | tf_op jit(solution)/shard_map/cond/branch_3_fun/gram/pallas_call | solution.py:324
  52.6 0.0 copy-start.4
  52.6 0.6 %copy-done.4 = f32[128,128]{1,0:T(8,128)} copy-done((f32[128,128]{1,0:T(8,128)}, f32[128,128]{1,0:T(8,128)S(1)}, u32[]{:S(2)}) %copy-start.4) | copy-done | bytes 65560
  (17 shorter events, 0.0 us)
Async XLA Ops:
  0.0 5.0 %collective-permute-start.120 = (bf16[8,1152,128]{2,1,0:T(8,128)(2,1)}, bf16[8,1152,128]{2,1,0:T(8,128)(2,1)S(1)}, u32[]{:S(2)}, u32[]{:S(2)}) collective-permute-start(bf16[8,1152,128]{2,1,0:T(8,128)(2,1)} %in_ref.1), channel_id=1, source_target_pairs={{0,1},{1,0},{2,3},{3,2},{4,5},{5,4},{6,7},{7,6},{8,9},{9,8},{10,11... | collective-permute-start | bytes 7077896 | tf_op jit(solution)/shard_map/ppermute | solution.py:278
  0.5 1.7 %copy-start = (bf16[8,1152,128]{2,1,0:T(8,128)(2,1)S(1)}, bf16[8,1152,128]{2,1,0:T(8,128)(2,1)}, u32[]{:S(2)}) copy-start(bf16[8,1152,128]{2,1,0:T(8,128)(2,1)} %in_ref.1) | copy-start | bytes 7077892
  2.1 1.0 %copy-start.1 = (s32[2304]{0:T(1024)S(1)}, s32[2304]{0:T(1024)}, u32[]{:S(2)}) copy-start(s32[2304]{0:T(1024)} %cycle_in.1) | copy-start | bytes 27652
  2.1 1.0 %copy-start.2 = (s32[2304]{0:T(1024)S(1)}, s32[2304]{0:T(1024)}, u32[]{:S(2)}) copy-start(s32[2304]{0:T(1024)} %valid_in.1) | copy-start | bytes 27652
  2.1 1.0 %copy-start.3 = (s32[32]{0:T(128)S(1)}, s32[32]{0:T(128)}, u32[]{:S(2)}) copy-start(s32[32]{0:T(128)} %owner_in.1) | copy-start | bytes 388
  8.8 11.4 %collective-permute-start.45 = (bf16[336,128]{1,0:T(8,128)(2,1)S(1)}, bf16[336,128]{1,0:T(8,128)(2,1)S(1)}, u32[]{:S(2)}, u32[]{:S(2)}) collective-permute-start(bf16[336,128]{1,0:T(8,128)(2,1)S(1)} %get-tuple-element.122), channel_id=1, source_target_pairs={{0,30},{2,28},{4,26},{6,24},{8,22},{10,20},{12,18},{14,16},{16,14}... | collective-permute-start | bytes 258056 | tf_op jit(solution)/shard_map/cond/branch_3_fun/ppermute | solution.py:322
  15.5 14.0 %collective-permute-start.46 = (bf16[336,128]{1,0:T(8,128)(2,1)S(1)}, bf16[336,128]{1,0:T(8,128)(2,1)S(1)}, u32[]{:S(2)}, u32[]{:S(2)}) collective-permute-start(bf16[336,128]{1,0:T(8,128)(2,1)S(1)} %get-tuple-element.123), channel_id=1, source_target_pairs={{0,28},{2,30},{4,24},{6,26},{8,20},{10,22},{12,16},{14,18},{16,12}... | collective-permute-start | bytes 258056 | tf_op jit(solution)/shard_map/cond/branch_3_fun/ppermute | solution.py:322
  15.7 16.5 %collective-permute-start.47 = (bf16[336,128]{1,0:T(8,128)(2,1)S(1)}, bf16[336,128]{1,0:T(8,128)(2,1)S(1)}, u32[]{:S(2)}, u32[]{:S(2)}) collective-permute-start(bf16[336,128]{1,0:T(8,128)(2,1)S(1)} %get-tuple-element.124), channel_id=1, source_target_pairs={{0,26},{2,24},{4,30},{6,28},{8,18},{10,16},{12,22},{14,20},{16,10}... | collective-permute-start | bytes 258056 | tf_op jit(solution)/shard_map/cond/branch_3_fun/ppermute | solution.py:322
  19.2 14.2 %collective-permute-start.48 = (bf16[336,128]{1,0:T(8,128)(2,1)S(1)}, bf16[336,128]{1,0:T(8,128)(2,1)S(1)}, u32[]{:S(2)}, u32[]{:S(2)}) collective-permute-start(bf16[336,128]{1,0:T(8,128)(2,1)S(1)} %get-tuple-element.125), channel_id=1, source_target_pairs={{0,14},{2,12},{4,10},{6,8},{8,6},{10,4},{12,2},{14,0},{16,30},{18,... | collective-permute-start | bytes 258056 | tf_op jit(solution)/shard_map/cond/branch_3_fun/ppermute | solution.py:322
  19.2 15.1 %collective-permute-start.49 = (bf16[336,128]{1,0:T(8,128)(2,1)S(1)}, bf16[336,128]{1,0:T(8,128)(2,1)S(1)}, u32[]{:S(2)}, u32[]{:S(2)}) collective-permute-start(bf16[336,128]{1,0:T(8,128)(2,1)S(1)} %get-tuple-element.126), channel_id=1, source_target_pairs={{0,24},{2,26},{4,28},{6,30},{8,16},{10,18},{12,20},{14,22},{16,8},... | collective-permute-start | bytes 258056 | tf_op jit(solution)/shard_map/cond/branch_3_fun/ppermute | solution.py:322
  25.1 11.2 %collective-permute-start.50 = (bf16[336,128]{1,0:T(8,128)(2,1)S(1)}, bf16[336,128]{1,0:T(8,128)(2,1)S(1)}, u32[]{:S(2)}, u32[]{:S(2)}) collective-permute-start(bf16[336,128]{1,0:T(8,128)(2,1)S(1)} %get-tuple-element.127), channel_id=1, source_target_pairs={{0,12},{2,14},{4,8},{6,10},{8,4},{10,6},{12,0},{14,2},{16,28},{18,... | collective-permute-start | bytes 258056 | tf_op jit(solution)/shard_map/cond/branch_3_fun/ppermute | solution.py:322
  29.5 10.5 %collective-permute-start.51 = (bf16[336,128]{1,0:T(8,128)(2,1)S(1)}, bf16[336,128]{1,0:T(8,128)(2,1)S(1)}, u32[]{:S(2)}, u32[]{:S(2)}) collective-permute-start(bf16[336,128]{1,0:T(8,128)(2,1)S(1)} %get-tuple-element.128), channel_id=1, source_target_pairs={{0,22},{2,20},{4,18},{6,16},{8,30},{10,28},{12,26},{14,24},{16,6},... | collective-permute-start | bytes 258056 | tf_op jit(solution)/shard_map/cond/branch_3_fun/ppermute | solution.py:322
  32.1 7.9 %collective-permute-start.52 = (bf16[336,128]{1,0:T(8,128)(2,1)S(1)}, bf16[336,128]{1,0:T(8,128)(2,1)S(1)}, u32[]{:S(2)}, u32[]{:S(2)}) collective-permute-start(bf16[336,128]{1,0:T(8,128)(2,1)S(1)} %get-tuple-element.129), channel_id=1, source_target_pairs={{0,10},{2,8},{4,14},{6,12},{8,2},{10,0},{12,6},{14,4},{16,26},{18,... | collective-permute-start | bytes 258056 | tf_op jit(solution)/shard_map/cond/branch_3_fun/ppermute | solution.py:322
  33.4 11.2 %collective-permute-start.53 = (bf16[336,128]{1,0:T(8,128)(2,1)S(1)}, bf16[336,128]{1,0:T(8,128)(2,1)S(1)}, u32[]{:S(2)}, u32[]{:S(2)}) collective-permute-start(bf16[336,128]{1,0:T(8,128)(2,1)S(1)} %get-tuple-element.130), channel_id=1, source_target_pairs={{0,20},{2,22},{4,16},{6,18},{8,28},{10,30},{12,24},{14,26},{16,4},... | collective-permute-start | bytes 258056 | tf_op jit(solution)/shard_map/cond/branch_3_fun/ppermute | solution.py:322
  34.3 10.7 %collective-permute-start.54 = (bf16[336,128]{1,0:T(8,128)(2,1)S(1)}, bf16[336,128]{1,0:T(8,128)(2,1)S(1)}, u32[]{:S(2)}, u32[]{:S(2)}) collective-permute-start(bf16[336,128]{1,0:T(8,128)(2,1)S(1)} %get-tuple-element.131), channel_id=1, source_target_pairs={{0,8},{2,10},{4,12},{6,14},{8,0},{10,2},{12,4},{14,6},{16,24},{18,... | collective-permute-start | bytes 258056 | tf_op jit(solution)/shard_map/cond/branch_3_fun/ppermute | solution.py:322
  36.3 10.7 %collective-permute-start.55 = (bf16[336,128]{1,0:T(8,128)(2,1)S(1)}, bf16[336,128]{1,0:T(8,128)(2,1)S(1)}, u32[]{:S(2)}, u32[]{:S(2)}) collective-permute-start(bf16[336,128]{1,0:T(8,128)(2,1)S(1)} %get-tuple-element.132), channel_id=1, source_target_pairs={{0,18},{2,16},{4,22},{6,20},{8,26},{10,24},{12,30},{14,28},{16,2},... | collective-permute-start | bytes 258056 | tf_op jit(solution)/shard_map/cond/branch_3_fun/ppermute | solution.py:322
  40.1 7.0 %collective-permute-start.56 = (bf16[336,128]{1,0:T(8,128)(2,1)S(1)}, bf16[336,128]{1,0:T(8,128)(2,1)S(1)}, u32[]{:S(2)}, u32[]{:S(2)}) collective-permute-start(bf16[336,128]{1,0:T(8,128)(2,1)S(1)} %get-tuple-element.133), channel_id=1, source_target_pairs={{0,6},{2,4},{4,2},{6,0},{8,14},{10,12},{12,10},{14,8},{16,22},{18,... | collective-permute-start | bytes 258056 | tf_op jit(solution)/shard_map/cond/branch_3_fun/ppermute | solution.py:322
  40.1 7.0 %collective-permute-start.57 = (bf16[336,128]{1,0:T(8,128)(2,1)S(1)}, bf16[336,128]{1,0:T(8,128)(2,1)S(1)}, u32[]{:S(2)}, u32[]{:S(2)}) collective-permute-start(bf16[336,128]{1,0:T(8,128)(2,1)S(1)} %get-tuple-element.134), channel_id=1, source_target_pairs={{0,16},{2,18},{4,20},{6,22},{8,24},{10,26},{12,28},{14,30},{16,0},... | collective-permute-start | bytes 258056 | tf_op jit(solution)/shard_map/cond/branch_3_fun/ppermute | solution.py:322
  44.6 4.5 %collective-permute-start.58 = (bf16[336,128]{1,0:T(8,128)(2,1)S(1)}, bf16[336,128]{1,0:T(8,128)(2,1)S(1)}, u32[]{:S(2)}, u32[]{:S(2)}) collective-permute-start(bf16[336,128]{1,0:T(8,128)(2,1)S(1)} %get-tuple-element.135), channel_id=1, source_target_pairs={{0,4},{2,6},{4,0},{6,2},{8,12},{10,14},{12,8},{14,10},{16,20},{18,... | collective-permute-start | bytes 258056 | tf_op jit(solution)/shard_map/cond/branch_3_fun/ppermute | solution.py:322
  45.1 4.5 %collective-permute-start.59 = (bf16[336,128]{1,0:T(8,128)(2,1)S(1)}, bf16[336,128]{1,0:T(8,128)(2,1)S(1)}, u32[]{:S(2)}, u32[]{:S(2)}) collective-permute-start(bf16[336,128]{1,0:T(8,128)(2,1)S(1)} %get-tuple-element.136), channel_id=1, source_target_pairs={{0,2},{2,0},{4,6},{6,4},{8,10},{10,8},{12,14},{14,12},{16,18},{18,... | collective-permute-start | bytes 258056 | tf_op jit(solution)/shard_map/cond/branch_3_fun/ppermute | solution.py:322
  52.6 0.6 %copy-start.4 = (f32[128,128]{1,0:T(8,128)}, f32[128,128]{1,0:T(8,128)S(1)}, u32[]{:S(2)}) copy-start(f32[128,128]{1,0:T(8,128)S(1)} %get-tuple-element.477) | copy-start | bytes 196612

commit v8 on v7

--- a/solution.py
+++ b/solution.py
@@ -11,7 +11,7 @@
 UNROLL = 32
 FIRST = 5
 QUAD = 4
-STEP = 128
+STEP = 384
 VMEM_LIMIT = 24 * 1024 * 1024
 LADDER = (32, 38, 40, 42, 44, 46, 56, 144)
 NT = (((1,), (1,)), ((), ()))
@@ -146,21 +146,23 @@
 
 def widen_kernel(part, in_ref, *rest):
     out_ref = rest[-1]
-    half = in_ref.shape[1]
-
-    def widen(i, _):
-        begin = pl.multiple_of(i * STEP, STEP)
-        rows = in_ref[:, pl.ds(begin, STEP), :].astype(jnp.float32)
-        out_ref[pl.ds(part * half + begin, STEP)] = jnp.transpose(rows, (1, 0, 2))
-        return 0
-
-    lax.fori_loop(0, half // STEP, widen, 0)
+    frames, half, _ = in_ref.shape
+    for f in range(frames):
+
+        def widen(i, _, f=f):
+            begin = pl.multiple_of(i * STEP, STEP)
+            rows = in_ref[f, pl.ds(begin, STEP), :].astype(jnp.float32)
+            out_ref[pl.ds(f * (2 * half + 1) + part * half + begin, STEP), :] = rows
+            return 0
+
+        lax.fori_loop(0, half // STEP, widen, 0)
 
 
 def pack_kernel(group, first, word_ref, scalar_ref, pool_ref, after_ref, *rest):
     out_refs, stage = rest[:-1], rest[-1]
     depth = out_refs[0].shape[0]
-    frames = pool_ref.shape[1]
+    frames = 8
+    stride = pool_ref.shape[0] // frames
     lane = lax.broadcasted_iota(jnp.int32, (frames, LANE), 1)
     begin, end = scalar_ref[3 + group], scalar_ref[4 + group]
 
@@ -169,7 +171,7 @@
         turned = []
         for j in range(UNROLL):
             word = word_ref[at + j]
-            turned.append(pltpu.roll(pool_ref[word & 4095], (word >> 12) & (LANE - 1), 1))
+            turned.append(pltpu.roll(pool_ref[pl.ds(word & 4095, frames, stride=stride), :], (word >> 12) & (LANE - 1), 1))
         for j in range(UNROLL):
             word = word_ref[at + j]
             shift = (word >> 12) & (LANE - 1)
@@ -267,7 +269,7 @@
     def widen(*given):
         return pl.pallas_call(
             functools.partial(widen_kernel, len(given) - 1),
-            out_shape=jax.ShapeDtypeStruct((2 * half, local_frames, LANE), jnp.float32),
+            out_shape=jax.ShapeDtypeStruct((local_frames * (2 * half + 1), LANE), jnp.float32),
             in_specs=[vmem] * len(given),
             out_specs=vmem,
             input_output_aliases={1: 0} if len(given) > 1 else {},

time: 53.4 us -> 53.5 us (level); the launches traced: 53.3 us -> 52.8 us
  Pallas kernels: 14.2 us -> 12.8 us
  waiting for transfers between devices: 7.34 us -> 8.09 us
    pallas_call x2, Pallas kernels: 1.95 us -> 0.8 us  [widen(): pl.pallas_call(functools.partial(widen_kernel, len(given) - 1), out_shape...]
    ppermute x15, waiting for transfers between devices: 7.33 us -> 7.99 us  [run(): got.append(lax.ppermute(part, 'tm', pairs) if apart else part)]
  transfers between devices with their start and end apart: 16 -> 16, of which waited for: 4 -> 6; matrix products, arithmetic and copies ran while one was open for 0% -> 0% of each run, Pallas kernels for 14% -> 13%
where the time goes in v8:
time: 53.5 us; the launch traced here: 52.8 us
  starting transfers between devices  28.9 us (54%)
  Pallas kernels  12.8 us (24%)
  waiting for transfers between devices  8.09 us (15%)
  local copies, waits for them, and re-layouts  2.61 us (5%)
    ppermute x15, starting transfers between devices, run(): got.append(lax.ppermute(part, 'tm', pairs) if apart else part)  28.5 us
    ppermute x15, waiting for transfers between devices, run(): got.append(lax.ppermute(part, 'tm', pairs) if apart else part)  7.99 us
    pallas_call x2, Pallas kernels, run(): pl.pallas_call(functools.partial(pack_kernel, group, first), out_shape=(j...  7.3 us
    pallas_call x1, Pallas kernels, run(): pl.pallas_call(gram_kernel, out_shape=jax.ShapeDtypeStruct((frame_count,...  2.83 us
    unnamed x10, local copies, waits for them, and re-layouts  2.61 us
    pallas_call x1, Pallas kernels, on_device_routed(): pl.pallas_call(plan_kernel, out_shape=(jax.ShapeDtypeStruct((list_rows, L...  1.83 us
  transfers between devices with their start and end apart: 16, of which 6 were waited for; matrix products, arithmetic and copies ran while one was open for 0% of the time, Pallas kernels for 13%

profile of v8, /device:TPU:0, one launch (start us, length us, event | category | flops | bytes accessed | tf_op | source)
XLA Modules:
  0.0 52.8 jit_solution(3745860610267132724)
XLA Ops:
  0.0 0.5 collective-permute-start.120
  0.5 1.7 %copy-done = bf16[8,1152,128]{2,1,0:T(8,128)(2,1)S(1)} copy-done((bf16[8,1152,128]{2,1,0:T(8,128)(2,1)S(1)}, bf16[8,1152,128]{2,1,0:T(8,128)(2,1)}, u32[]{:S(2)}) %copy-start) | copy-done | bytes 2359320
  2.1 0.4 widen.2.rest_0_
  2.5 0.3 copy-done.1
  2.8 0.0 copy-done.2
  2.8 1.8 %plan.1 = (s32[24,128]{1,0:T(8,128)S(1)}, s32[6]{0:T(128)S(1)}) custom-call(s32[32]{0:T(128)S(1)} %copy-done.3, s32[2304]{0:T(1024)S(1)} %copy-done.1, s32[2304]{0:T(1024)S(1)} %copy-done.2), custom_call_target="tpu_custom_call" | custom-call | tf_op jit(solution)/shard_map/plan/pallas_call | solution.py:281
  4.7 0.1 collective-permute-done.120.in_ref
  4.8 0.4 widen.3
  5.2 46.9 %conditional.1 = (f32[128,128]{1,0:T(8,128)S(1)}) conditional(s32[]{:T(128)} %bitcast.8, (s32[24,128]{1,0:T(8,128)S(1)}, s32[6]{0:T(128)S(1)}, f32[18440,128]{1,0:T(8,128)S(1)}) %tuple.29, (s32[24,128]{1,0:T(8,128)S(1)}, s32[6]{0:T(128)S(1)}, f32[18440,128]{1,0:T(8,128)S(1)}) %tuple.29, (s32[24,128]{1,0:T(8,128)S(1)}, ...), branch_computations={%region_0.0_spmd, %region_1.0_spmd, %region_2.0_spmd, %region_3.0_... | conditional | flops 4000000 | bytes 49695328 | solution.py:342
  5.3 2.6 %pack.22 = (bf16[336,128]{1,0:T(8,128)(2,1)S(1)}, bf16[336,128]{1,0:T(8,128)(2,1)S(1)}, bf16[336,128]{1,0:T(8,128)(2,1)S(1)}, bf16[336,128]{1,0:T(8,128)(2,1)S(1)}, bf16[336,128]{1,0:T(8,128)(2,1)S(1)}) custom-call(s32[3072]{0:T(1024)S(1)} %bitcast.16, s32[6]{0:T(128)S(1)} %get-tuple-element.119.scalar_ref.after_ref, ...), custom_call_target="tpu_custom_call" | custom-call | flops 2000000 | bytes 16000000 | tf_op jit(solution)/shard_map/cond/branch_3_fun/pack/pallas_call | solution.py:308
  7.9 6.9 %collective-permute-start.45 = (bf16[336,128]{1,0:T(8,128)(2,1)S(1)}, bf16[336,128]{1,0:T(8,128)(2,1)S(1)}, u32[]{:S(2)}, u32[]{:S(2)}) collective-permute-start(bf16[336,128]{1,0:T(8,128)(2,1)S(1)} %get-tuple-element.122), channel_id=1, source_target_pairs={{0,30},{2,28},{4,26},{6,24},{8,22},{10,20},{12,18},{14,16},{16,14}... | collective-permute-start | bytes 258056 | tf_op jit(solution)/shard_map/cond/branch_3_fun/ppermute | solution.py:324
  14.8 0.2 collective-permute-start.46
  15.0 3.6 %collective-permute-start.47 = (bf16[336,128]{1,0:T(8,128)(2,1)S(1)}, bf16[336,128]{1,0:T(8,128)(2,1)S(1)}, u32[]{:S(2)}, u32[]{:S(2)}) collective-permute-start(bf16[336,128]{1,0:T(8,128)(2,1)S(1)} %get-tuple-element.124), channel_id=1, source_target_pairs={{0,26},{2,24},{4,30},{6,28},{8,18},{10,16},{12,22},{14,20},{16,10}... | collective-permute-start | bytes 258056 | tf_op jit(solution)/shard_map/cond/branch_3_fun/ppermute | solution.py:324
  18.6 1.0 %collective-permute-start.49 = (bf16[336,128]{1,0:T(8,128)(2,1)S(1)}, bf16[336,128]{1,0:T(8,128)(2,1)S(1)}, u32[]{:S(2)}, u32[]{:S(2)}) collective-permute-start(bf16[336,128]{1,0:T(8,128)(2,1)S(1)} %get-tuple-element.126), channel_id=1, source_target_pairs={{0,24},{2,26},{4,28},{6,30},{8,16},{10,18},{12,20},{14,22},{16,8},... | collective-permute-start | bytes 258056 | tf_op jit(solution)/shard_map/cond/branch_3_fun/ppermute | solution.py:324
  19.6 4.7 %pack.23 = (bf16[336,128]{1,0:T(8,128)(2,1)S(1)}, bf16[336,128]{1,0:T(8,128)(2,1)S(1)}, bf16[336,128]{1,0:T(8,128)(2,1)S(1)}, bf16[336,128]{1,0:T(8,128)(2,1)S(1...) custom-call(s32[3072]{0:T(1024)S(1)} %bitcast.17, ...), custom_call_target="tpu_custom_call" | custom-call | flops 2000000 | bytes 16000000 | tf_op jit(solution)/shard_map/cond/branch_3_fun/pack/pallas_call | solution.py:308
  24.2 4.6 %collective-permute-start.50 = (bf16[336,128]{1,0:T(8,128)(2,1)S(1)}, bf16[336,128]{1,0:T(8,128)(2,1)S(1)}, u32[]{:S(2)}, u32[]{:S(2)}) collective-permute-start(bf16[336,128]{1,0:T(8,128)(2,1)S(1)} %get-tuple-element.127), channel_id=1, source_target_pairs={{0,12},{2,14},{4,8},{6,10},{8,4},{10,6},{12,0},{14,2},{16,28},{18,... | collective-permute-start | bytes 258056 | tf_op jit(solution)/shard_map/cond/branch_3_fun/ppermute | solution.py:324
  28.8 2.3 %collective-permute-start.51 = (bf16[336,128]{1,0:T(8,128)(2,1)S(1)}, bf16[336,128]{1,0:T(8,128)(2,1)S(1)}, u32[]{:S(2)}, u32[]{:S(2)}) collective-permute-start(bf16[336,128]{1,0:T(8,128)(2,1)S(1)} %get-tuple-element.128), channel_id=1, source_target_pairs={{0,22},{2,20},{4,18},{6,16},{8,30},{10,28},{12,26},{14,24},{16,6},... | collective-permute-start | bytes 258056 | tf_op jit(solution)/shard_map/cond/branch_3_fun/ppermute | solution.py:324
  31.1 1.4 %collective-permute-start.52 = (bf16[336,128]{1,0:T(8,128)(2,1)S(1)}, bf16[336,128]{1,0:T(8,128)(2,1)S(1)}, u32[]{:S(2)}, u32[]{:S(2)}) collective-permute-start(bf16[336,128]{1,0:T(8,128)(2,1)S(1)} %get-tuple-element.129), channel_id=1, source_target_pairs={{0,10},{2,8},{4,14},{6,12},{8,2},{10,0},{12,6},{14,4},{16,26},{18,... | collective-permute-start | bytes 258056 | tf_op jit(solution)/shard_map/cond/branch_3_fun/ppermute | solution.py:324
  32.5 1.0 %collective-permute-start.53 = (bf16[336,128]{1,0:T(8,128)(2,1)S(1)}, bf16[336,128]{1,0:T(8,128)(2,1)S(1)}, u32[]{:S(2)}, u32[]{:S(2)}) collective-permute-start(bf16[336,128]{1,0:T(8,128)(2,1)S(1)} %get-tuple-element.130), channel_id=1, source_target_pairs={{0,20},{2,22},{4,16},{6,18},{8,28},{10,30},{12,24},{14,26},{16,4},... | collective-permute-start | bytes 258056 | tf_op jit(solution)/shard_map/cond/branch_3_fun/ppermute | solution.py:324
  33.5 2.1 %collective-permute-start.54 = (bf16[336,128]{1,0:T(8,128)(2,1)S(1)}, bf16[336,128]{1,0:T(8,128)(2,1)S(1)}, u32[]{:S(2)}, u32[]{:S(2)}) collective-permute-start(bf16[336,128]{1,0:T(8,128)(2,1)S(1)} %get-tuple-element.131), channel_id=1, source_target_pairs={{0,8},{2,10},{4,12},{6,14},{8,0},{10,2},{12,4},{14,6},{16,24},{18,... | collective-permute-start | bytes 258056 | tf_op jit(solution)/shard_map/cond/branch_3_fun/ppermute | solution.py:324
  35.6 2.3 %collective-permute-start.55 = (bf16[336,128]{1,0:T(8,128)(2,1)S(1)}, bf16[336,128]{1,0:T(8,128)(2,1)S(1)}, u32[]{:S(2)}, u32[]{:S(2)}) collective-permute-start(bf16[336,128]{1,0:T(8,128)(2,1)S(1)} %get-tuple-element.132), channel_id=1, source_target_pairs={{0,18},{2,16},{4,22},{6,20},{8,26},{10,24},{12,30},{14,28},{16,2},... | collective-permute-start | bytes 258056 | tf_op jit(solution)/shard_map/cond/branch_3_fun/ppermute | solution.py:324
  37.9 1.1 %collective-permute-done.51.refs_6_ = bf16[336,128]{1,0:T(8,128)(2,1)S(1)} collective-permute-done((bf16[336,128]{1,0:T(8,128)(2,1)S(1)}, bf16[336,128]{1,0:T(8,128)(2,1)S(1)}, u32[]{:S(2)}, u32[]{:S(2)}) %collective-permute-start.51) | collective-permute-done | bytes 86048 | tf_op jit(solution)/shard_map/cond/branch_3_fun/ppermute | solution.py:324
  39.0 0.9 %collective-permute-start.57 = (bf16[336,128]{1,0:T(8,128)(2,1)S(1)}, bf16[336,128]{1,0:T(8,128)(2,1)S(1)}, u32[]{:S(2)}, u32[]{:S(2)}) collective-permute-start(bf16[336,128]{1,0:T(8,128)(2,1)S(1)} %get-tuple-element.134), channel_id=1, source_target_pairs={{0,16},{2,18},{4,20},{6,22},{8,24},{10,26},{12,28},{14,30},{16,0},... | collective-permute-start | bytes 258056 | tf_op jit(solution)/shard_map/cond/branch_3_fun/ppermute | solution.py:324
  39.9 3.6 %collective-permute-done.53.refs_8_ = bf16[336,128]{1,0:T(8,128)(2,1)S(1)} collective-permute-done((bf16[336,128]{1,0:T(8,128)(2,1)S(1)}, bf16[336,128]{1,0:T(8,128)(2,1)S(1)}, u32[]{:S(2)}, u32[]{:S(2)}) %collective-permute-start.53) | collective-permute-done | bytes 86048 | tf_op jit(solution)/shard_map/cond/branch_3_fun/ppermute | solution.py:324
  43.5 1.1 %collective-permute-start.58 = (bf16[336,128]{1,0:T(8,128)(2,1)S(1)}, bf16[336,128]{1,0:T(8,128)(2,1)S(1)}, u32[]{:S(2)}, u32[]{:S(2)}) collective-permute-start(bf16[336,128]{1,0:T(8,128)(2,1)S(1)} %get-tuple-element.135), channel_id=1, source_target_pairs={{0,4},{2,6},{4,0},{6,2},{8,12},{10,14},{12,8},{14,10},{16,20},{18,... | collective-permute-start | bytes 258056 | tf_op jit(solution)/shard_map/cond/branch_3_fun/ppermute | solution.py:324
  44.6 1.3 %collective-permute-start.59 = (bf16[336,128]{1,0:T(8,128)(2,1)S(1)}, bf16[336,128]{1,0:T(8,128)(2,1)S(1)}, u32[]{:S(2)}, u32[]{:S(2)}) collective-permute-start(bf16[336,128]{1,0:T(8,128)(2,1)S(1)} %get-tuple-element.136), channel_id=1, source_target_pairs={{0,2},{2,0},{4,6},{6,4},{8,10},{10,8},{12,14},{14,12},{16,18},{18,... | collective-permute-start | bytes 258056 | tf_op jit(solution)/shard_map/cond/branch_3_fun/ppermute | solution.py:324
  45.9 0.2 collective-permute-done.57.refs_12_
  46.1 1.9 %collective-permute-done.58.refs_13_ = bf16[336,128]{1,0:T(8,128)(2,1)S(1)} collective-permute-done((bf16[336,128]{1,0:T(8,128)(2,1)S(1)}, bf16[336,128]{1,0:T(8,128)(2,1)S(1)}, u32[]{:S(2)}, u32[]{:S(2)}) %collective-permute-start.58) | collective-permute-done | bytes 86048 | tf_op jit(solution)/shard_map/cond/branch_3_fun/ppermute | solution.py:324
  48.0 1.1 %collective-permute-done.59.refs_14_ = bf16[336,128]{1,0:T(8,128)(2,1)S(1)} collective-permute-done((bf16[336,128]{1,0:T(8,128)(2,1)S(1)}, bf16[336,128]{1,0:T(8,128)(2,1)S(1)}, u32[]{:S(2)}, u32[]{:S(2)}) %collective-permute-start.59) | collective-permute-done | bytes 86048 | tf_op jit(solution)/shard_map/cond/branch_3_fun/ppermute | solution.py:324
  49.1 2.8 %gram.11 = f32[128,128]{1,0:T(8,128)S(1)} custom-call(s32[6]{0:T(128)S(1)} %get-tuple-element.119.scalar_ref.after_ref, bf16[336,128]{1,0:T(8,128)(2,1)S(1)} %collective-permute-done.45.after_ref.refs_0_, bf16[336,128]{1,0:T(8,128)(2,1)S(1)} %collective-permute-done.46.refs_1_, bf16[336,128]{1,0:T(8,128)(2,1)S(1)} %collective-permute-done.47.refs_2_, ...), custom_call_target="tpu_custom_call" | custom-call | tf_op jit(solution)/shard_map/cond/branch_3_fun/gram/pallas_call | solution.py:326
  52.1 0.0 copy-start.4
  52.1 0.6 %copy-done.4 = f32[128,128]{1,0:T(8,128)} copy-done((f32[128,128]{1,0:T(8,128)}, f32[128,128]{1,0:T(8,128)S(1)}, u32[]{:S(2)}) %copy-start.4) | copy-done | bytes 65560
  (17 shorter events, 0.0 us)
Async XLA Ops:
  0.0 4.8 %collective-permute-start.120 = (bf16[8,1152,128]{2,1,0:T(8,128)(2,1)}, bf16[8,1152,128]{2,1,0:T(8,128)(2,1)S(1)}, u32[]{:S(2)}, u32[]{:S(2)}) collective-permute-start(bf16[8,1152,128]{2,1,0:T(8,128)(2,1)} %in_ref.1), channel_id=1, source_target_pairs={{0,1},{1,0},{2,3},{3,2},{4,5},{5,4},{6,7},{7,6},{8,9},{9,8},{10,11... | collective-permute-start | bytes 7077896 | tf_op jit(solution)/shard_map/ppermute | solution.py:280
  0.5 1.7 %copy-start = (bf16[8,1152,128]{2,1,0:T(8,128)(2,1)S(1)}, bf16[8,1152,128]{2,1,0:T(8,128)(2,1)}, u32[]{:S(2)}) copy-start(bf16[8,1152,128]{2,1,0:T(8,128)(2,1)} %in_ref.1) | copy-start | bytes 7077892
  2.1 0.7 %copy-start.1 = (s32[2304]{0:T(1024)S(1)}, s32[2304]{0:T(1024)}, u32[]{:S(2)}) copy-start(s32[2304]{0:T(1024)} %cycle_in.1) | copy-start | bytes 27652
  2.1 0.7 %copy-start.2 = (s32[2304]{0:T(1024)S(1)}, s32[2304]{0:T(1024)}, u32[]{:S(2)}) copy-start(s32[2304]{0:T(1024)} %valid_in.1) | copy-start | bytes 27652
  2.1 0.7 %copy-start.3 = (s32[32]{0:T(128)S(1)}, s32[32]{0:T(128)}, u32[]{:S(2)}) copy-start(s32[32]{0:T(128)} %owner_in.1) | copy-start | bytes 388
  7.9 11.6 %collective-permute-start.45 = (bf16[336,128]{1,0:T(8,128)(2,1)S(1)}, bf16[336,128]{1,0:T(8,128)(2,1)S(1)}, u32[]{:S(2)}, u32[]{:S(2)}) collective-permute-start(bf16[336,128]{1,0:T(8,128)(2,1)S(1)} %get-tuple-element.122), channel_id=1, source_target_pairs={{0,30},{2,28},{4,26},{6,24},{8,22},{10,20},{12,18},{14,16},{16,14}... | collective-permute-start | bytes 258056 | tf_op jit(solution)/shard_map/cond/branch_3_fun/ppermute | solution.py:324
  14.8 14.0 %collective-permute-start.46 = (bf16[336,128]{1,0:T(8,128)(2,1)S(1)}, bf16[336,128]{1,0:T(8,128)(2,1)S(1)}, u32[]{:S(2)}, u32[]{:S(2)}) collective-permute-start(bf16[336,128]{1,0:T(8,128)(2,1)S(1)} %get-tuple-element.123), channel_id=1, source_target_pairs={{0,28},{2,30},{4,24},{6,26},{8,20},{10,22},{12,16},{14,18},{16,12}... | collective-permute-start | bytes 258056 | tf_op jit(solution)/shard_map/cond/branch_3_fun/ppermute | solution.py:324
  15.0 16.1 %collective-permute-start.47 = (bf16[336,128]{1,0:T(8,128)(2,1)S(1)}, bf16[336,128]{1,0:T(8,128)(2,1)S(1)}, u32[]{:S(2)}, u32[]{:S(2)}) collective-permute-start(bf16[336,128]{1,0:T(8,128)(2,1)S(1)} %get-tuple-element.124), channel_id=1, source_target_pairs={{0,26},{2,24},{4,30},{6,28},{8,18},{10,16},{12,22},{14,20},{16,10}... | collective-permute-start | bytes 258056 | tf_op jit(solution)/shard_map/cond/branch_3_fun/ppermute | solution.py:324
  18.6 14.0 %collective-permute-start.48 = (bf16[336,128]{1,0:T(8,128)(2,1)S(1)}, bf16[336,128]{1,0:T(8,128)(2,1)S(1)}, u32[]{:S(2)}, u32[]{:S(2)}) collective-permute-start(bf16[336,128]{1,0:T(8,128)(2,1)S(1)} %get-tuple-element.125), channel_id=1, source_target_pairs={{0,14},{2,12},{4,10},{6,8},{8,6},{10,4},{12,2},{14,0},{16,30},{18,... | collective-permute-start | bytes 258056 | tf_op jit(solution)/shard_map/cond/branch_3_fun/ppermute | solution.py:324
  18.6 14.9 %collective-permute-start.49 = (bf16[336,128]{1,0:T(8,128)(2,1)S(1)}, bf16[336,128]{1,0:T(8,128)(2,1)S(1)}, u32[]{:S(2)}, u32[]{:S(2)}) collective-permute-start(bf16[336,128]{1,0:T(8,128)(2,1)S(1)} %get-tuple-element.126), channel_id=1, source_target_pairs={{0,24},{2,26},{4,28},{6,30},{8,16},{10,18},{12,20},{14,22},{16,8},... | collective-permute-start | bytes 258056 | tf_op jit(solution)/shard_map/cond/branch_3_fun/ppermute | solution.py:324
  24.2 11.4 %collective-permute-start.50 = (bf16[336,128]{1,0:T(8,128)(2,1)S(1)}, bf16[336,128]{1,0:T(8,128)(2,1)S(1)}, u32[]{:S(2)}, u32[]{:S(2)}) collective-permute-start(bf16[336,128]{1,0:T(8,128)(2,1)S(1)} %get-tuple-element.127), channel_id=1, source_target_pairs={{0,12},{2,14},{4,8},{6,10},{8,4},{10,6},{12,0},{14,2},{16,28},{18,... | collective-permute-start | bytes 258056 | tf_op jit(solution)/shard_map/cond/branch_3_fun/ppermute | solution.py:324
  28.8 10.2 %collective-permute-start.51 = (bf16[336,128]{1,0:T(8,128)(2,1)S(1)}, bf16[336,128]{1,0:T(8,128)(2,1)S(1)}, u32[]{:S(2)}, u32[]{:S(2)}) collective-permute-start(bf16[336,128]{1,0:T(8,128)(2,1)S(1)} %get-tuple-element.128), channel_id=1, source_target_pairs={{0,22},{2,20},{4,18},{6,16},{8,30},{10,28},{12,26},{14,24},{16,6},... | collective-permute-start | bytes 258056 | tf_op jit(solution)/shard_map/cond/branch_3_fun/ppermute | solution.py:324
  31.1 7.9 %collective-permute-start.52 = (bf16[336,128]{1,0:T(8,128)(2,1)S(1)}, bf16[336,128]{1,0:T(8,128)(2,1)S(1)}, u32[]{:S(2)}, u32[]{:S(2)}) collective-permute-start(bf16[336,128]{1,0:T(8,128)(2,1)S(1)} %get-tuple-element.129), channel_id=1, source_target_pairs={{0,10},{2,8},{4,14},{6,12},{8,2},{10,0},{12,6},{14,4},{16,26},{18,... | collective-permute-start | bytes 258056 | tf_op jit(solution)/shard_map/cond/branch_3_fun/ppermute | solution.py:324
  32.5 11.0 %collective-permute-start.53 = (bf16[336,128]{1,0:T(8,128)(2,1)S(1)}, bf16[336,128]{1,0:T(8,128)(2,1)S(1)}, u32[]{:S(2)}, u32[]{:S(2)}) collective-permute-start(bf16[336,128]{1,0:T(8,128)(2,1)S(1)} %get-tuple-element.130), channel_id=1, source_target_pairs={{0,20},{2,22},{4,16},{6,18},{8,28},{10,30},{12,24},{14,26},{16,4},... | collective-permute-start | bytes 258056 | tf_op jit(solution)/shard_map/cond/branch_3_fun/ppermute | solution.py:324
  33.5 11.1 %collective-permute-start.54 = (bf16[336,128]{1,0:T(8,128)(2,1)S(1)}, bf16[336,128]{1,0:T(8,128)(2,1)S(1)}, u32[]{:S(2)}, u32[]{:S(2)}) collective-permute-start(bf16[336,128]{1,0:T(8,128)(2,1)S(1)} %get-tuple-element.131), channel_id=1, source_target_pairs={{0,8},{2,10},{4,12},{6,14},{8,0},{10,2},{12,4},{14,6},{16,24},{18,... | collective-permute-start | bytes 258056 | tf_op jit(solution)/shard_map/cond/branch_3_fun/ppermute | solution.py:324
  35.6 10.3 %collective-permute-start.55 = (bf16[336,128]{1,0:T(8,128)(2,1)S(1)}, bf16[336,128]{1,0:T(8,128)(2,1)S(1)}, u32[]{:S(2)}, u32[]{:S(2)}) collective-permute-start(bf16[336,128]{1,0:T(8,128)(2,1)S(1)} %get-tuple-element.132), channel_id=1, source_target_pairs={{0,18},{2,16},{4,22},{6,20},{8,26},{10,24},{12,30},{14,28},{16,2},... | collective-permute-start | bytes 258056 | tf_op jit(solution)/shard_map/cond/branch_3_fun/ppermute | solution.py:324
  39.0 6.9 %collective-permute-start.56 = (bf16[336,128]{1,0:T(8,128)(2,1)S(1)}, bf16[336,128]{1,0:T(8,128)(2,1)S(1)}, u32[]{:S(2)}, u32[]{:S(2)}) collective-permute-start(bf16[336,128]{1,0:T(8,128)(2,1)S(1)} %get-tuple-element.133), channel_id=1, source_target_pairs={{0,6},{2,4},{4,2},{6,0},{8,14},{10,12},{12,10},{14,8},{16,22},{18,... | collective-permute-start | bytes 258056 | tf_op jit(solution)/shard_map/cond/branch_3_fun/ppermute | solution.py:324
  39.0 7.1 %collective-permute-start.57 = (bf16[336,128]{1,0:T(8,128)(2,1)S(1)}, bf16[336,128]{1,0:T(8,128)(2,1)S(1)}, u32[]{:S(2)}, u32[]{:S(2)}) collective-permute-start(bf16[336,128]{1,0:T(8,128)(2,1)S(1)} %get-tuple-element.134), channel_id=1, source_target_pairs={{0,16},{2,18},{4,20},{6,22},{8,24},{10,26},{12,28},{14,30},{16,0},... | collective-permute-start | bytes 258056 | tf_op jit(solution)/shard_map/cond/branch_3_fun/ppermute | solution.py:324
  43.5 4.5 %collective-permute-start.58 = (bf16[336,128]{1,0:T(8,128)(2,1)S(1)}, bf16[336,128]{1,0:T(8,128)(2,1)S(1)}, u32[]{:S(2)}, u32[]{:S(2)}) collective-permute-start(bf16[336,128]{1,0:T(8,128)(2,1)S(1)} %get-tuple-element.135), channel_id=1, source_target_pairs={{0,4},{2,6},{4,0},{6,2},{8,12},{10,14},{12,8},{14,10},{16,20},{18,... | collective-permute-start | bytes 258056 | tf_op jit(solution)/shard_map/cond/branch_3_fun/ppermute | solution.py:324
  44.6 4.5 %collective-permute-start.59 = (bf16[336,128]{1,0:T(8,128)(2,1)S(1)}, bf16[336,128]{1,0:T(8,128)(2,1)S(1)}, u32[]{:S(2)}, u32[]{:S(2)}) collective-permute-start(bf16[336,128]{1,0:T(8,128)(2,1)S(1)} %get-tuple-element.136), channel_id=1, source_target_pairs={{0,2},{2,0},{4,6},{6,4},{8,10},{10,8},{12,14},{14,12},{16,18},{18,... | collective-permute-start | bytes 258056 | tf_op jit(solution)/shard_map/cond/branch_3_fun/ppermute | solution.py:324
  52.1 0.6 %copy-start.4 = (f32[128,128]{1,0:T(8,128)}, f32[128,128]{1,0:T(8,128)S(1)}, u32[]{:S(2)}) copy-start(f32[128,128]{1,0:T(8,128)S(1)} %get-tuple-element.477) | copy-start | bytes 196612

commit v9 on v8

--- a/solution.py
+++ b/solution.py
@@ -9,7 +9,7 @@
 
 LANE = 128
 UNROLL = 32
-FIRST = 5
+FIRST = 4
 QUAD = 4
 STEP = 384
 VMEM_LIMIT = 24 * 1024 * 1024

time: 53.5 us -> 53.1 us (level)
  starting transfers between devices: 28.9 us -> 28.2 us
    ppermute x15, starting transfers between devices: 28.5 us -> 27.8 us  [run(): got.append(lax.ppermute(part, 'tm', pairs) if apart else part)]
  transfers between devices with their start and end apart: 16 -> 16, of which waited for: 6 -> 6; matrix products, arithmetic and copies ran while one was open for 0% -> 0% of each run, Pallas kernels for 13% -> 14%
where the time goes in v9:
time: 53.1 us; the launch traced here: 52.4 us
  starting transfers between devices  28.2 us (53%)
  Pallas kernels  12.6 us (24%)
  waiting for transfers between devices  8.61 us (16%)
  local copies, waits for them, and re-layouts  2.61 us (5%)
    ppermute x15, starting transfers between devices, run(): got.append(lax.ppermute(part, 'tm', pairs) if apart else part)  27.8 us
    ppermute x15, waiting for transfers between devices, run(): got.append(lax.ppermute(part, 'tm', pairs) if apart else part)  8.5 us
    pallas_call x2, Pallas kernels, run(): pl.pallas_call(functools.partial(pack_kernel, group, first), out_shape=(j...  7.14 us
    pallas_call x1, Pallas kernels, run(): pl.pallas_call(gram_kernel, out_shape=jax.ShapeDtypeStruct((frame_count,...  2.83 us
    unnamed x10, local copies, waits for them, and re-layouts  2.61 us
    pallas_call x1, Pallas kernels, on_device_routed(): pl.pallas_call(plan_kernel, out_shape=(jax.ShapeDtypeStruct((list_rows, L...  1.83 us
  transfers between devices with their start and end apart: 16, of which 6 were waited for; matrix products, arithmetic and copies ran while one was open for 0% of the time, Pallas kernels for 14%

profile of v9, /device:TPU:0, one launch (start us, length us, event | category | flops | bytes accessed | tf_op | source)
XLA Modules:
  0.0 52.4 jit_solution(12216026992765241453)
XLA Ops:
  0.0 0.5 collective-permute-start.120
  0.5 1.7 %copy-done = bf16[8,1152,128]{2,1,0:T(8,128)(2,1)S(1)} copy-done((bf16[8,1152,128]{2,1,0:T(8,128)(2,1)S(1)}, bf16[8,1152,128]{2,1,0:T(8,128)(2,1)}, u32[]{:S(2)}) %copy-start) | copy-done | bytes 2359320
  2.1 0.4 widen.2.rest_0_
  2.5 0.3 copy-done.1
  2.8 0.0 copy-done.2
  2.8 1.8 %plan.1 = (s32[24,128]{1,0:T(8,128)S(1)}, s32[6]{0:T(128)S(1)}) custom-call(s32[32]{0:T(128)S(1)} %copy-done.3, s32[2304]{0:T(1024)S(1)} %copy-done.1, s32[2304]{0:T(1024)S(1)} %copy-done.2), custom_call_target="tpu_custom_call" | custom-call | tf_op jit(solution)/shard_map/plan/pallas_call | solution.py:281
  4.7 0.1 collective-permute-done.120.in_ref
  4.8 0.4 widen.3
  5.2 46.5 %conditional.1 = (f32[128,128]{1,0:T(8,128)S(1)}) conditional(s32[]{:T(128)} %bitcast.8, (s32[24,128]{1,0:T(8,128)S(1)}, s32[6]{0:T(128)S(1)}, f32[18440,128]{1,0:T(8,128)S(1)}) %tuple.29, (s32[24,128]{1,0:T(8,128)S(1)}, s32[6]{0:T(128)S(1)}, f32[18440,128]{1,0:T(8,128)S(1)}) %tuple.29, (s32[24,128]{1,0:T(8,128)S(1)}, ...), branch_computations={%region_0.0_spmd, %region_1.0_spmd, %region_2.0_spmd, %region_3.0_... | conditional | flops 4000000 | bytes 49695328 | solution.py:342
  5.3 2.2 %pack.20 = (bf16[320,128]{1,0:T(8,128)(2,1)S(1)}, bf16[320,128]{1,0:T(8,128)(2,1)S(1)}, bf16[320,128]{1,0:T(8,128)(2,1)S(1)}, bf16[320,128]{1,0:T(8,128)(2,1)S(1)}) custom-call(s32[3072]{0:T(1024)S(1)} %bitcast.14, s32[6]{0:T(128)S(1)} %get-tuple-element.100.scalar_ref.after_ref, f32[18440,128]{1,0:T(8,128)S(1)} %get-tuple-element.102.pool_ref, ...), custom_call_target="tpu_custom_call" | custom-call | flops 2000000 | bytes 16000000 | tf_op jit(solution)/shard_map/cond/branch_2_fun/pack/pallas_call | solution.py:308
  7.4 6.9 %collective-permute-start.30 = (bf16[320,128]{1,0:T(8,128)(2,1)S(1)}, bf16[320,128]{1,0:T(8,128)(2,1)S(1)}, u32[]{:S(2)}, u32[]{:S(2)}) collective-permute-start(bf16[320,128]{1,0:T(8,128)(2,1)S(1)} %get-tuple-element.103), channel_id=1, source_target_pairs={{0,30},{2,28},{4,26},{6,24},{8,22},{10,20},{12,18},{14,16},{16,14}... | collective-permute-start | bytes 245768 | tf_op jit(solution)/shard_map/cond/branch_2_fun/ppermute | solution.py:324
  14.3 0.2 collective-permute-start.31
  14.5 3.6 %collective-permute-start.32 = (bf16[320,128]{1,0:T(8,128)(2,1)S(1)}, bf16[320,128]{1,0:T(8,128)(2,1)S(1)}, u32[]{:S(2)}, u32[]{:S(2)}) collective-permute-start(bf16[320,128]{1,0:T(8,128)(2,1)S(1)} %get-tuple-element.105), channel_id=1, source_target_pairs={{0,26},{2,24},{4,30},{6,28},{8,18},{10,16},{12,22},{14,20},{16,10}... | collective-permute-start | bytes 245768 | tf_op jit(solution)/shard_map/cond/branch_2_fun/ppermute | solution.py:324
  18.1 5.0 %pack.21 = (bf16[320,128]{1,0:T(8,128)(2,1)S(1)}, bf16[320,128]{1,0:T(8,128)(2,1)S(1)}, bf16[320,128]{1,0:T(8,128)(2,1)S(1)}, bf16[320,128]{1,0:T(8,128)(2,1)S(1...) custom-call(s32[3072]{0:T(1024)S(1)} %bitcast.15, ...), custom_call_target="tpu_custom_call" | custom-call | flops 2000000 | bytes 16000000 | tf_op jit(solution)/shard_map/cond/branch_2_fun/pack/pallas_call | solution.py:308
  23.1 3.4 %collective-permute-start.34 = (bf16[320,128]{1,0:T(8,128)(2,1)S(1)}, bf16[320,128]{1,0:T(8,128)(2,1)S(1)}, u32[]{:S(2)}, u32[]{:S(2)}) collective-permute-start(bf16[320,128]{1,0:T(8,128)(2,1)S(1)} %get-tuple-element.107), channel_id=1, source_target_pairs={{0,24},{2,26},{4,28},{6,30},{8,16},{10,18},{12,20},{14,22},{16,8},... | collective-permute-start | bytes 245768 | tf_op jit(solution)/shard_map/cond/branch_2_fun/ppermute | solution.py:324
  26.5 2.1 %collective-permute-start.35 = (bf16[320,128]{1,0:T(8,128)(2,1)S(1)}, bf16[320,128]{1,0:T(8,128)(2,1)S(1)}, u32[]{:S(2)}, u32[]{:S(2)}) collective-permute-start(bf16[320,128]{1,0:T(8,128)(2,1)S(1)} %get-tuple-element.108), channel_id=1, source_target_pairs={{0,12},{2,14},{4,8},{6,10},{8,4},{10,6},{12,0},{14,2},{16,28},{18,... | collective-permute-start | bytes 245768 | tf_op jit(solution)/shard_map/cond/branch_2_fun/ppermute | solution.py:324
  28.6 1.9 %collective-permute-start.36 = (bf16[320,128]{1,0:T(8,128)(2,1)S(1)}, bf16[320,128]{1,0:T(8,128)(2,1)S(1)}, u32[]{:S(2)}, u32[]{:S(2)}) collective-permute-start(bf16[320,128]{1,0:T(8,128)(2,1)S(1)} %get-tuple-element.109), channel_id=1, source_target_pairs={{0,22},{2,20},{4,18},{6,16},{8,30},{10,28},{12,26},{14,24},{16,6},... | collective-permute-start | bytes 245768 | tf_op jit(solution)/shard_map/cond/branch_2_fun/ppermute | solution.py:324
  30.5 1.8 %collective-permute-start.37 = (bf16[320,128]{1,0:T(8,128)(2,1)S(1)}, bf16[320,128]{1,0:T(8,128)(2,1)S(1)}, u32[]{:S(2)}, u32[]{:S(2)}) collective-permute-start(bf16[320,128]{1,0:T(8,128)(2,1)S(1)} %get-tuple-element.110), channel_id=1, source_target_pairs={{0,10},{2,8},{4,14},{6,12},{8,2},{10,0},{12,6},{14,4},{16,26},{18,... | collective-permute-start | bytes 245768 | tf_op jit(solution)/shard_map/cond/branch_2_fun/ppermute | solution.py:324
  32.4 2.5 %collective-permute-start.38 = (bf16[320,128]{1,0:T(8,128)(2,1)S(1)}, bf16[320,128]{1,0:T(8,128)(2,1)S(1)}, u32[]{:S(2)}, u32[]{:S(2)}) collective-permute-start(bf16[320,128]{1,0:T(8,128)(2,1)S(1)} %get-tuple-element.111), channel_id=1, source_target_pairs={{0,20},{2,22},{4,16},{6,18},{8,28},{10,30},{12,24},{14,26},{16,4},... | collective-permute-start | bytes 245768 | tf_op jit(solution)/shard_map/cond/branch_2_fun/ppermute | solution.py:324
  34.8 0.6 %collective-permute-start.39 = (bf16[320,128]{1,0:T(8,128)(2,1)S(1)}, bf16[320,128]{1,0:T(8,128)(2,1)S(1)}, u32[]{:S(2)}, u32[]{:S(2)}) collective-permute-start(bf16[320,128]{1,0:T(8,128)(2,1)S(1)} %get-tuple-element.112), channel_id=1, source_target_pairs={{0,8},{2,10},{4,12},{6,14},{8,0},{10,2},{12,4},{14,6},{16,24},{18,... | collective-permute-start | bytes 245768 | tf_op jit(solution)/shard_map/cond/branch_2_fun/ppermute | solution.py:324
  35.4 1.9 %collective-permute-start.40 = (bf16[320,128]{1,0:T(8,128)(2,1)S(1)}, bf16[320,128]{1,0:T(8,128)(2,1)S(1)}, u32[]{:S(2)}, u32[]{:S(2)}) collective-permute-start(bf16[320,128]{1,0:T(8,128)(2,1)S(1)} %get-tuple-element.113), channel_id=1, source_target_pairs={{0,18},{2,16},{4,22},{6,20},{8,26},{10,24},{12,30},{14,28},{16,2},... | collective-permute-start | bytes 245768 | tf_op jit(solution)/shard_map/cond/branch_2_fun/ppermute | solution.py:324
  37.3 1.9 %collective-permute-done.36.refs_6_ = bf16[320,128]{1,0:T(8,128)(2,1)S(1)} collective-permute-done((bf16[320,128]{1,0:T(8,128)(2,1)S(1)}, bf16[320,128]{1,0:T(8,128)(2,1)S(1)}, u32[]{:S(2)}, u32[]{:S(2)}) %collective-permute-start.36) | collective-permute-done | bytes 81952 | tf_op jit(solution)/shard_map/cond/branch_2_fun/ppermute | solution.py:324
  39.2 0.6 %collective-permute-start.41 = (bf16[320,128]{1,0:T(8,128)(2,1)S(1)}, bf16[320,128]{1,0:T(8,128)(2,1)S(1)}, u32[]{:S(2)}, u32[]{:S(2)}) collective-permute-start(bf16[320,128]{1,0:T(8,128)(2,1)S(1)} %get-tuple-element.114), channel_id=1, source_target_pairs={{0,6},{2,4},{4,2},{6,0},{8,14},{10,12},{12,10},{14,8},{16,22},{18,... | collective-permute-start | bytes 245768 | tf_op jit(solution)/shard_map/cond/branch_2_fun/ppermute | solution.py:324
  39.8 0.9 %collective-permute-start.42 = (bf16[320,128]{1,0:T(8,128)(2,1)S(1)}, bf16[320,128]{1,0:T(8,128)(2,1)S(1)}, u32[]{:S(2)}, u32[]{:S(2)}) collective-permute-start(bf16[320,128]{1,0:T(8,128)(2,1)S(1)} %get-tuple-element.115), channel_id=1, source_target_pairs={{0,16},{2,18},{4,20},{6,22},{8,24},{10,26},{12,28},{14,30},{16,0},... | collective-permute-start | bytes 245768 | tf_op jit(solution)/shard_map/cond/branch_2_fun/ppermute | solution.py:324
  40.7 3.5 %collective-permute-done.38.refs_8_ = bf16[320,128]{1,0:T(8,128)(2,1)S(1)} collective-permute-done((bf16[320,128]{1,0:T(8,128)(2,1)S(1)}, bf16[320,128]{1,0:T(8,128)(2,1)S(1)}, u32[]{:S(2)}, u32[]{:S(2)}) %collective-permute-start.38) | collective-permute-done | bytes 81952 | tf_op jit(solution)/shard_map/cond/branch_2_fun/ppermute | solution.py:324
  44.1 0.1 collective-permute-start.43
  44.3 1.3 %collective-permute-start.44 = (bf16[320,128]{1,0:T(8,128)(2,1)S(1)}, bf16[320,128]{1,0:T(8,128)(2,1)S(1)}, u32[]{:S(2)}, u32[]{:S(2)}) collective-permute-start(bf16[320,128]{1,0:T(8,128)(2,1)S(1)} %get-tuple-element.117), channel_id=1, source_target_pairs={{0,2},{2,0},{4,6},{6,4},{8,10},{10,8},{12,14},{14,12},{16,18},{18,... | collective-permute-start | bytes 245768 | tf_op jit(solution)/shard_map/cond/branch_2_fun/ppermute | solution.py:324
  45.6 0.4 collective-permute-done.42.refs_12_
  46.0 2.6 %collective-permute-done.43.refs_13_ = bf16[320,128]{1,0:T(8,128)(2,1)S(1)} collective-permute-done((bf16[320,128]{1,0:T(8,128)(2,1)S(1)}, bf16[320,128]{1,0:T(8,128)(2,1)S(1)}, u32[]{:S(2)}, u32[]{:S(2)}) %collective-permute-start.43) | collective-permute-done | bytes 81952 | tf_op jit(solution)/shard_map/cond/branch_2_fun/ppermute | solution.py:324
  48.6 0.1 collective-permute-done.44.refs_14_
  48.7 2.8 %gram.10 = f32[128,128]{1,0:T(8,128)S(1)} custom-call(s32[6]{0:T(128)S(1)} %get-tuple-element.100.scalar_ref.after_ref, bf16[320,128]{1,0:T(8,128)(2,1)S(1)} %collective-permute-done.30.after_ref.refs_0_, bf16[320,128]{1,0:T(8,128)(2,1)S(1)} %collective-permute-done.31.refs_1_, bf16[320,128]{1,0:T(8,128)(2,1)S(1)} %collective-permute-done.32.refs_2_, ...), custom_call_target="tpu_custom_call" | custom-call | tf_op jit(solution)/shard_map/cond/branch_2_fun/gram/pallas_call | solution.py:326
  51.8 0.6 %copy-done.4 = f32[128,128]{1,0:T(8,128)} copy-done((f32[128,128]{1,0:T(8,128)}, f32[128,128]{1,0:T(8,128)S(1)}, u32[]{:S(2)}) %copy-start.4) | copy-done | bytes 65560
  (17 shorter events, 0.0 us)
Async XLA Ops:
  0.0 4.8 %collective-permute-start.120 = (bf16[8,1152,128]{2,1,0:T(8,128)(2,1)}, bf16[8,1152,128]{2,1,0:T(8,128)(2,1)S(1)}, u32[]{:S(2)}, u32[]{:S(2)}) collective-permute-start(bf16[8,1152,128]{2,1,0:T(8,128)(2,1)} %in_ref.1), channel_id=1, source_target_pairs={{0,1},{1,0},{2,3},{3,2},{4,5},{5,4},{6,7},{7,6},{8,9},{9,8},{10,11... | collective-permute-start | bytes 7077896 | tf_op jit(solution)/shard_map/ppermute | solution.py:280
  0.5 1.7 %copy-start = (bf16[8,1152,128]{2,1,0:T(8,128)(2,1)S(1)}, bf16[8,1152,128]{2,1,0:T(8,128)(2,1)}, u32[]{:S(2)}) copy-start(bf16[8,1152,128]{2,1,0:T(8,128)(2,1)} %in_ref.1) | copy-start | bytes 7077892
  2.1 0.7 %copy-start.1 = (s32[2304]{0:T(1024)S(1)}, s32[2304]{0:T(1024)}, u32[]{:S(2)}) copy-start(s32[2304]{0:T(1024)} %cycle_in.1) | copy-start | bytes 27652
  2.1 0.7 %copy-start.2 = (s32[2304]{0:T(1024)S(1)}, s32[2304]{0:T(1024)}, u32[]{:S(2)}) copy-start(s32[2304]{0:T(1024)} %valid_in.1) | copy-start | bytes 27652
  2.1 0.7 %copy-start.3 = (s32[32]{0:T(128)S(1)}, s32[32]{0:T(128)}, u32[]{:S(2)}) copy-start(s32[32]{0:T(128)} %owner_in.1) | copy-start | bytes 388
  7.4 10.7 %collective-permute-start.30 = (bf16[320,128]{1,0:T(8,128)(2,1)S(1)}, bf16[320,128]{1,0:T(8,128)(2,1)S(1)}, u32[]{:S(2)}, u32[]{:S(2)}) collective-permute-start(bf16[320,128]{1,0:T(8,128)(2,1)S(1)} %get-tuple-element.103), channel_id=1, source_target_pairs={{0,30},{2,28},{4,26},{6,24},{8,22},{10,20},{12,18},{14,16},{16,14}... | collective-permute-start | bytes 245768 | tf_op jit(solution)/shard_map/cond/branch_2_fun/ppermute | solution.py:324
  14.3 14.3 %collective-permute-start.31 = (bf16[320,128]{1,0:T(8,128)(2,1)S(1)}, bf16[320,128]{1,0:T(8,128)(2,1)S(1)}, u32[]{:S(2)}, u32[]{:S(2)}) collective-permute-start(bf16[320,128]{1,0:T(8,128)(2,1)S(1)} %get-tuple-element.104), channel_id=1, source_target_pairs={{0,28},{2,30},{4,24},{6,26},{8,20},{10,22},{12,16},{14,18},{16,12}... | collective-permute-start | bytes 245768 | tf_op jit(solution)/shard_map/cond/branch_2_fun/ppermute | solution.py:324
  14.5 16.0 %collective-permute-start.32 = (bf16[320,128]{1,0:T(8,128)(2,1)S(1)}, bf16[320,128]{1,0:T(8,128)(2,1)S(1)}, u32[]{:S(2)}, u32[]{:S(2)}) collective-permute-start(bf16[320,128]{1,0:T(8,128)(2,1)S(1)} %get-tuple-element.105), channel_id=1, source_target_pairs={{0,26},{2,24},{4,30},{6,28},{8,18},{10,16},{12,22},{14,20},{16,10}... | collective-permute-start | bytes 245768 | tf_op jit(solution)/shard_map/cond/branch_2_fun/ppermute | solution.py:324
  18.1 14.3 %collective-permute-start.33 = (bf16[320,128]{1,0:T(8,128)(2,1)S(1)}, bf16[320,128]{1,0:T(8,128)(2,1)S(1)}, u32[]{:S(2)}, u32[]{:S(2)}) collective-permute-start(bf16[320,128]{1,0:T(8,128)(2,1)S(1)} %get-tuple-element.106), channel_id=1, source_target_pairs={{0,14},{2,12},{4,10},{6,8},{8,6},{10,4},{12,2},{14,0},{16,30},{18,... | collective-permute-start | bytes 245768 | tf_op jit(solution)/shard_map/cond/branch_2_fun/ppermute | solution.py:324
  23.1 11.7 %collective-permute-start.34 = (bf16[320,128]{1,0:T(8,128)(2,1)S(1)}, bf16[320,128]{1,0:T(8,128)(2,1)S(1)}, u32[]{:S(2)}, u32[]{:S(2)}) collective-permute-start(bf16[320,128]{1,0:T(8,128)(2,1)S(1)} %get-tuple-element.107), channel_id=1, source_target_pairs={{0,24},{2,26},{4,28},{6,30},{8,16},{10,18},{12,20},{14,22},{16,8},... | collective-permute-start | bytes 245768 | tf_op jit(solution)/shard_map/cond/branch_2_fun/ppermute | solution.py:324
  26.5 8.9 %collective-permute-start.35 = (bf16[320,128]{1,0:T(8,128)(2,1)S(1)}, bf16[320,128]{1,0:T(8,128)(2,1)S(1)}, u32[]{:S(2)}, u32[]{:S(2)}) collective-permute-start(bf16[320,128]{1,0:T(8,128)(2,1)S(1)} %get-tuple-element.108), channel_id=1, source_target_pairs={{0,12},{2,14},{4,8},{6,10},{8,4},{10,6},{12,0},{14,2},{16,28},{18,... | collective-permute-start | bytes 245768 | tf_op jit(solution)/shard_map/cond/branch_2_fun/ppermute | solution.py:324
  28.6 10.5 %collective-permute-start.36 = (bf16[320,128]{1,0:T(8,128)(2,1)S(1)}, bf16[320,128]{1,0:T(8,128)(2,1)S(1)}, u32[]{:S(2)}, u32[]{:S(2)}) collective-permute-start(bf16[320,128]{1,0:T(8,128)(2,1)S(1)} %get-tuple-element.109), channel_id=1, source_target_pairs={{0,22},{2,20},{4,18},{6,16},{8,30},{10,28},{12,26},{14,24},{16,6},... | collective-permute-start | bytes 245768 | tf_op jit(solution)/shard_map/cond/branch_2_fun/ppermute | solution.py:324
  30.5 9.3 %collective-permute-start.37 = (bf16[320,128]{1,0:T(8,128)(2,1)S(1)}, bf16[320,128]{1,0:T(8,128)(2,1)S(1)}, u32[]{:S(2)}, u32[]{:S(2)}) collective-permute-start(bf16[320,128]{1,0:T(8,128)(2,1)S(1)} %get-tuple-element.110), channel_id=1, source_target_pairs={{0,10},{2,8},{4,14},{6,12},{8,2},{10,0},{12,6},{14,4},{16,26},{18,... | collective-permute-start | bytes 245768 | tf_op jit(solution)/shard_map/cond/branch_2_fun/ppermute | solution.py:324
  32.4 11.8 %collective-permute-start.38 = (bf16[320,128]{1,0:T(8,128)(2,1)S(1)}, bf16[320,128]{1,0:T(8,128)(2,1)S(1)}, u32[]{:S(2)}, u32[]{:S(2)}) collective-permute-start(bf16[320,128]{1,0:T(8,128)(2,1)S(1)} %get-tuple-element.111), channel_id=1, source_target_pairs={{0,20},{2,22},{4,16},{6,18},{8,28},{10,30},{12,24},{14,26},{16,4},... | collective-permute-start | bytes 245768 | tf_op jit(solution)/shard_map/cond/branch_2_fun/ppermute | solution.py:324
  34.8 9.4 %collective-permute-start.39 = (bf16[320,128]{1,0:T(8,128)(2,1)S(1)}, bf16[320,128]{1,0:T(8,128)(2,1)S(1)}, u32[]{:S(2)}, u32[]{:S(2)}) collective-permute-start(bf16[320,128]{1,0:T(8,128)(2,1)S(1)} %get-tuple-element.112), channel_id=1, source_target_pairs={{0,8},{2,10},{4,12},{6,14},{8,0},{10,2},{12,4},{14,6},{16,24},{18,... | collective-permute-start | bytes 245768 | tf_op jit(solution)/shard_map/cond/branch_2_fun/ppermute | solution.py:324
  35.4 10.2 %collective-permute-start.40 = (bf16[320,128]{1,0:T(8,128)(2,1)S(1)}, bf16[320,128]{1,0:T(8,128)(2,1)S(1)}, u32[]{:S(2)}, u32[]{:S(2)}) collective-permute-start(bf16[320,128]{1,0:T(8,128)(2,1)S(1)} %get-tuple-element.113), channel_id=1, source_target_pairs={{0,18},{2,16},{4,22},{6,20},{8,26},{10,24},{12,30},{14,28},{16,2},... | collective-permute-start | bytes 245768 | tf_op jit(solution)/shard_map/cond/branch_2_fun/ppermute | solution.py:324
  39.2 6.4 %collective-permute-start.41 = (bf16[320,128]{1,0:T(8,128)(2,1)S(1)}, bf16[320,128]{1,0:T(8,128)(2,1)S(1)}, u32[]{:S(2)}, u32[]{:S(2)}) collective-permute-start(bf16[320,128]{1,0:T(8,128)(2,1)S(1)} %get-tuple-element.114), channel_id=1, source_target_pairs={{0,6},{2,4},{4,2},{6,0},{8,14},{10,12},{12,10},{14,8},{16,22},{18,... | collective-permute-start | bytes 245768 | tf_op jit(solution)/shard_map/cond/branch_2_fun/ppermute | solution.py:324
  39.8 6.2 %collective-permute-start.42 = (bf16[320,128]{1,0:T(8,128)(2,1)S(1)}, bf16[320,128]{1,0:T(8,128)(2,1)S(1)}, u32[]{:S(2)}, u32[]{:S(2)}) collective-permute-start(bf16[320,128]{1,0:T(8,128)(2,1)S(1)} %get-tuple-element.115), channel_id=1, source_target_pairs={{0,16},{2,18},{4,20},{6,22},{8,24},{10,26},{12,28},{14,30},{16,0},... | collective-permute-start | bytes 245768 | tf_op jit(solution)/shard_map/cond/branch_2_fun/ppermute | solution.py:324
  44.1 4.4 %collective-permute-start.43 = (bf16[320,128]{1,0:T(8,128)(2,1)S(1)}, bf16[320,128]{1,0:T(8,128)(2,1)S(1)}, u32[]{:S(2)}, u32[]{:S(2)}) collective-permute-start(bf16[320,128]{1,0:T(8,128)(2,1)S(1)} %get-tuple-element.116), channel_id=1, source_target_pairs={{0,4},{2,6},{4,0},{6,2},{8,12},{10,14},{12,8},{14,10},{16,20},{18,... | collective-permute-start | bytes 245768 | tf_op jit(solution)/shard_map/cond/branch_2_fun/ppermute | solution.py:324
  44.3 4.4 %collective-permute-start.44 = (bf16[320,128]{1,0:T(8,128)(2,1)S(1)}, bf16[320,128]{1,0:T(8,128)(2,1)S(1)}, u32[]{:S(2)}, u32[]{:S(2)}) collective-permute-start(bf16[320,128]{1,0:T(8,128)(2,1)S(1)} %get-tuple-element.117), channel_id=1, source_target_pairs={{0,2},{2,0},{4,6},{6,4},{8,10},{10,8},{12,14},{14,12},{16,18},{18,... | collective-permute-start | bytes 245768 | tf_op jit(solution)/shard_map/cond/branch_2_fun/ppermute | solution.py:324
  51.8 0.6 %copy-start.4 = (f32[128,128]{1,0:T(8,128)}, f32[128,128]{1,0:T(8,128)S(1)}, u32[]{:S(2)}) copy-start(f32[128,128]{1,0:T(8,128)S(1)} %get-tuple-element.477) | copy-start | bytes 196612
